TPU v7x, 128 devices: a whole 4x4x4 slice. The times are simulated.
128 devices in a mesh: pipe: 4 (over x_lo, core), dp: 4 (over z), tensor: 8 (over x_hi, y).
Axes of the slice: x: 4 (x_hi: 2, x_lo: 2; x = x_hi * 2 + x_lo), y: 4, z: 4, core: 2. Of those that a mesh axis runs over, the one named last changes fastest.
Arguments:
- hidden_in: bfloat16 [4, 4096, 8192], P('pipe', ('dp', 'tensor')), may hold values from -6 to 6
- norm_gain: bfloat16 [4, 8192], P('pipe'), may hold values from 0.5 to 1.5
- qkv_weight: bfloat16 [4, 8192, 6144], P('pipe', None, 'tensor'), may hold values from -0.0625 to 0.0625
- qkv_grad: bfloat16 [4, 4096, 6144], P('pipe', 'dp', 'tensor'), may hold values from -0.3984375 to 0.3984375
- upper_grad: bfloat16 [4, 4096, 8192], P('pipe', ('dp', 'tensor')), may hold values from -0.59765625 to 0.59765625
Outputs:
- weight_grad: bfloat16 [4, 8192, 6144], P('pipe', 'dp', 'tensor')
- input_grad: bfloat16 [4, 4096, 8192], P('pipe', ('dp', 'tensor'))
All inputs are finite; a program needn't handle non-finite values.
Results may differ from a plain program's by a relative error of at most 0.013.
Values may be sent and summed in bfloat16 or wider, within the bound.
No kernel may reach another device: no remote copies, remote signals or barrier semaphores. Data moves between devices by JAX's collectives and lax.ppermute only.
A program may use at most 128 MiB of HBM per device.

v0:
```python
import jax
import jax.numpy as jnp
from jax import lax
from jax.sharding import PartitionSpec as P


def shifted(block, axis, distance):
    devices = range(lax.axis_size(axis))
    route = [(i - distance, i) for i in devices if i - distance in devices]
    return lax.ppermute(block, axis, route)


def shards(hidden_in, norm_gain, qkv_weight, qkv_grad, upper_grad):
    input_rows = hidden_in[0].astype(jnp.float32)
    scale_factor = norm_gain[0].astype(jnp.float32)
    weight = qkv_weight[0]
    grads = qkv_grad[0]
    inverse_deviation = lax.rsqrt(jnp.mean(input_rows * input_rows, axis=-1, keepdims=True) + 1e-06)
    centered_input = input_rows * inverse_deviation
    normed_input = (centered_input * scale_factor).astype(jnp.bfloat16)
    hidden_grad = lax.psum_scatter(
        lax.dot_general(
            grads, weight, (((1,), (1,)), ((), ())), preferred_element_type=jnp.float32
        ).astype(jnp.bfloat16),
        "tensor",
        scatter_dimension=0,
        tiled=True,
    ).astype(jnp.float32)
    gathered = lax.all_gather(normed_input, "tensor", axis=0, tiled=True)
    summed = lax.psum_scatter(
        lax.dot_general(
            gathered, grads, (((0,), (0,)), ((), ())), preferred_element_type=jnp.float32
        ).astype(jnp.bfloat16),
        "dp",
        scatter_dimension=0,
        tiled=True,
    )
    weight_out = summed[None]
    received_gradient = shifted(upper_grad, "pipe", -1)[0].astype(jnp.float32)
    scaled_gradient = scale_factor * hidden_grad
    inner_product = jnp.mean(scaled_gradient * centered_input, axis=-1, keepdims=True)
    final_output = received_gradient + inverse_deviation * (
        scaled_gradient - centered_input * inner_product
    )
    return (weight_out, final_output.astype(jnp.bfloat16)[None])


def solution(mesh):
    placed = (
        P("pipe", ("dp", "tensor"), None),
        P("pipe", None),
        P("pipe", None, "tensor"),
        P("pipe", "dp", "tensor"),
        P("pipe", ("dp", "tensor"), None),
    )
    return jax.shard_map(
        shards,
        mesh=mesh,
        in_specs=placed,
        out_specs=(P("pipe", "dp", "tensor"), P("pipe", ("dp", "tensor"), None)),
        check_vma=False,
    )
```

profile of v0, /device:TPU:0, one launch (start us, length us, event | category | flops | bytes accessed | tf_op | source)
XLA Modules:
  0.0 564.8 jit_solution(97119519133002299)
XLA Ops:
  7.2 0.0 copy-start
  7.2 0.0 reduce-scatter.5.cloned.1.call-start
  7.2 1.4 copy-done
  8.6 20.4 %convolution_convert_fusion = bf16[1024,8192]{1,0:T(8,128)(2,1)} fusion(bf16[1,8192,768]{2,1,0:T(8,128)(2,1)} %param.7, bf16[1,1024,768]{2,1,0:T(8,128)(2,1)S(1)} %copy-done), kind=kOutput, calls=%fused_computation | convolution fusion | flops 12893290496 | bytes 30932992 | tf_op jit(solution)/shard_map/dot_general | solution.py:22
  29.0 0.0 copy-start.3
  29.0 0.0 reduce-scatter.5.cloned.1.call-update
  29.0 0.0 all-gather.2.cloned.1.call-start
  29.0 1.3 collective-permute-start
  30.3 0.0 copy-done.3
  30.4 2.1 fusion.10
  32.5 199.3 %reduce-scatter.5.cloned.1.call-done = bf16[128,8192]{1,0:T(8,128)(2,1)} async-done(((bf16[1024,8192]{1,0:T(8,128)(2,1)}), bf16[128,8192]{1,0:T(8,128)(2,1)}) %reduce-scatter.5.cloned.1.call-update) | async-done | bytes 2097168 | tf_op jit(solution)/shard_map/reduce_scatter | solution.py:21
  231.7 0.0 copy-start.1
  231.7 0.0 copy-start.2
  231.7 3.3 fusion.5
  235.1 0.0 collective-permute-done
  235.1 0.0 copy-done.1
  235.1 0.1 copy-done.2
  235.2 5.3 fusion.11
  240.5 0.0 all-gather.2.cloned.1.call-update
  240.6 0.0 reduce-scatter.3.cloned.1.call-start
  240.6 182.6 %all-gather.2.cloned.1.call-done = bf16[1024,8192]{1,0:T(8,128)(2,1)} async-done(((bf16[128,8192]{1,0:T(8,128)(2,1)}), bf16[1024,8192]{1,0:T(8,128)(2,1)}) %all-gather.2.cloned.1.call-update) | async-done | bytes 16777232 | tf_op jit(solution)/shard_map/all_gather | solution.py:29
  423.2 22.3 %convolution_convert_fusion.1 = bf16[8192,768]{1,0:T(8,128)(2,1)} fusion(bf16[1024,8192]{1,0:T(8,128)(2,1)} %all-gather.2.cloned.1.call-done, bf16[1,1024,768]{2,1,0:T(8,128)(2,1)S(1)} %copy-done), kind=kOutput, calls=%fused_computation.1 | convolution fusion | flops 12891193344 | bytes 30932992 | tf_op jit(solution)/shard_map/dot_general | solution.py:31
  445.5 0.0 reduce-scatter.3.cloned.1.call-update
  445.5 112.8 %reduce-scatter.3.cloned.1.call-done = bf16[2048,768]{1,0:T(8,128)(2,1)} async-done(((bf16[8192,768]{1,0:T(8,128)(2,1)}), bf16[2048,768]{1,0:T(8,128)(2,1)}) %reduce-scatter.3.cloned.1.call-update) | async-done | bytes 3145744 | tf_op jit(solution)/shard_map/reduce_scatter | solution.py:30
  (3 shorter events, 0.1 us)
Async XLA Ops:
  7.2 1.4 copy-start
  7.2 224.5 %reduce-scatter.5.cloned.1.call-start = ((), (), s32[]{:S(2)}) async-start(), calls=%async_computation.4 | async-start | bytes 18874368 | tf_op jit(solution)/shard_map/reduce_scatter | solution.py:21
  29.0 1.4 copy-start.3
  29.0 394.3 %all-gather.2.cloned.1.call-start = ((), (), s32[]{:S(2)}) async-start(), calls=%async_computation.2 | async-start | bytes 18874368 | tf_op jit(solution)/shard_map/all_gather | solution.py:29
  29.0 206.0 %collective-permute-start = (bf16[1,128,8192]{2,1,0:T(8,128)(2,1)}, bf16[1,128,8192]{2,1,0:T(8,128)(2,1)}, u32[]{:S(2)}, u32[]{:S(2)}) collective-permute-start(bf16[1,128,8192]{2,1,0:T(8,128)(2,1)} %param.9), channel_id=1, source_target_pairs={{32,0},{64,32},{96,64},{33,1},{65,33},{97,65},{34,2},{66,34},{98,6... | collective-permute-start | bytes 6291464 | tf_op jit(solution)/shard_map/ppermute | solution.py:10
  231.7 3.4 copy-start.1
  231.7 3.5 copy-start.2
  240.6 317.7 %reduce-scatter.3.cloned.1.call-start = ((), (), s32[]{:S(2)}) async-start(), calls=%async_computation.3 | async-start | bytes 15728640 | tf_op jit(solution)/shard_map/reduce_scatter | solution.py:30
Sparse Core Ops, SparseCore 0:
  29.1 202.5 reduce-scatter.4
  240.7 182.5 all-gather.1
  445.6 112.5 reduce-scatter.2
where the time goes:
time: 566 us; the launch traced here: 565 us
  waiting for transfers between devices  495 us (87%)
  matrix products  42.6 us (8%)
  between operations  13.8 us (2%)
  other arithmetic  10.8 us (2%)
    reduce_scatter x1, waiting for transfers between devices, shards(): lax.psum_scatter(lax.dot_general(grads, weight, (((1,), (1,)), ((), ())),...  199 us
    all_gather x1, waiting for transfers between devices, shards(): gathered = lax.all_gather(normed_input, 'tensor', axis=0, tiled=True)  183 us
    reduce_scatter x1, waiting for transfers between devices, shards(): lax.psum_scatter(lax.dot_general(gathered, grads, (((0,), (0,)), ((), ())...  113 us
    dot_general x1, matrix products, shards(): lax.dot_general(gathered, grads, (((0,), (0,)), ((), ())), preferred_elem...  22.3 us
    dot_general x1, matrix products, shards(): lax.dot_general(grads, weight, (((1,), (1,)), ((), ())), preferred_elemen...  20.4 us
  transfers between devices with their start and end apart: 4, of which 3 were waited for; matrix products, arithmetic and copies ran while one was open for 1% of the time, Pallas kernels for 0%

commit v1 on v0

v1 whole, which is shorter than its diff:
```python
import jax
import jax.numpy as jnp
from jax import lax
from jax.sharding import PartitionSpec as P

N_Z = 4
N_Y = 4
F32 = jnp.float32
BF16 = jnp.bfloat16


def from_z(block, o):
    return lax.ppermute(block, "dp", [((i + o) % N_Z, i) for i in range(N_Z)])


def from_y(block, o):
    return lax.ppermute(
        block,
        "tensor",
        [(x * N_Y + (i + o) % N_Y, x * N_Y + i) for x in range(2) for i in range(N_Y)],
    )


def from_x(block):
    return lax.ppermute(block, "tensor", [(i, (i + N_Y) % (2 * N_Y)) for i in range(2 * N_Y)])


def dot_nt(a, b):
    return lax.dot_general(a, b, (((1,), (1,)), ((), ())), preferred_element_type=F32)


def dot_tn(a, b):
    return lax.dot_general(a, b, (((0,), (0,)), ((), ())), preferred_element_type=F32)


def shards(hidden_in, norm_gain, qkv_weight, qkv_grad, upper_grad):
    place = lax.axis_index("tensor")
    xh, y, z = place // N_Y, place % N_Y, lax.axis_index("dp")
    rows = hidden_in.shape[1]
    width = hidden_in.shape[2]
    part = width // N_Z
    half = part // 2
    cols = qkv_grad.shape[2]
    layers = lax.axis_size("pipe")

    grads = qkv_grad[0].reshape(2, N_Y, rows, cols)

    def turned(which):
        side = lax.dynamic_index_in_dim(grads, which, 0, keepdims=False)
        return jnp.concatenate(
            [lax.dynamic_slice_in_dim(side, (y + q) % N_Y, 1, 0) for q in range(N_Y)], 0
        )

    partner = from_x(turned(1 - xh))
    g_own = jnp.concatenate([turned(xh), partner], -1)
    weight = lax.dynamic_slice_in_dim(qkv_weight[0], z * part, part, 0)
    w_both = jnp.concatenate([weight, from_x(weight)], 1)
    received_gradient = lax.ppermute(upper_grad, "pipe", [(i + 1, i) for i in range(layers - 1)])

    input_rows = hidden_in[0].astype(F32)
    scale_factor = norm_gain[0].astype(F32)
    inverse_deviation = lax.rsqrt(jnp.mean(input_rows * input_rows, axis=-1, keepdims=True) + 1e-06)

    def normed(block):
        at = (block % N_Z) * part
        x = lax.dynamic_slice_in_dim(hidden_in[0], at, part, 1).astype(F32)
        s = lax.dynamic_slice_in_dim(norm_gain[0], at, part, 0).astype(F32)
        return ((x * inverse_deviation) * s).astype(BF16)

    n_far = jnp.concatenate([from_z(normed(z - o), o) for o in (1, 3, 2)], 0)
    n_near = normed(z)

    def gather_y(block):
        up, down = from_y(block, 1), from_y(block, 3)
        cut = block.shape[0] // 2
        across = jnp.concatenate([from_y(up[:cut], 1), from_y(down[cut:], 3)], 0)
        return [block, up, across, down]

    near, far = gather_y(n_near), gather_y(n_far)

    g_up, g_down = from_z(g_own, 1), from_z(g_own, 3)
    g_across = jnp.concatenate([from_z(g_up[:2], 1), from_z(g_down[2:], 3)], 0)
    g_all = jnp.stack([g_up, g_down, g_across, g_own], 1)

    def summed(first, last):
        count = last - first

        def partial(q):
            return dot_nt(g_all[q, first:last].reshape(count * rows, 2 * cols), w_both)

        p2 = partial(2).astype(BF16)
        first_hop_up = from_y(p2[:, :half], 3)
        first_hop_down = from_y(p2[:, half:], 1)
        p1, p3 = partial(1), partial(3)
        up_own = from_y(p1[:, half:].astype(BF16), 3)
        down_own = from_y(p3[:, :half].astype(BF16), 1)
        up_sum = from_y((p1[:, :half] + first_hop_up.astype(F32)).astype(BF16), 3)
        down_sum = from_y((p3[:, half:] + first_hop_down.astype(F32)).astype(BF16), 1)
        p0 = partial(0)
        left = p0[:, :half] + up_sum.astype(F32) + down_own.astype(F32)
        right = p0[:, half:] + down_sum.astype(F32) + up_own.astype(F32)
        return jnp.concatenate([left, right], 1).astype(BF16).reshape(count, rows, part)

    h_far = summed(0, 3)
    h_near = summed(3, 4)
    h1 = from_z(h_far[1], 1)
    h3 = from_z(h_far[0], 3)
    h2 = from_z(h_far[2], 2)
    turned_h = jnp.stack([h_near[0], h1, h2, h3], 0)
    hidden_grad = jnp.concatenate(
        [
            lax.dynamic_index_in_dim(turned_h, (b - z) % N_Z, 0, keepdims=False)
            for b in range(N_Z)
        ],
        1,
    ).astype(F32)

    n_all = jnp.concatenate([jnp.concatenate([far[q], near[q]], 0) for q in range(N_Y)], 0)
    g_flat = g_all.reshape(N_Y * N_Z * rows, 2 * cols)
    dw_partner = dot_tn(n_all, g_flat[:, cols:]).astype(BF16)
    dw_got = from_x(dw_partner)
    weight_out = (dot_tn(n_all, g_flat[:, :cols]) + dw_got.astype(F32)).astype(BF16)

    centered_input = input_rows * inverse_deviation
    scaled_gradient = scale_factor * hidden_grad
    inner_product = jnp.mean(scaled_gradient * centered_input, axis=-1, keepdims=True)
    final_output = received_gradient[0].astype(F32) + inverse_deviation * (
        scaled_gradient - centered_input * inner_product
    )
    return (weight_out[None], final_output.astype(BF16)[None])


def solution(mesh):
    placed = (
        P("pipe", ("dp", "tensor"), None),
        P("pipe", None),
        P("pipe", None, "tensor"),
        P("pipe", "dp", "tensor"),
        P("pipe", ("dp", "tensor"), None),
    )
    return jax.shard_map(
        shards,
        mesh=mesh,
        in_specs=placed,
        out_specs=(P("pipe", "dp", "tensor"), P("pipe", ("dp", "tensor"), None)),
        check_vma=False,
    )
```

time: 566 us -> 336 us (0.59)
  waiting for transfers between devices: 495 us -> 148 us
  starting transfers between devices: 1.41 us -> 75.6 us
  local copies, waits for them, and re-layouts: 1.49 us -> 36.6 us
  other arithmetic: 10.8 us -> 23.7 us
  between operations: 13.8 us -> 1.42 us
    reduce_scatter x2 -> x0, waiting for transfers between devices: 312 us -> none  [the longest x1 199 us: shards(): lax.psum_scatter(lax.dot_general(grads, weight, (((1,), (1,)), ((), ())),...]
    all_gather x1 -> x0, waiting for transfers between devices: 183 us -> none  [shards(): gathered = lax.all_gather(normed_input, 'tensor', axis=0, tiled=True)]
    ppermute x1 -> x34, waiting for transfers between devices: 0.01 us -> 148 us  [the longest x3 76.8 us: from_x(): lax.ppermute(block, 'tensor', [(i, (i + N_Y) % (2 * N_Y)) for i in range(...]
    ppermute x1 -> x34, starting transfers between devices: 1.29 us -> 75.6 us  [the longest x20 39.7 us: from_y(): lax.ppermute(block, 'tensor', [(x * N_Y + (i + o) % N_Y, x * N_Y + i) for...]
    unnamed x8 -> x30, local copies, waits for them, and re-layouts: 1.49 us -> 17.4 us
    slice x0 -> x13, local copies, waits for them, and re-layouts: none -> 9.5 us  [the longest x4 5.39 us: gather_y(): across = jnp.concatenate([from_y(up[:cut], 1), from_y(down[cut:], 3)], 0)]
    another operation x0 -> x5, other arithmetic: none -> 8.68 us  [the longest x3 6.16 us: shards(): g_all = jnp.stack([g_up, g_down, g_across, g_own], 1)]
    dot_general x2 -> x10, matrix products: 42.6 us -> 45.6 us  [the longest x8 26.3 us: dot_nt(): lax.dot_general(a, b, (((1,), (1,)), ((), ())), preferred_element_type=F32)]
  transfers between devices with their start and end apart: 4 -> 34, of which waited for: 3 -> 13; matrix products, arithmetic and copies ran while one was open for 1% -> 27% of each run, Pallas kernels for 0% -> 0%
where the time goes in v1:
time: 336 us; the launch traced here: 331 us
  waiting for transfers between devices  148 us (44%)
  starting transfers between devices  75.6 us (22%)
  matrix products  45.6 us (14%)
  local copies, waits for them, and re-layouts  36.6 us (11%)
  other arithmetic  23.7 us (7%)
    ppermute x3, waiting for transfers between devices, from_x(): lax.ppermute(block, 'tensor', [(i, (i + N_Y) % (2 * N_Y)) for i in range(...  76.8 us
    ppermute x20, starting transfers between devices, from_y(): lax.ppermute(block, 'tensor', [(x * N_Y + (i + o) % N_Y, x * N_Y + i) for...  39.7 us
    ppermute x10, waiting for transfers between devices, from_z(): return lax.ppermute(block, 'dp', [((i + o) % N_Z, i) for i in range(N_Z)])  38.1 us
    ppermute x20, waiting for transfers between devices, from_y(): lax.ppermute(block, 'tensor', [(x * N_Y + (i + o) % N_Y, x * N_Y + i) for...  33.1 us
    dot_general x8, matrix products, dot_nt(): lax.dot_general(a, b, (((1,), (1,)), ((), ())), preferred_element_type=F32)  26.3 us
    ppermute x10, starting transfers between devices, from_z(): return lax.ppermute(block, 'dp', [((i + o) % N_Z, i) for i in range(N_Z)])  25.4 us
    dot_general x2, matrix products, dot_tn(): lax.dot_general(a, b, (((0,), (0,)), ((), ())), preferred_element_type=F32)  19.2 us
    unnamed x30, local copies, waits for them, and re-layouts  17.4 us
  transfers between devices with their start and end apart: 34, of which 13 were waited for; matrix products, arithmetic and copies ran while one was open for 27% of the time, Pallas kernels for 0%

profile of v1, /device:TPU:0, one launch (start us, length us, event | category | flops | bytes accessed | tf_op | source)
XLA Modules:
  0.0 331.0 jit_solution(15164488685261673738)
XLA Ops:
  0.7 2.2 fusion.2
  3.8 1.4 fusion.24
  5.2 4.1 %collective-permute-start = (bf16[128,2048]{1,0:T(8,128)(2,1)}, bf16[128,2048]{1,0:T(8,128)(2,1)}, u32[]{:S(2)}, u32[]{:S(2)}) collective-permute-start(bf16[128,2048]{1,0:T(8,128)(2,1)} %get-tuple-element.12), channel_id=1, source_target_pairs={{8,0},{16,8},{24,16},{0,24},{9,1},{17,9},{25,17},{1,25},{10,2},{18... | collective-permute-start | bytes 1572872 | tf_op jit(solution)/shard_map/ppermute | solution.py:13
  9.3 1.9 collective-permute-start.2
  11.2 1.6 dynamic-slice_bitcast_fusion.8
  12.9 3.1 collective-permute-start.11
  16.0 16.1 %collective-permute-done = bf16[128,2048]{1,0:T(8,128)(2,1)} collective-permute-done((bf16[128,2048]{1,0:T(8,128)(2,1)}, bf16[128,2048]{1,0:T(8,128)(2,1)}, u32[]{:S(2)}, u32[]{:S(2)}) %collective-permute-start) | collective-permute-done | bytes 524320 | tf_op jit(solution)/shard_map/ppermute | solution.py:13
  32.1 2.1 constant_dynamic-update-slice_fusion.2
  34.2 1.3 collective-permute-done.1
  35.5 2.1 constant_dynamic-update-slice_fusion.1
  37.6 2.2 constant_dynamic-update-slice_fusion
  39.8 3.0 collective-permute-start.3
  42.8 1.4 pad_maximum_fusion.4
  44.1 2.4 collective-permute-start.12
  46.6 1.2 constant_dynamic-update-slice_fusion.11
  47.7 3.2 collective-permute-start.4
  51.0 27.0 %collective-permute-done.3 = bf16[384,2048]{1,0:T(8,128)(2,1)} collective-permute-done((bf16[384,2048]{1,0:T(8,128)(2,1)}, bf16[384,2048]{1,0:T(8,128)(2,1)}, u32[]{:S(2)}, u32[]{:S(2)}) %collective-permute-start.3) | collective-permute-done | bytes 1572896 | tf_op jit(solution)/shard_map/ppermute | solution.py:17
  79.0 2.1 slice.155
  81.1 2.7 collective-permute-start.5
  83.8 3.8 %dynamic-slice_bitcast_fusion = bf16[2048,768]{1,0:T(8,128)(2,1)} fusion(bf16[1,8192,768]{2,1,0:T(8,128)(2,1)} %param.7, s32[]{:T(128)S(6)} %select_n.160), kind=kLoop, calls=%fused_computation.19 | loop fusion | bytes 6291460 | tf_op jit(solution)/shard_map/dynamic_slice | solution.py:56
  87.6 1.3 slice.156
  92.3 3.1 collective-permute-start.18
  96.3 2.7 constant_dynamic-update-slice_fusion.10
  99.1 1.9 constant_dynamic-update-slice_fusion.9
  101.0 2.7 collective-permute-start.8
  103.6 1.2 slice.159
  104.9 1.2 slice.160
  106.1 2.5 collective-permute-start.14
  108.6 2.1 constant_dynamic-update-slice_fusion.8
  113.2 2.8 constant_dynamic-update-slice_fusion.4
  116.0 1.9 constant_dynamic-update-slice_fusion.3
  117.9 3.5 %collective-permute-done.14 = bf16[2,128,1536]{2,1,0:T(8,128)(2,1)S(1)} collective-permute-done((bf16[2,128,1536]{2,1,0:T(8,128)(2,1)S(1)}, bf16[2,128,1536]{2,1,0:T(8,128)(2,1)S(1)}, u32[]{:S(2)}, u32[]{:S(2)}) %collective-permute-start.14) | collective-permute-done | bytes 786464 | tf_op jit(solution)/shard_map/ppermute | solution.py:13
  121.4 5.5 %collective-permute-done.15 = bf16[2,128,1536]{2,1,0:T(8,128)(2,1)S(1)} collective-permute-done((bf16[2,128,1536]{2,1,0:T(8,128)(2,1)S(1)}, bf16[2,128,1536]{2,1,0:T(8,128)(2,1)S(1)}, u32[]{:S(2)}, u32[]{:S(2)}) %collective-permute-start.15) | collective-permute-done | bytes 786464 | tf_op jit(solution)/shard_map/ppermute | solution.py:13
  127.0 2.1 pad_maximum_fusion.2
  129.5 27.2 %collective-permute-done.18 = bf16[2048,768]{1,0:T(8,128)(2,1)S(1)} collective-permute-done((bf16[2048,768]{1,0:T(8,128)(2,1)S(1)}, bf16[2048,768]{1,0:T(8,128)(2,1)S(1)}, u32[]{:S(2)}, u32[]{:S(2)}) %collective-permute-start.18) | collective-permute-done | bytes 3145760 | tf_op jit(solution)/shard_map/ppermute | solution.py:25
  156.7 2.6 fusion.42
  159.5 3.3 collective-permute-start.27
  162.7 2.9 convolution_convert_fusion.1
  166.6 1.1 copy-done.5
  167.8 2.6 fusion.43
  170.6 3.2 collective-permute-start.28
  173.8 3.3 convolution_convert_fusion.2
  177.3 3.0 pad_maximum_fusion
  180.3 10.6 %convolution_convert_fusion = bf16[2048,768]{1,0:T(8,128)(2,1)} fusion(bf16[2048,2048]{1,0:T(8,128)(2,1)} %constant_dynamic-update-slice_fusion.3, bf16[2048,1536]{1,0:T(8,128)(2,1)S(1)} %bitcast.98), kind=kOutput, calls=%fused_computation.16 | convolution fusion | flops 6444023808 | bytes 14680064 | tf_op jit(solution)/shard_map/dot_general | solution.py:33
  190.9 4.3 %fusion.44 = f32[384,2048]{1,0:T(8,128)S(1)} fusion(bf16[384,1536]{1,0:T(8,128)(2,1)S(1)} %bitcast.105, bf16[2048,768]{1,0:T(8,128)(2,1)} %copy-done.4, bf16[2048,768]{1,0:T(8,128)(2,1)S(1)} %copy-done.1), kind=kOutput, calls=%fused_computation.115 | convolution fusion | flops 2428502016 | bytes 10616832 | tf_op jit(solution)/shard_map/dot_general | solution.py:29
  195.1 3.8 %fusion.37 = f32[128,2048]{1,0:T(8,128)S(1)} fusion(bf16[4,128,1536]{2,1,0:T(8,128)(2,1)} %pad_maximum_fusion.4, bf16[2048,768]{1,0:T(8,128)(2,1)} %copy-done.4, bf16[2048,768]{1,0:T(8,128)(2,1)S(1)} %copy-done.1), kind=kOutput, calls=%fused_computation.70 | convolution fusion | flops 817889280 | bytes 7733248 | tf_op jit(solution)/shard_map/dot_general | solution.py:29
  199.0 3.3 collective-permute-start.22
  202.9 3.7 %collective-permute-done.19 = bf16[128,1024]{1,0:T(8,128)(2,1)S(1)} collective-permute-done((bf16[128,1024]{1,0:T(8,128)(2,1)S(1)}, bf16[128,1024]{1,0:T(8,128)(2,1)S(1)}, u32[]{:S(2)}, u32[]{:S(2)}) %collective-permute-start.19) | collective-permute-done | bytes 262176 | tf_op jit(solution)/shard_map/ppermute | solution.py:17
  206.5 10.1 %collective-permute-start.29 = (bf16[384,1024]{1,0:T(8,128)(2,1)S(1)}, bf16[384,1024]{1,0:T(8,128)(2,1)S(1)}, u32[]{:S(2)}, u32[]{:S(2)}) collective-permute-start(bf16[384,1024]{1,0:T(8,128)(2,1)S(1)} %fusion.15), channel_id=1, source_target_pairs={{1,0},{2,1},{3,2},{0,3},{5,4},{6,5},{7,6},{4,7},{9,8},{10,9},{11,1... | collective-permute-start | bytes 2359304 | tf_op jit(solution)/shard_map/ppermute | solution.py:17
  216.7 3.8 %fusion.38 = f32[128,2048]{1,0:T(8,128)S(1)} fusion(bf16[4,128,1536]{2,1,0:T(8,128)(2,1)} %pad_maximum_fusion.4, bf16[2048,768]{1,0:T(8,128)(2,1)} %copy-done.4, bf16[2048,768]{1,0:T(8,128)(2,1)S(1)} %copy-done.1), kind=kOutput, calls=%fused_computation.73 | convolution fusion | flops 817889280 | bytes 7733248 | tf_op jit(solution)/shard_map/dot_general | solution.py:29
  220.6 1.3 collective-permute-start.17
  225.6 2.0 collective-permute-done.29
  227.7 3.1 collective-permute-start.23
  230.8 2.3 fusion.20
  233.3 2.0 collective-permute-start.33
  235.3 7.7 %collective-permute-start.32 = (bf16[128,2048]{1,0:T(8,128)(2,1)S(1)}, bf16[128,2048]{1,0:T(8,128)(2,1)S(1)}, u32[]{:S(2)}, u32[]{:S(2)}) collective-permute-start(bf16[128,2048]{1,0:T(8,128)(2,1)S(1)} %get-tuple-element.19), channel_id=1, source_target_pairs={{16,0},{24,8},{0,16},{8,24},{17,1},{25,9},{1,17},{9,25},{18,2},{26... | collective-permute-start | bytes 1572872 | tf_op jit(solution)/shard_map/ppermute | solution.py:13
  243.0 4.8 %collective-permute-start.31 = (bf16[128,2048]{1,0:T(8,128)(2,1)S(1)}, bf16[128,2048]{1,0:T(8,128)(2,1)S(1)}, u32[]{:S(2)}, u32[]{:S(2)}) collective-permute-start(bf16[128,2048]{1,0:T(8,128)(2,1)S(1)} %get-tuple-element.17), channel_id=1, source_target_pairs={{8,0},{16,8},{24,16},{0,24},{9,1},{17,9},{25,17},{1,25},{10,2},{18... | collective-permute-start | bytes 1572872 | tf_op jit(solution)/shard_map/ppermute | solution.py:13
  247.8 3.1 fusion.39
  250.9 3.1 collective-permute-start.16
  254.2 10.8 %collective-permute-done.32 = bf16[128,2048]{1,0:T(8,128)(2,1)S(1)} collective-permute-done((bf16[128,2048]{1,0:T(8,128)(2,1)S(1)}, bf16[128,2048]{1,0:T(8,128)(2,1)S(1)}, u32[]{:S(2)}, u32[]{:S(2)}) %collective-permute-start.32) | collective-permute-done | bytes 524320 | tf_op jit(solution)/shard_map/ppermute | solution.py:13
  266.6 3.5 %fusion.4 = f32[128]{0:T(128)S(1)} fusion(bf16[1,128,8192]{2,1,0:T(8,128)(2,1)S(1)} %copy-done, bf16[128,2048]{1,0:T(8,128)(2,1)S(1)} %bitcast.101, bf16[128,2048]{1,0:T(8,128)(2,1)S(1)} %bitcast.102, bf16[128,2048]{1,0:T(8,128)(2,1)S(1)} %bitcast.103, bf16[128,2048]{1,0:T(8,128)(2,1)S(1)} %bitcast.100, f32[128]{0:T(128)S(1)} %add_rsqrt_fusion, ...), kind=kLoop, calls=%fused_computation.10 | loop fusion | flops 13631360 | bytes 4228096 | tf_op jit(solution)/shard_map/reduce_sum | solution.py:126
  270.1 2.4 fusion.9
  272.5 49.7 %collective-permute-done.16 = bf16[2048,768]{1,0:T(8,128)(2,1)S(1)} collective-permute-done((bf16[2048,768]{1,0:T(8,128)(2,1)S(1)}, bf16[2048,768]{1,0:T(8,128)(2,1)S(1)}, u32[]{:S(2)}, u32[]{:S(2)}) %collective-permute-start.16) | collective-permute-done | bytes 3145760 | tf_op jit(solution)/shard_map/ppermute | solution.py:25
  322.2 8.6 %fusion.12 = bf16[1,2048,768]{2,1,0:T(8,128)(2,1)} fusion(bf16[2048,768]{1,0:T(8,128)(2,1)S(1)} %collective-permute-done.16, bf16[2048,2048]{1,0:T(8,128)(2,1)S(1)} %bitcast.119, bf16[2048,1536]{1,0:T(8,128)(2,1)S(1)} %bitcast.99), kind=kOutput, calls=%fused_computation.20 | convolution fusion | flops 6447169536 | bytes 17825792 | tf_op jit(solution)/shard_map/dot_general | solution.py:33
  (86 shorter events, 17.2 us)
Async XLA Ops:
  0.6 3.1 copy-start
  5.2 26.9 %collective-permute-start = (bf16[128,2048]{1,0:T(8,128)(2,1)}, bf16[128,2048]{1,0:T(8,128)(2,1)}, u32[]{:S(2)}, u32[]{:S(2)}) collective-permute-start(bf16[128,2048]{1,0:T(8,128)(2,1)} %get-tuple-element.12), channel_id=1, source_target_pairs={{8,0},{16,8},{24,16},{0,24},{9,1},{17,9},{25,17},{1,25},{10,2},{18... | collective-permute-start | bytes 1572872 | tf_op jit(solution)/shard_map/ppermute | solution.py:13
  9.3 26.1 %collective-permute-start.1 = (bf16[128,2048]{1,0:T(8,128)(2,1)}, bf16[128,2048]{1,0:T(8,128)(2,1)}, u32[]{:S(2)}, u32[]{:S(2)}) collective-permute-start(bf16[128,2048]{1,0:T(8,128)(2,1)} %get-tuple-element.11), channel_id=1, source_target_pairs={{24,0},{0,8},{8,16},{16,24},{25,1},{1,9},{9,17},{17,25},{26,2},{2,... | collective-permute-start | bytes 1572872 | tf_op jit(solution)/shard_map/ppermute | solution.py:13
  9.3 28.3 %collective-permute-start.2 = (bf16[128,2048]{1,0:T(8,128)(2,1)}, bf16[128,2048]{1,0:T(8,128)(2,1)}, u32[]{:S(2)}, u32[]{:S(2)}) collective-permute-start(bf16[128,2048]{1,0:T(8,128)(2,1)} %get-tuple-element.10), channel_id=1, source_target_pairs={{16,0},{24,8},{0,16},{8,24},{17,1},{25,9},{1,17},{9,25},{18,2},{26... | collective-permute-start | bytes 1572872 | tf_op jit(solution)/shard_map/ppermute | solution.py:13
  12.8 30.0 %copy-start.2 = (bf16[1,128,768]{2,1,0:T(8,128)(2,1)}, bf16[1,128,768]{2,1,0:T(8,128)(2,1)S(1)}, u32[]{:S(2)}) copy-start(bf16[1,128,768]{2,1,0:T(8,128)(2,1)S(1)} %get-tuple-element.29) | copy-start | bytes 589828
  12.9 29.9 %collective-permute-start.11 = (bf16[4,128,768]{2,1,0:T(8,128)(2,1)S(1)}, bf16[4,128,768]{2,1,0:T(8,128)(2,1)S(1)}, u32[]{:S(2)}, u32[]{:S(2)}) collective-permute-start(bf16[4,128,768]{2,1,0:T(8,128)(2,1)S(1)} %pad_maximum_fusion.5), channel_id=1, source_target_pairs={{0,4},{1,5},{2,6},{3,7},{4,0},{5,1},{6,2},{7,3},{8,12},{9,13},{10,... | collective-permute-start | bytes 2359304 | tf_op jit(solution)/shard_map/ppermute | solution.py:25
  39.8 38.2 %collective-permute-start.3 = (bf16[384,2048]{1,0:T(8,128)(2,1)}, bf16[384,2048]{1,0:T(8,128)(2,1)}, u32[]{:S(2)}, u32[]{:S(2)}) collective-permute-start(bf16[384,2048]{1,0:T(8,128)(2,1)} %get-tuple-element.34), channel_id=1, source_target_pairs={{1,0},{2,1},{3,2},{0,3},{5,4},{6,5},{7,6},{4,7},{9,8},{10,9},{11,1... | collective-permute-start | bytes 4718600 | tf_op jit(solution)/shard_map/ppermute | solution.py:17
  42.8 38.3 %collective-permute-start.6 = (bf16[384,2048]{1,0:T(8,128)(2,1)}, bf16[384,2048]{1,0:T(8,128)(2,1)}, u32[]{:S(2)}, u32[]{:S(2)}) collective-permute-start(bf16[384,2048]{1,0:T(8,128)(2,1)} %get-tuple-element.34), channel_id=1, source_target_pairs={{3,0},{0,1},{1,2},{2,3},{7,4},{4,5},{5,6},{6,7},{11,8},{8,9},{9,10... | collective-permute-start | bytes 4718600 | tf_op jit(solution)/shard_map/ppermute | solution.py:17
  44.1 56.8 %collective-permute-start.12 = (bf16[4,128,1536]{2,1,0:T(8,128)(2,1)}, bf16[4,128,1536]{2,1,0:T(8,128)(2,1)}, u32[]{:S(2)}, u32[]{:S(2)}) collective-permute-start(bf16[4,128,1536]{2,1,0:T(8,128)(2,1)} %pad_maximum_fusion.4), channel_id=1, source_target_pairs={{8,0},{16,8},{24,16},{0,24},{9,1},{17,9},{25,17},{1,25},{10,2},{18... | collective-permute-start | bytes 4718600 | tf_op jit(solution)/shard_map/ppermute | solution.py:13
  46.6 58.2 %collective-permute-start.13 = (bf16[4,128,1536]{2,1,0:T(8,128)(2,1)}, bf16[4,128,1536]{2,1,0:T(8,128)(2,1)}, u32[]{:S(2)}, u32[]{:S(2)}) collective-permute-start(bf16[4,128,1536]{2,1,0:T(8,128)(2,1)} %pad_maximum_fusion.4), channel_id=1, source_target_pairs={{24,0},{0,8},{8,16},{16,24},{25,1},{1,9},{9,17},{17,25},{26,2},{2,... | collective-permute-start | bytes 4718600 | tf_op jit(solution)/shard_map/ppermute | solution.py:13
  47.7 41.5 %collective-permute-start.4 = (bf16[128,2048]{1,0:T(8,128)(2,1)}, bf16[128,2048]{1,0:T(8,128)(2,1)}, u32[]{:S(2)}, u32[]{:S(2)}) collective-permute-start(bf16[128,2048]{1,0:T(8,128)(2,1)} %get-tuple-element.3), channel_id=1, source_target_pairs={{1,0},{2,1},{3,2},{0,3},{5,4},{6,5},{7,6},{4,7},{9,8},{10,9},{11,1... | collective-permute-start | bytes 1572872 | tf_op jit(solution)/shard_map/ppermute | solution.py:17
  77.9 14.3 %collective-permute-start.9 = (bf16[128,2048]{1,0:T(8,128)(2,1)}, bf16[128,2048]{1,0:T(8,128)(2,1)}, u32[]{:S(2)}, u32[]{:S(2)}) collective-permute-start(bf16[128,2048]{1,0:T(8,128)(2,1)} %get-tuple-element.3), channel_id=1, source_target_pairs={{3,0},{0,1},{1,2},{2,3},{7,4},{4,5},{5,6},{6,7},{11,8},{8,9},{9,10... | collective-permute-start | bytes 1572872 | tf_op jit(solution)/shard_map/ppermute | solution.py:17
  81.1 6.4 %copy-start.3 = (bf16[1,8192]{1,0:T(2,128)(2,1)S(1)}, bf16[1,8192]{1,0:T(2,128)(2,1)}, u32[]{:S(2)}) copy-start(bf16[1,8192]{1,0:T(2,128)(2,1)} %param.6) | copy-start | bytes 49156
  81.1 25.0 %collective-permute-start.5 = (bf16[192,2048]{1,0:T(8,128)(2,1)}, bf16[192,2048]{1,0:T(8,128)(2,1)}, u32[]{:S(2)}, u32[]{:S(2)}) collective-permute-start(bf16[192,2048]{1,0:T(8,128)(2,1)} %slice.155), channel_id=1, source_target_pairs={{1,0},{2,1},{3,2},{0,3},{5,4},{6,5},{7,6},{4,7},{9,8},{10,9},{11,1... | collective-permute-start | bytes 2359304 | tf_op jit(solution)/shard_map/ppermute | solution.py:17
  87.6 4.7 %copy-start.1 = (bf16[2048,768]{1,0:T(8,128)(2,1)S(1)}, bf16[2048,768]{1,0:T(8,128)(2,1)}, u32[]{:S(2)}) copy-start(bf16[2048,768]{1,0:T(8,128)(2,1)} %dynamic-slice_bitcast_fusion) | copy-start | bytes 9437188
  89.2 21.5 %collective-permute-start.7 = (bf16[192,2048]{1,0:T(8,128)(2,1)S(1)}, bf16[192,2048]{1,0:T(8,128)(2,1)S(1)}, u32[]{:S(2)}, u32[]{:S(2)}) collective-permute-start(bf16[192,2048]{1,0:T(8,128)(2,1)S(1)} %slice.156), channel_id=1, source_target_pairs={{3,0},{0,1},{1,2},{2,3},{7,4},{4,5},{5,6},{6,7},{11,8},{8,9},{9,10... | collective-permute-start | bytes 2359304 | tf_op jit(solution)/shard_map/ppermute | solution.py:17
  92.3 64.5 %collective-permute-start.18 = (bf16[2048,768]{1,0:T(8,128)(2,1)S(1)}, bf16[2048,768]{1,0:T(8,128)(2,1)S(1)}, u32[]{:S(2)}, u32[]{:S(2)}) collective-permute-start(bf16[2048,768]{1,0:T(8,128)(2,1)S(1)} %copy-done.1), channel_id=1, source_target_pairs={{0,4},{1,5},{2,6},{3,7},{4,0},{5,1},{6,2},{7,3},{8,12},{9,13},{10,... | collective-permute-start | bytes 9437192 | tf_op jit(solution)/shard_map/ppermute | solution.py:25
  101.0 10.7 %collective-permute-start.8 = (bf16[64,2048]{1,0:T(8,128)(2,1)S(1)}, bf16[64,2048]{1,0:T(8,128)(2,1)S(1)}, u32[]{:S(2)}, u32[]{:S(2)}) collective-permute-start(bf16[64,2048]{1,0:T(8,128)(2,1)S(1)} %slice.157), channel_id=1, source_target_pairs={{1,0},{2,1},{3,2},{0,3},{5,4},{6,5},{7,6},{4,7},{9,8},{10,9},{11,1... | collective-permute-start | bytes 786440 | tf_op jit(solution)/shard_map/ppermute | solution.py:17
  104.8 7.7 %collective-permute-start.10 = (bf16[64,2048]{1,0:T(8,128)(2,1)S(1)}, bf16[64,2048]{1,0:T(8,128)(2,1)S(1)}, u32[]{:S(2)}, u32[]{:S(2)}) collective-permute-start(bf16[64,2048]{1,0:T(8,128)(2,1)S(1)} %slice.158), channel_id=1, source_target_pairs={{3,0},{0,1},{1,2},{2,3},{7,4},{4,5},{5,6},{6,7},{11,8},{8,9},{9,10... | collective-permute-start | bytes 786440 | tf_op jit(solution)/shard_map/ppermute | solution.py:17
  106.1 15.3 %collective-permute-start.14 = (bf16[2,128,1536]{2,1,0:T(8,128)(2,1)S(1)}, bf16[2,128,1536]{2,1,0:T(8,128)(2,1)S(1)}, u32[]{:S(2)}, u32[]{:S(2)}) collective-permute-start(bf16[2,128,1536]{2,1,0:T(8,128)(2,1)S(1)} %slice.159), channel_id=1, source_target_pairs={{8,0},{16,8},{24,16},{0,24},{9,1},{17,9},{25,17},{1,25},{10,2},{18... | collective-permute-start | bytes 2359304 | tf_op jit(solution)/shard_map/ppermute | solution.py:13
  110.7 16.2 %collective-permute-start.15 = (bf16[2,128,1536]{2,1,0:T(8,128)(2,1)S(1)}, bf16[2,128,1536]{2,1,0:T(8,128)(2,1)S(1)}, u32[]{:S(2)}, u32[]{:S(2)}) collective-permute-start(bf16[2,128,1536]{2,1,0:T(8,128)(2,1)S(1)} %slice.160), channel_id=1, source_target_pairs={{24,0},{0,8},{8,16},{16,24},{25,1},{1,9},{9,17},{17,25},{26,2},{2,... | collective-permute-start | bytes 2359304 | tf_op jit(solution)/shard_map/ppermute | solution.py:13
  156.7 6.0 %copy-start.4 = (bf16[2048,768]{1,0:T(8,128)(2,1)}, bf16[2048,768]{1,0:T(8,128)(2,1)S(1)}, u32[]{:S(2)}) copy-start(bf16[2048,768]{1,0:T(8,128)(2,1)S(1)} %collective-permute-done.18) | copy-start | bytes 9437188
  159.5 63.5 %collective-permute-start.27 = (bf16[384,1024]{1,0:T(8,128)(2,1)S(1)}, bf16[384,1024]{1,0:T(8,128)(2,1)}, u32[]{:S(2)}, u32[]{:S(2)}) collective-permute-start(bf16[384,1024]{1,0:T(8,128)(2,1)S(1)} %slice.258), channel_id=1, source_target_pairs={{1,0},{2,1},{3,2},{0,3},{5,4},{6,5},{7,6},{4,7},{9,8},{10,9},{11,1... | collective-permute-start | bytes 2359304 | tf_op jit(solution)/shard_map/ppermute | solution.py:17
  165.6 2.2 copy-start.5
  166.6 32.3 %collective-permute-start.25 = (bf16[384,1024]{1,0:T(8,128)(2,1)}, bf16[384,1024]{1,0:T(8,128)(2,1)S(1)}, u32[]{:S(2)}, u32[]{:S(2)}) collective-permute-start(bf16[384,1024]{1,0:T(8,128)(2,1)} %get-tuple-element.20), channel_id=1, source_target_pairs={{3,0},{0,1},{1,2},{2,3},{7,4},{4,5},{5,6},{6,7},{11,8},{8,9},{9,10... | collective-permute-start | bytes 2359304 | tf_op jit(solution)/shard_map/ppermute | solution.py:17
  170.5 53.4 %collective-permute-start.30 = (bf16[384,1024]{1,0:T(8,128)(2,1)S(1)}, bf16[384,1024]{1,0:T(8,128)(2,1)}, u32[]{:S(2)}, u32[]{:S(2)}) collective-permute-start(bf16[384,1024]{1,0:T(8,128)(2,1)S(1)} %slice.257), channel_id=1, source_target_pairs={{3,0},{0,1},{1,2},{2,3},{7,4},{4,5},{5,6},{6,7},{11,8},{8,9},{9,10... | collective-permute-start | bytes 2359304 | tf_op jit(solution)/shard_map/ppermute | solution.py:17
  170.6 31.9 %collective-permute-start.28 = (bf16[384,1024]{1,0:T(8,128)(2,1)S(1)}, bf16[384,1024]{1,0:T(8,128)(2,1)S(1)}, u32[]{:S(2)}, u32[]{:S(2)}) collective-permute-start(bf16[384,1024]{1,0:T(8,128)(2,1)S(1)} %get-tuple-element.21), channel_id=1, source_target_pairs={{1,0},{2,1},{3,2},{0,3},{5,4},{6,5},{7,6},{4,7},{9,8},{10,9},{11,1... | collective-permute-start | bytes 2359304 | tf_op jit(solution)/shard_map/ppermute | solution.py:17
  177.2 29.3 %collective-permute-start.19 = (bf16[128,1024]{1,0:T(8,128)(2,1)S(1)}, bf16[128,1024]{1,0:T(8,128)(2,1)S(1)}, u32[]{:S(2)}, u32[]{:S(2)}) collective-permute-start(bf16[128,1024]{1,0:T(8,128)(2,1)S(1)} %get-tuple-element.32), channel_id=1, source_target_pairs={{3,0},{0,1},{1,2},{2,3},{7,4},{4,5},{5,6},{6,7},{11,8},{8,9},{9,10... | collective-permute-start | bytes 786440 | tf_op jit(solution)/shard_map/ppermute | solution.py:17
  199.0 21.6 %collective-permute-start.22 = (bf16[128,1024]{1,0:T(8,128)(2,1)S(1)}, bf16[128,1024]{1,0:T(8,128)(2,1)}, u32[]{:S(2)}, u32[]{:S(2)}) collective-permute-start(bf16[128,1024]{1,0:T(8,128)(2,1)S(1)} %get-tuple-element.33), channel_id=1, source_target_pairs={{1,0},{2,1},{3,2},{0,3},{5,4},{6,5},{7,6},{4,7},{9,8},{10,9},{11,1... | collective-permute-start | bytes 786440 | tf_op jit(solution)/shard_map/ppermute | solution.py:17
  202.5 22.5 %collective-permute-start.26 = (bf16[384,1024]{1,0:T(8,128)(2,1)S(1)}, bf16[384,1024]{1,0:T(8,128)(2,1)S(1)}, u32[]{:S(2)}, u32[]{:S(2)}) collective-permute-start(bf16[384,1024]{1,0:T(8,128)(2,1)S(1)} %fusion.18), channel_id=1, source_target_pairs={{3,0},{0,1},{1,2},{2,3},{7,4},{4,5},{5,6},{6,7},{11,8},{8,9},{9,10... | collective-permute-start | bytes 2359304 | tf_op jit(solution)/shard_map/ppermute | solution.py:17
  206.5 21.1 %collective-permute-start.29 = (bf16[384,1024]{1,0:T(8,128)(2,1)S(1)}, bf16[384,1024]{1,0:T(8,128)(2,1)S(1)}, u32[]{:S(2)}, u32[]{:S(2)}) collective-permute-start(bf16[384,1024]{1,0:T(8,128)(2,1)S(1)} %fusion.15), channel_id=1, source_target_pairs={{1,0},{2,1},{3,2},{0,3},{5,4},{6,5},{7,6},{4,7},{9,8},{10,9},{11,1... | collective-permute-start | bytes 2359304 | tf_op jit(solution)/shard_map/ppermute | solution.py:17
  220.6 49.5 %collective-permute-start.17 = (bf16[1,128,8192]{2,1,0:T(8,128)(2,1)}, bf16[1,128,8192]{2,1,0:T(8,128)(2,1)S(1)}, u32[]{:S(2)}, u32[]{:S(2)}) collective-permute-start(bf16[1,128,8192]{2,1,0:T(8,128)(2,1)} %param.9), channel_id=1, source_target_pairs={{32,0},{64,32},{96,64},{33,1},{65,33},{97,65},{34,2},{66,34},{98,6... | collective-permute-start | bytes 6291464 | tf_op jit(solution)/shard_map/ppermute | solution.py:58
  222.9 10.3 %collective-permute-start.21 = (bf16[128,1024]{1,0:T(8,128)(2,1)S(1)}, bf16[128,1024]{1,0:T(8,128)(2,1)S(1)}, u32[]{:S(2)}, u32[]{:S(2)}) collective-permute-start(bf16[128,1024]{1,0:T(8,128)(2,1)S(1)} %slice.260), channel_id=1, source_target_pairs={{1,0},{2,1},{3,2},{0,3},{5,4},{6,5},{7,6},{4,7},{9,8},{10,9},{11,1... | collective-permute-start | bytes 786440 | tf_op jit(solution)/shard_map/ppermute | solution.py:17
  223.9 11.4 %collective-permute-start.24 = (bf16[128,1024]{1,0:T(8,128)(2,1)S(1)}, bf16[128,1024]{1,0:T(8,128)(2,1)S(1)}, u32[]{:S(2)}, u32[]{:S(2)}) collective-permute-start(bf16[128,1024]{1,0:T(8,128)(2,1)S(1)} %slice.259), channel_id=1, source_target_pairs={{3,0},{0,1},{1,2},{2,3},{7,4},{4,5},{5,6},{6,7},{11,8},{8,9},{9,10... | collective-permute-start | bytes 786440 | tf_op jit(solution)/shard_map/ppermute | solution.py:17
  225.0 18.0 %collective-permute-start.20 = (bf16[128,1024]{1,0:T(8,128)(2,1)S(1)}, bf16[128,1024]{1,0:T(8,128)(2,1)S(1)}, u32[]{:S(2)}, u32[]{:S(2)}) collective-permute-start(bf16[128,1024]{1,0:T(8,128)(2,1)S(1)} %fusion.34), channel_id=1, source_target_pairs={{3,0},{0,1},{1,2},{2,3},{7,4},{4,5},{5,6},{6,7},{11,8},{8,9},{9,10... | collective-permute-start | bytes 786440 | tf_op jit(solution)/shard_map/ppermute | solution.py:17
  227.7 23.2 %collective-permute-start.23 = (bf16[128,1024]{1,0:T(8,128)(2,1)S(1)}, bf16[128,1024]{1,0:T(8,128)(2,1)S(1)}, u32[]{:S(2)}, u32[]{:S(2)}) collective-permute-start(bf16[128,1024]{1,0:T(8,128)(2,1)S(1)} %fusion.31), channel_id=1, source_target_pairs={{1,0},{2,1},{3,2},{0,3},{5,4},{6,5},{7,6},{4,7},{9,8},{10,9},{11,1... | collective-permute-start | bytes 786440 | tf_op jit(solution)/shard_map/ppermute | solution.py:17
  233.1 14.7 %copy-start.6 = (bf16[2048,768]{1,0:T(8,128)(2,1)S(1)}, bf16[2048,768]{1,0:T(8,128)(2,1)}, u32[]{:S(2)}) copy-start(bf16[2048,768]{1,0:T(8,128)(2,1)} %copy-done.4) | copy-start | bytes 9437188
  233.3 21.0 %collective-permute-start.33 = (bf16[128,2048]{1,0:T(8,128)(2,1)S(1)}, bf16[128,2048]{1,0:T(8,128)(2,1)S(1)}, u32[]{:S(2)}, u32[]{:S(2)}) collective-permute-start(bf16[128,2048]{1,0:T(8,128)(2,1)S(1)} %get-tuple-element.18), channel_id=1, source_target_pairs={{24,0},{0,8},{8,16},{16,24},{25,1},{1,9},{9,17},{17,25},{26,2},{2,... | collective-permute-start | bytes 1572872 | tf_op jit(solution)/shard_map/ppermute | solution.py:13
  235.3 29.8 %collective-permute-start.32 = (bf16[128,2048]{1,0:T(8,128)(2,1)S(1)}, bf16[128,2048]{1,0:T(8,128)(2,1)S(1)}, u32[]{:S(2)}, u32[]{:S(2)}) collective-permute-start(bf16[128,2048]{1,0:T(8,128)(2,1)S(1)} %get-tuple-element.19), channel_id=1, source_target_pairs={{16,0},{24,8},{0,16},{8,24},{17,1},{25,9},{1,17},{9,25},{18,2},{26... | collective-permute-start | bytes 1572872 | tf_op jit(solution)/shard_map/ppermute | solution.py:13
  243.0 7.9 %copy-start.7 = (bf16[2048,768]{1,0:T(8,128)(2,1)S(1)}, bf16[2048,768]{1,0:T(8,128)(2,1)}, u32[]{:S(2)}) copy-start(bf16[2048,768]{1,0:T(8,128)(2,1)} %convolution_convert_fusion) | copy-start | bytes 9437188
  243.0 23.1 %collective-permute-start.31 = (bf16[128,2048]{1,0:T(8,128)(2,1)S(1)}, bf16[128,2048]{1,0:T(8,128)(2,1)S(1)}, u32[]{:S(2)}, u32[]{:S(2)}) collective-permute-start(bf16[128,2048]{1,0:T(8,128)(2,1)S(1)} %get-tuple-element.17), channel_id=1, source_target_pairs={{8,0},{16,8},{24,16},{0,24},{9,1},{17,9},{25,17},{1,25},{10,2},{18... | collective-permute-start | bytes 1572872 | tf_op jit(solution)/shard_map/ppermute | solution.py:13
  250.9 71.3 %collective-permute-start.16 = (bf16[2048,768]{1,0:T(8,128)(2,1)S(1)}, bf16[2048,768]{1,0:T(8,128)(2,1)S(1)}, u32[]{:S(2)}, u32[]{:S(2)}) collective-permute-start(bf16[2048,768]{1,0:T(8,128)(2,1)S(1)} %copy-done.7), channel_id=1, source_target_pairs={{0,4},{1,5},{2,6},{3,7},{4,0},{5,1},{6,2},{7,3},{8,12},{9,13},{10,... | collective-permute-start | bytes 9437192 | tf_op jit(solution)/shard_map/ppermute | solution.py:25
  266.3 55.9 %slice-start = ((s8[8388608]{0:T(1024)(128)(4,1)}), s8[4194304]{0:T(1024)(128)(4,1)S(1)}, s32[]{:S(2)}) async-start(s8[8388608]{0:T(1024)(128)(4,1)} %bitcast.118), calls=%async_computation | async-start | bytes 8388608
  266.6 55.6 %slice-start.1 = ((s8[8388608]{0:T(1024)(128)(4,1)}), s8[4194304]{0:T(1024)(128)(4,1)S(1)}, s32[]{:S(2)}) async-start(s8[8388608]{0:T(1024)(128)(4,1)} %bitcast.118), calls=%async_computation.1 | async-start | bytes 8388608

commit v2 on v0

v2 whole, which is shorter than its diff:
```python
import functools

import jax
import jax.numpy as jnp
from jax import lax
from jax.experimental import pallas as pl
from jax.experimental.pallas import tpu as pltpu
from jax.sharding import PartitionSpec as P

N_Z = 4
N_Y = 4
F32 = jnp.float32
BF16 = jnp.bfloat16
VMEM_BYTES = 40 * 2**20


class Chains:
    def __init__(self):
        self.last = {}

    def __call__(self, key, block, send):
        if key in self.last:
            block, _ = lax.optimization_barrier((block, self.last[key]))
        self.last[key] = send(block)
        return self.last[key]


def from_z(block, o):
    return lax.ppermute(block, "dp", [((i + o) % N_Z, i) for i in range(N_Z)])


def from_y(block, o):
    return lax.ppermute(
        block,
        "tensor",
        [(x * N_Y + (i + o) % N_Y, x * N_Y + i) for x in range(2) for i in range(N_Y)],
    )


def from_x(block):
    return lax.ppermute(block, "tensor", [(i, (i + N_Y) % (2 * N_Y)) for i in range(2 * N_Y)])


def dot_nt(a, b):
    return lax.dot_general(a, b, (((1,), (1,)), ((), ())), preferred_element_type=F32)


def dot_nn(a, b):
    return lax.dot_general(a, b, (((1,), (0,)), ((), ())), preferred_element_type=F32)


def call(kernel, grid, in_specs, out_specs, out_shape, flops=0, bytes_accessed=0, name=None):
    return pl.pallas_call(
        kernel,
        grid=grid,
        in_specs=in_specs,
        out_specs=out_specs,
        out_shape=out_shape,
        name=name,
        compiler_params=pltpu.CompilerParams(vmem_limit_bytes=VMEM_BYTES),
        cost_estimate=pl.CostEstimate(
            flops=flops, bytes_accessed=bytes_accessed, transcendentals=0
        ),
    )


SMEM = pl.BlockSpec(memory_space=pltpu.SMEM)
WHOLE = pl.BlockSpec(memory_space=pltpu.VMEM)


def normalize(z, hidden, gain):
    rows, width = hidden.shape
    part = width // N_Z

    def kernel(z_ref, h_ref, g_ref, r_ref, *out_refs):
        x = h_ref[...].astype(F32)
        r = lax.rsqrt(jnp.mean(x * x, axis=-1, keepdims=True) + 1e-06)
        r_ref[...] = jnp.broadcast_to(r, r_ref.shape)
        for d in range(N_Z):
            at = pl.multiple_of(lax.rem(z_ref[0] + d, N_Z) * part, part)
            x = h_ref[:, pl.ds(at, part)].astype(F32)
            g = g_ref[:, pl.ds(at, part)].astype(F32)
            out_refs[d][...] = ((x * r) * g).T.astype(BF16)

    return call(
        kernel,
        (),
        [SMEM, WHOLE, WHOLE],
        [WHOLE] * (1 + N_Z),
        [jax.ShapeDtypeStruct((rows, 128), F32)]
        + [jax.ShapeDtypeStruct((part, rows), BF16)] * N_Z,
        bytes_accessed=4 * rows * width,
        name="normalize",
    )(z, hidden, gain)


def partial_sums(jobs, g_own, g_par, w_own, w_par, extras, per_sequence=False):
    _, rows, cols = g_own[0].shape
    part = w_own.shape[0]
    half = part // 2
    step = 256
    steps = half // step
    qs = sorted({q for q, _, _ in jobs})
    sides = sorted({side for _, side, _ in jobs})
    n_g, n_w, n_e = 2 * N_Z * len(qs), 2 * len(sides), len(extras)

    def kernel(*refs):
        g_refs, w_refs = refs[:n_g], refs[n_g : n_g + n_w]
        e_refs, outs = refs[n_g + n_w : n_g + n_w + n_e], refs[n_g + n_w + n_e :]
        for k, (q, side, adds) in enumerate(jobs):
            at = qs.index(q) * 2 * N_Z
            left = jnp.concatenate([g_refs[at + o][0] for o in range(N_Z)], 0)
            right = jnp.concatenate([g_refs[at + N_Z + o][0] for o in range(N_Z)], 0)
            s = sides.index(side) * 2
            total = dot_nt(left, w_refs[s][...]) + dot_nt(right, w_refs[s + 1][...])
            total = total.reshape(N_Z, rows, step)
            for e in adds:
                total = total + e_refs[e][...].astype(F32)
            if per_sequence:
                for o in range(N_Z):
                    outs[o][side] = total[o].astype(BF16)
            else:
                outs[k][...] = total.astype(BF16)

    in_specs, operands = [], []
    for q in qs:
        for arrays in (g_own, g_par):
            for o in range(N_Z):
                in_specs.append(pl.BlockSpec((1, rows, cols), functools.partial(lambda q, i: (q, 0, 0), q)))
                operands.append(arrays[o])
    for side in sides:
        for w in (w_own, w_par):
            in_specs.append(
                pl.BlockSpec((step, cols), functools.partial(lambda s, i: (s * steps + i, 0), side))
            )
            operands.append(w)
    chunk = pl.BlockSpec((N_Z, rows, step), lambda i: (0, 0, i))
    in_specs += [chunk] * n_e
    operands += list(extras)
    if per_sequence:
        out_specs = [pl.BlockSpec((2, rows, step), lambda i: (0, 0, i))] * N_Z
        out_shape = [jax.ShapeDtypeStruct((2, rows, half), BF16)] * N_Z
    else:
        out_specs = [chunk] * len(jobs)
        out_shape = [jax.ShapeDtypeStruct((N_Z, rows, half), BF16)] * len(jobs)
    return call(
        kernel, (steps,), in_specs, out_specs, out_shape, name="partial_sums"
    )(*operands)


def weight_terms(n_pieces, g):
    part, rows = n_pieces[0][0].shape
    cols = g[0].shape[2]
    step = 256

    def kernel(*refs):
        n_refs, g_refs, out_ref = refs[: N_Z * N_Y], refs[N_Z * N_Y : -1], refs[-1]
        total = None
        for o in range(N_Z):
            left = jnp.concatenate([n_refs[o * N_Y + q][...] for q in range(N_Y)], 1)
            term = dot_nn(left, g_refs[o][...].reshape(N_Y * rows, cols))
            total = term if total is None else total + term
        out_ref[...] = total.astype(BF16)

    return call(
        kernel,
        (part // step,),
        [pl.BlockSpec((step, rows), lambda i: (i, 0))] * (N_Z * N_Y)
        + [pl.BlockSpec((N_Y, rows, cols), lambda i: (0, 0, 0))] * N_Z,
        pl.BlockSpec((step, cols), lambda i: (i, 0)),
        jax.ShapeDtypeStruct((part, cols), BF16),
        name="weight_terms",
    )(*[n_pieces[o][q] for o in range(N_Z) for q in range(N_Y)], *g)


def finish(z, deviation, gain, hidden, received, h):
    rows, width = hidden.shape
    part = width // N_Z
    half = part // 2
    step = 32

    def kernel(z_ref, r_ref, g_ref, x_ref, u_ref, *refs):
        h_refs, out_ref = refs[:-1], refs[-1]
        r = r_ref[:, :1]
        spots = [
            (o, s, pl.multiple_of(lax.rem(z_ref[0] + o, N_Z) * part + s * half, half))
            for o in range(N_Z)
            for s in range(2)
        ]

        def terms(o, s, at):
            xhat = x_ref[:, pl.ds(at, half)].astype(F32) * r
            scaled = g_ref[:, pl.ds(at, half)].astype(F32) * h_refs[o][s].astype(F32)
            return xhat, scaled

        total = jnp.zeros((step, 1), F32)
        for spot in spots:
            xhat, scaled = terms(*spot)
            total += jnp.sum(scaled * xhat, axis=-1, keepdims=True)
        mean = total / width
        for spot in spots:
            xhat, scaled = terms(*spot)
            at = spot[2]
            up = u_ref[0, :, pl.ds(at, half)].astype(F32)
            out_ref[0, :, pl.ds(at, half)] = (up + r * (scaled - xhat * mean)).astype(BF16)

    return call(
        kernel,
        (rows // step,),
        [
            SMEM,
            pl.BlockSpec((step, 128), lambda i: (i, 0)),
            pl.BlockSpec((1, width), lambda i: (0, 0)),
            pl.BlockSpec((step, width), lambda i: (i, 0)),
            pl.BlockSpec((1, step, width), lambda i: (0, i, 0)),
        ]
        + [pl.BlockSpec((2, step, half), lambda i: (0, i, 0))] * N_Z,
        pl.BlockSpec((1, step, width), lambda i: (0, i, 0)),
        jax.ShapeDtypeStruct((1, rows, width), BF16),
        name="finish",
    )(z, deviation, gain, hidden, received, *h)


def shards(hidden_in, norm_gain, qkv_weight, qkv_grad, upper_grad):
    place = lax.axis_index("tensor")
    xh, y, z = place // N_Y, place % N_Y, lax.axis_index("dp")
    z_array = z.reshape(1).astype(jnp.int32)
    rows = hidden_in.shape[1]
    part = hidden_in.shape[2] // N_Z
    cols = qkv_grad.shape[2]
    layers = lax.axis_size("pipe")

    chains = Chains()

    def zz(block, o):
        return chains("z%d" % o, block, lambda b: from_z(b, o))

    def yy(block, o):
        return chains("y%d" % o, block, lambda b: from_y(b, o))

    def xx(block):
        return chains("x", block, from_x)

    grads = qkv_grad[0].reshape(2, N_Y, rows, cols)

    def turned(which):
        side = lax.dynamic_index_in_dim(grads, which, 0, keepdims=False)
        return jnp.concatenate(
            [lax.dynamic_slice_in_dim(side, (y + q) % N_Y, 1, 0) for q in range(N_Y)], 0
        )

    par0 = xx(turned(1 - xh))
    own0 = turned(xh)
    w_own = lax.dynamic_slice_in_dim(qkv_weight[0], z * part, part, 0)
    w_par = xx(w_own)
    received = lax.ppermute(upper_grad, "pipe", [(i + 1, i) for i in range(layers - 1)])

    deviation, *n_to = normalize(z_array, hidden_in[0], norm_gain)
    n_near = [n_to[0], zz(n_to[3], 1), zz(n_to[2], 2), zz(n_to[1], 3)]

    n_pieces = []
    for o, piece in enumerate(n_near):
        up, down = yy(piece, 1), yy(piece, 3)
        across = yy(up, 1) if o in (0, 1) else yy(down, 3)
        n_pieces.append([piece, up, across, down])

    own1, own3 = zz(own0, 1), zz(own0, 3)
    own2 = zz(own1, 1)
    par1, par3 = zz(par0, 1), zz(par0, 3)
    par2 = zz(par3, 3)
    g_own, g_par = [own0, own1, own2, own3], [par0, par1, par2, par3]

    sums = functools.partial(partial_sums, g_own=g_own, g_par=g_par, w_own=w_own, w_par=w_par)
    p2a, p2b = sums([(2, 0, ()), (2, 1, ())], extras=[])
    hop_up, hop_down = yy(p2a, 3), yy(p2b, 1)
    p1b, p3a = sums([(1, 1, ()), (3, 0, ())], extras=[])
    up_b, down_a = yy(p1b, 3), yy(p3a, 1)
    p1a, p3b = sums([(1, 0, (0,)), (3, 1, (1,))], extras=[hop_up, hop_down])
    up_a, down_b = yy(p1a, 3), yy(p3b, 1)
    h_to = sums(
        [(0, 0, (0, 1)), (0, 1, (2, 3))],
        extras=[up_a, down_a, down_b, up_b],
        per_sequence=True,
    )
    h = [h_to[0], zz(h_to[3], 1), zz(h_to[2], 2), zz(h_to[1], 3)]

    dw_got = xx(weight_terms(n_pieces, g_par))
    dw_own = weight_terms(n_pieces, g_own)
    weight_out = (dw_own.astype(F32) + dw_got.astype(F32)).astype(BF16)

    input_out = finish(z_array, deviation, norm_gain, hidden_in[0], received, h)
    return (weight_out[None], input_out)


def solution(mesh):
    placed = (
        P("pipe", ("dp", "tensor"), None),
        P("pipe", None),
        P("pipe", None, "tensor"),
        P("pipe", "dp", "tensor"),
        P("pipe", ("dp", "tensor"), None),
    )
    return jax.shard_map(
        shards,
        mesh=mesh,
        in_specs=placed,
        out_specs=(P("pipe", "dp", "tensor"), P("pipe", ("dp", "tensor"), None)),
        check_vma=False,
    )
```

time: 566 us -> 223 us (0.39)
  waiting for transfers between devices: 495 us -> 87.4 us
  starting transfers between devices: 1.41 us -> 64.3 us
  Pallas kernels: 0 us -> 49.3 us
  matrix products: 42.6 us -> 0 us
  between operations: 13.8 us -> 0.9 us
  local copies, waits for them, and re-layouts: 1.49 us -> 12.6 us
    reduce_scatter x2 -> x0, waiting for transfers between devices: 312 us -> none  [the longest x1 199 us: shards(): lax.psum_scatter(lax.dot_general(grads, weight, (((1,), (1,)), ((), ())),...]
    all_gather x1 -> x0, waiting for transfers between devices: 183 us -> none  [shards(): gathered = lax.all_gather(normed_input, 'tensor', axis=0, tiled=True)]
    ppermute x1 -> x34, waiting for transfers between devices: 0.01 us -> 87.4 us  [the longest x12 49.4 us: from_z(): return lax.ppermute(block, 'dp', [((i + o) % N_Z, i) for i in range(N_Z)])]
    ppermute x1 -> x34, starting transfers between devices: 1.29 us -> 64.3 us  [the longest x18 29.1 us: from_y(): lax.ppermute(block, 'tensor', [(x * N_Y + (i + o) % N_Y, x * N_Y + i) for...]
    pallas_call x0 -> x8, Pallas kernels: none -> 49.3 us  [the longest x4 24.5 us: partial_sums(): call(kernel, (steps,), in_specs, out_specs, out_shape, name='partial_sums')]
    dot_general x2 -> x0, matrix products: 42.6 us -> none  [the longest x1 22.3 us: shards(): lax.dot_general(gathered, grads, (((0,), (0,)), ((), ())), preferred_elem...]
    unnamed x8 -> x40, local copies, waits for them, and re-layouts: 1.49 us -> 7.83 us
  transfers between devices with their start and end apart: 4 -> 34, of which waited for: 3 -> 17; matrix products, arithmetic and copies ran while one was open for 1% -> 3% of each run, Pallas kernels for 0% -> 20%
where the time goes in v2:
time: 223 us; the launch traced here: 220 us
  waiting for transfers between devices  87.4 us (39%)
  starting transfers between devices  64.3 us (29%)
  Pallas kernels  49.3 us (22%)
  local copies, waits for them, and re-layouts  12.6 us (6%)
  other arithmetic  5.42 us (2%)
    ppermute x12, waiting for transfers between devices, from_z(): return lax.ppermute(block, 'dp', [((i + o) % N_Z, i) for i in range(N_Z)])  49.4 us
    ppermute x18, waiting for transfers between devices, from_y(): lax.ppermute(block, 'tensor', [(x * N_Y + (i + o) % N_Y, x * N_Y + i) for...  33.2 us
    ppermute x18, starting transfers between devices, from_y(): lax.ppermute(block, 'tensor', [(x * N_Y + (i + o) % N_Y, x * N_Y + i) for...  29.1 us
    ppermute x12, starting transfers between devices, from_z(): return lax.ppermute(block, 'dp', [((i + o) % N_Z, i) for i in range(N_Z)])  27.5 us
    pallas_call x4, Pallas kernels, partial_sums(): call(kernel, (steps,), in_specs, out_specs, out_shape, name='partial_sums')  24.5 us
    pallas_call x2, Pallas kernels, weight_terms(): call(kernel, (part // step,), [pl.BlockSpec((step, rows), lambda i: (i, 0...  17.5 us
    unnamed x40, local copies, waits for them, and re-layouts  7.83 us
    ppermute x3, starting transfers between devices, from_x(): lax.ppermute(block, 'tensor', [(i, (i + N_Y) % (2 * N_Y)) for i in range(...  6.55 us
  transfers between devices with their start and end apart: 34, of which 17 were waited for; matrix products, arithmetic and copies ran while one was open for 3% of the time, Pallas kernels for 20%

profile of v2, /device:TPU:0, one launch (start us, length us, event | category | flops | bytes accessed | tf_op | source)
XLA Modules:
  0.0 219.9 jit_solution(16672897218278737911)
XLA Ops:
  0.8 2.5 %dynamic-slice_bitcast_fusion.8 = (bf16[1,128,768]{2,1,0:T(8,128)(2,1)}, bf16[1,128,768]{2,1,0:T(8,128)(2,1)S(1)}, bf16[1,128,768]{2,1,0:T(8,128)(2,1)S(1)}, bf1...) fusion(bf16[2,4,128,768]{3,2,1,0:T(8,128)(2,1)} %bitcast.25, ...), kind=kLoop, calls=%fused_computation.12 | loop fusion | bytes 3145752 | tf_op jit(solution)/shard_map/dynamic_slice | solution.py:249
  3.3 1.0 pad_maximum_fusion.1
  4.3 3.1 %collective-permute-start.18 = (bf16[4,128,768]{2,1,0:T(8,128)(2,1)}, bf16[4,128,768]{2,1,0:T(8,128)(2,1)S(1)}, u32[]{:S(2)}, u32[]{:S(2)}) collective-permute-start(bf16[4,128,768]{2,1,0:T(8,128)(2,1)} %pad_maximum_fusion.1), channel_id=1, source_target_pairs={{0,4},{1,5},{2,6},{3,7},{4,0},{5,1},{6,2},{7,3},{8,12},{9,13},{10,... | collective-permute-start | bytes 2359304 | tf_op jit(solution)/shard_map/ppermute | solution.py:41
  7.4 2.1 normalize.1
  9.5 0.8 copy-done.11
  10.3 0.8 copy-done.13
  11.0 3.0 %collective-permute-start = (bf16[2048,128]{1,0:T(8,128)(2,1)S(1)}, bf16[2048,128]{1,0:T(8,128)(2,1)S(1)}, u32[]{:S(2)}, u32[]{:S(2)}) collective-permute-start(bf16[2048,128]{1,0:T(8,128)(2,1)S(1)} %get-tuple-element.44.refs_0_), channel_id=1, source_target_pairs={{1,0},{2,1},{3,2},{0,3},{5,4},{6,5},{7,6},{4,7},{9,8},{10,9},{11,1... | collective-permute-start | bytes 1572872 | tf_op jit(solution)/shard_map/ppermute | solution.py:33
  14.1 4.0 %collective-permute-start.3 = (bf16[2048,128]{1,0:T(8,128)(2,1)}, bf16[2048,128]{1,0:T(8,128)(2,1)S(1)}, u32[]{:S(2)}, u32[]{:S(2)}) collective-permute-start(bf16[2048,128]{1,0:T(8,128)(2,1)} %get-tuple-element.46), channel_id=1, source_target_pairs={{8,0},{16,8},{24,16},{0,24},{9,1},{17,9},{25,17},{1,25},{10,2},{18... | collective-permute-start | bytes 1572872 | tf_op jit(solution)/shard_map/ppermute | solution.py:29
  18.1 2.2 %dynamic-slice_bitcast_fusion.refs_8_.refs_10_.refs_16_.refs_18_ = bf16[2048,768]{1,0:T(8,128)(2,1)S(1)} fusion(bf16[1,8192,768]{2,1,0:T(8,128)(2,1)} %param.7, s32[]{:T(128)S(6)} %select_n.91), kind=kLoop, calls=%fused_computation.2 | loop fusion | bytes 6291460 | tf_op jit(solution)/shard_map/dynamic_slice | solution.py:254
  20.4 4.8 %collective-permute-done.18.refs_16_.refs_4_.refs_12_ = bf16[4,128,768]{2,1,0:T(8,128)(2,1)S(1)} collective-permute-done((bf16[4,128,768]{2,1,0:T(8,128)(2,1)}, bf16[4,128,768]{2,1,0:T(8,128)(2,1)S(1)}, u32[]{:S(2)}, u32[]{:S(2)}) %collective-permute-start.18) | collective-permute-done | bytes 786464 | tf_op jit(solution)/shard_map/ppermute | solution.py:41
  25.1 3.2 %collective-permute-start.22 = (bf16[2048,768]{1,0:T(8,128)(2,1)S(1)}, bf16[2048,768]{1,0:T(8,128)(2,1)}, u32[]{:S(2)}, u32[]{:S(2)}) collective-permute-start(bf16[2048,768]{1,0:T(8,128)(2,1)S(1)} %dynamic-slice_bitcast_fusion.refs_8_.refs_10_.refs_16_.refs_18_), channel_id=1, source_target_pairs={{0,4},{1,5},{2,6},{3,7},{4,0},{5,1},{6,2},{7,3},{8,12},{9,13},{10,... | collective-permute-start | bytes 9437192 | tf_op jit(solution)/shard_map/ppermute | solution.py:41
  28.4 1.9 collective-permute-start.11
  30.3 3.6 %collective-permute-start.7 = (bf16[2048,128]{1,0:T(8,128)(2,1)S(1)}, bf16[2048,128]{1,0:T(8,128)(2,1)S(1)}, u32[]{:S(2)}, u32[]{:S(2)}) collective-permute-start(bf16[2048,128]{1,0:T(8,128)(2,1)S(1)} %copy-done.12), channel_id=1, source_target_pairs={{16,0},{24,8},{0,16},{8,24},{17,1},{25,9},{1,17},{9,25},{18,2},{26... | collective-permute-start | bytes 1572872 | tf_op jit(solution)/shard_map/ppermute | solution.py:29
  33.9 1.6 collective-permute-start.6
  35.5 1.7 collective-permute-start.1
  37.3 7.1 %collective-permute-done.11.refs_12_ = bf16[2048,128]{1,0:T(8,128)(2,1)S(1)} collective-permute-done((bf16[2048,128]{1,0:T(8,128)(2,1)S(1)}, bf16[2048,128]{1,0:T(8,128)(2,1)S(1)}, u32[]{:S(2)}, u32[]{:S(2)}) %collective-permute-start.11) | collective-permute-done | bytes 524320 | tf_op jit(solution)/shard_map/ppermute | solution.py:29
  44.4 2.9 %collective-permute-start.15 = (bf16[4,128,768]{2,1,0:T(8,128)(2,1)S(1)}, bf16[4,128,768]{2,1,0:T(8,128)(2,1)S(1)}, u32[]{:S(2)}, u32[]{:S(2)}) collective-permute-start(bf16[4,128,768]{2,1,0:T(8,128)(2,1)S(1)} %pad_maximum_fusion.refs_16_.refs_0_.refs_8_), channel_id=1, source_target_pairs={{8,0},{16,8},{24,16},{0,24},{9,1},{17,9},{25,17},{1,25},{10,2},{18... | collective-permute-start | bytes 2359304 | tf_op jit(solution)/shard_map/ppermute | solution.py:29
  47.3 9.5 %collective-permute-done.7.refs_8_ = bf16[2048,128]{1,0:T(8,128)(2,1)S(1)} collective-permute-done((bf16[2048,128]{1,0:T(8,128)(2,1)S(1)}, bf16[2048,128]{1,0:T(8,128)(2,1)S(1)}, u32[]{:S(2)}, u32[]{:S(2)}) %collective-permute-start.7) | collective-permute-done | bytes 524320 | tf_op jit(solution)/shard_map/ppermute | solution.py:29
  56.8 1.6 collective-permute-start.9
  58.4 1.7 collective-permute-start.4
  60.1 0.8 copy-done.3
  60.9 6.3 %collective-permute-done.15.refs_17_.refs_1_.refs_9_ = bf16[4,128,768]{2,1,0:T(8,128)(2,1)S(1)} collective-permute-done((bf16[4,128,768]{2,1,0:T(8,128)(2,1)S(1)}, bf16[4,128,768]{2,1,0:T(8,128)(2,1)S(1)}, u32[]{:S(2)}, u32[]{:S(2)}) %collective-permute-start.15) | collective-permute-done | bytes 786464 | tf_op jit(solution)/shard_map/ppermute | solution.py:29
  67.2 4.4 %collective-permute-start.16 = (bf16[4,128,768]{2,1,0:T(8,128)(2,1)S(1)}, bf16[4,128,768]{2,1,0:T(8,128)(2,1)S(1)}, u32[]{:S(2)}, u32[]{:S(2)}) collective-permute-start(bf16[4,128,768]{2,1,0:T(8,128)(2,1)S(1)} %collective-permute-done.15.refs_17_.refs_1_.refs_9_), channel_id=1, source_target_pairs={{8,0},{16,8},{24,16},{0,24},{9,1},{17,9},{25,17},{1,25},{10,2},{18... | collective-permute-start | bytes 2359304 | tf_op jit(solution)/shard_map/ppermute | solution.py:29
  71.7 2.5 %collective-permute-done.17.refs_19_.refs_3_.refs_11_ = bf16[4,128,768]{2,1,0:T(8,128)(2,1)S(1)} collective-permute-done((bf16[4,128,768]{2,1,0:T(8,128)(2,1)S(1)}, bf16[4,128,768]{2,1,0:T(8,128)(2,1)S(1)}, u32[]{:S(2)}, u32[]{:S(2)}) %collective-permute-start.17) | collective-permute-done | bytes 786464 | tf_op jit(solution)/shard_map/ppermute | solution.py:29
  74.1 1.6 collective-permute-start.10
  75.7 1.8 collective-permute-start.5
  77.5 8.7 %collective-permute-done.10.refs_10_ = bf16[2048,128]{1,0:T(8,128)(2,1)S(1)} collective-permute-done((bf16[2048,128]{1,0:T(8,128)(2,1)S(1)}, bf16[2048,128]{1,0:T(8,128)(2,1)S(1)}, u32[]{:S(2)}, u32[]{:S(2)}) %collective-permute-start.10) | collective-permute-done | bytes 524320 | tf_op jit(solution)/shard_map/ppermute | solution.py:33
  86.2 1.5 collective-permute-start.13
  87.7 1.7 collective-permute-start.8
  89.4 3.3 %collective-permute-start.19 = (bf16[4,128,768]{2,1,0:T(8,128)(2,1)S(1)}, bf16[4,128,768]{2,1,0:T(8,128)(2,1)S(1)}, u32[]{:S(2)}, u32[]{:S(2)}) collective-permute-start(bf16[4,128,768]{2,1,0:T(8,128)(2,1)S(1)} %collective-permute-done.18.refs_16_.refs_4_.refs_12_), channel_id=1, source_target_pairs={{8,0},{16,8},{24,16},{0,24},{9,1},{17,9},{25,17},{1,25},{10,2},{18... | collective-permute-start | bytes 2359304 | tf_op jit(solution)/shard_map/ppermute | solution.py:29
  93.3 5.1 %collective-permute-done.13.refs_15_ = bf16[2048,128]{1,0:T(8,128)(2,1)S(1)} collective-permute-done((bf16[2048,128]{1,0:T(8,128)(2,1)S(1)}, bf16[2048,128]{1,0:T(8,128)(2,1)S(1)}, u32[]{:S(2)}, u32[]{:S(2)}) %collective-permute-start.13) | collective-permute-done | bytes 524320 | tf_op jit(solution)/shard_map/ppermute | solution.py:33
  98.4 1.5 collective-permute-start.14
  100.2 1.7 collective-permute-start.12
  101.9 0.9 collective-permute-done.19.refs_17_.refs_5_.refs_13_
  102.9 5.9 %collective-permute-done.21.refs_18_.refs_6_.refs_14_ = bf16[4,128,768]{2,1,0:T(8,128)(2,1)S(1)} collective-permute-done((bf16[4,128,768]{2,1,0:T(8,128)(2,1)S(1)}, bf16[4,128,768]{2,1,0:T(8,128)(2,1)S(1)}, u32[]{:S(2)}, u32[]{:S(2)}) %collective-permute-start.21) | collective-permute-done | bytes 786464 | tf_op jit(solution)/shard_map/ppermute | solution.py:29
  108.8 6.2 %partial_sums.4 = (bf16[4,128,1024]{2,1,0:T(8,128)(2,1)}, bf16[4,128,1024]{2,1,0:T(8,128)(2,1)S(1)}) custom-call(bf16[4,128,768]{2,1,0:T(8,128)(2,1)S(1)} %pad_maximum_fusion.refs_16_.refs_0_.refs_8_, bf16[4,128,768]{2,1,0:T(8,128)(2,1)S(1)} %collective-permute-done.15.refs_17_.refs_1_.refs_9_, ...), custom_call_target="tpu_custom_call" | custom-call | tf_op jit(solution)/shard_map/partial_sums/pallas_call | solution.py:146
  115.0 1.6 collective-permute-start.25
  116.5 1.7 collective-permute-start.26
  118.2 8.7 %weight_terms.3 = bf16[2048,768]{1,0:T(8,128)(2,1)} custom-call(bf16[2048,128]{1,0:T(8,128)(2,1)S(1)} %get-tuple-element.44.refs_0_, bf16[2048,128]{1,0:T(8,128)(2,1)S(1)} %collective-permute-done.refs_1_, bf16[2048,128]{1,0:T(8,128)(2,1)S(1)} %collective-permute-done.1.refs_2_, bf16[2048,128]{1,0:T(8,128)(2,1)S(1)} %collective-permute-done.2.refs_3_, ...), custom_call_target="tpu_custom_call" | custom-call | tf_op jit(solution)/shard_map/weight_terms/pallas_call | solution.py:165
  127.1 6.4 %partial_sums.6 = (bf16[4,128,1024]{2,1,0:T(8,128)(2,1)}, bf16[4,128,1024]{2,1,0:T(8,128)(2,1)}) custom-call(bf16[4,128,768]{2,1,0:T(8,128)(2,1)S(1)} %pad_maximum_fusion.refs_16_.refs_0_.refs_8_, bf16[4,128,768]{2,1,0:T(8,128)(2,1)S(1)} %collective-permute-done.15.refs_17_.refs_1_.refs_9_, ...), custom_call_target="tpu_custom_call" | custom-call | tf_op jit(solution)/shard_map/partial_sums/pallas_call | solution.py:146
  133.5 3.8 %collective-permute-done.25.refs_20_ = bf16[4,128,1024]{2,1,0:T(8,128)(2,1)S(1)} collective-permute-done((bf16[4,128,1024]{2,1,0:T(8,128)(2,1)}, bf16[4,128,1024]{2,1,0:T(8,128)(2,1)S(1)}, u32[]{:S(2)}, u32[]{:S(2)}) %collective-permute-start.25) | collective-permute-done | bytes 1048608 | tf_op jit(solution)/shard_map/ppermute | solution.py:33
  137.3 1.0 copy-done.5
  138.3 1.6 collective-permute-start.27
  139.9 1.0 copy-done.7
  140.9 1.7 collective-permute-start.29
  142.6 1.3 collective-permute-start.24
  143.9 1.2 copy-done.6
  145.1 1.2 copy-done.8
  146.3 5.6 %partial_sums.5 = (bf16[4,128,1024]{2,1,0:T(8,128)(2,1)S(1)}, bf16[4,128,1024]{2,1,0:T(8,128)(2,1)S(1)}) custom-call(bf16[4,128,768]{2,1,0:T(8,128)(2,1)S(1)} %pad_maximum_fusion.refs_16_.refs_0_.refs_8_, bf16[4,128,768]{2,1,0:T(8,128)(2,1)S(1)} %collective-permute-done.15.refs_17_.refs_1_.refs_9_, ...), custom_call_target="tpu_custom_call" | custom-call | tf_op jit(solution)/shard_map/partial_sums/pallas_call | solution.py:146
  151.9 1.0 copy-done.10
  152.9 4.9 %collective-permute-done.27.refs_15_ = bf16[4,128,1024]{2,1,0:T(8,128)(2,1)S(1)} collective-permute-done((bf16[4,128,1024]{2,1,0:T(8,128)(2,1)}, bf16[4,128,1024]{2,1,0:T(8,128)(2,1)S(1)}, u32[]{:S(2)}, u32[]{:S(2)}) %collective-permute-start.27) | collective-permute-done | bytes 1048608 | tf_op jit(solution)/shard_map/ppermute | solution.py:33
  157.8 1.4 collective-permute-start.28
  159.2 1.8 collective-permute-start.30
  161.0 8.8 %weight_terms.2 = bf16[2048,768]{1,0:T(8,128)(2,1)} custom-call(bf16[2048,128]{1,0:T(8,128)(2,1)S(1)} %get-tuple-element.44.refs_0_, bf16[2048,128]{1,0:T(8,128)(2,1)S(1)} %collective-permute-done.refs_1_, bf16[2048,128]{1,0:T(8,128)(2,1)S(1)} %collective-permute-done.1.refs_2_, bf16[2048,128]{1,0:T(8,128)(2,1)S(1)} %collective-permute-done.2.refs_3_, ...), custom_call_target="tpu_custom_call" | custom-call | tf_op jit(solution)/shard_map/weight_terms/pallas_call | solution.py:165
  169.8 10.5 %collective-permute-done.28.refs_12_ = bf16[4,128,1024]{2,1,0:T(8,128)(2,1)S(1)} collective-permute-done((bf16[4,128,1024]{2,1,0:T(8,128)(2,1)S(1)}, bf16[4,128,1024]{2,1,0:T(8,128)(2,1)S(1)}, u32[]{:S(2)}, u32[]{:S(2)}) %collective-permute-start.28) | collective-permute-done | bytes 1048608 | tf_op jit(solution)/shard_map/ppermute | solution.py:33
  180.3 6.4 %partial_sums.7 = (bf16[2,128,1024]{2,1,0:T(8,128)(2,1)S(1)}, bf16[2,128,1024]{2,1,0:T(8,128)(2,1)S(1)}, bf16[2,128,1024]{2,1,0:T(8,128)(2,1)S(1)}, bf16[2,128,1024]{2,1,0:T(8,128)(2,1)S(1)}) custom-call(bf16[4,128,768]{2,1,0:T(8,128)(2,1)S(1)} %pad_maximum_fusion.refs_16_.refs_0_.refs_8_, ...), custom_call_target="tpu_custom_call" | custom-call | tf_op jit(solution)/shard_map/partial_sums/pallas_call | solution.py:146
  186.7 1.0 collective-permute-start.31
  187.7 5.0 %collective-permute-start.32 = (bf16[2,128,1024]{2,1,0:T(8,128)(2,1)S(1)}, bf16[2,128,1024]{2,1,0:T(8,128)(2,1)S(1)}, u32[]{:S(2)}, u32[]{:S(2)}) collective-permute-start(bf16[2,128,1024]{2,1,0:T(8,128)(2,1)S(1)} %get-tuple-element.83), channel_id=1, source_target_pairs={{16,0},{24,8},{0,16},{8,24},{17,1},{25,9},{1,17},{9,25},{18,2},{26... | collective-permute-start | bytes 1572872 | tf_op jit(solution)/shard_map/ppermute | solution.py:29
  192.7 1.3 collective-permute-start.33
  194.0 4.3 %fusion = bf16[1,2048,768]{2,1,0:T(8,128)(2,1)} fusion(bf16[2048,768]{1,0:T(8,128)(2,1)} %collective-permute-done.23, bf16[2048,768]{1,0:T(8,128)(2,1)S(1)} %copy-done.15), kind=kLoop, calls=%fused_computation.1 | loop fusion | flops 6291456 | bytes 9437184 | tf_op jit(solution)/shard_map/broadcast_in_dim | solution.py:292
  198.4 3.9 %collective-permute-done.31.refs_1_ = bf16[2,128,1024]{2,1,0:T(8,128)(2,1)S(1)} collective-permute-done((bf16[2,128,1024]{2,1,0:T(8,128)(2,1)S(1)}, bf16[2,128,1024]{2,1,0:T(8,128)(2,1)S(1)}, u32[]{:S(2)}, u32[]{:S(2)}) %collective-permute-start.31) | collective-permute-done | bytes 524320 | tf_op jit(solution)/shard_map/ppermute | solution.py:29
  202.3 3.3 %collective-permute-done.32.refs_2_ = bf16[2,128,1024]{2,1,0:T(8,128)(2,1)S(1)} collective-permute-done((bf16[2,128,1024]{2,1,0:T(8,128)(2,1)S(1)}, bf16[2,128,1024]{2,1,0:T(8,128)(2,1)S(1)}, u32[]{:S(2)}, u32[]{:S(2)}) %collective-permute-start.32) | collective-permute-done | bytes 524320 | tf_op jit(solution)/shard_map/ppermute | solution.py:29
  205.6 9.2 %collective-permute-done.33.refs_3_ = bf16[2,128,1024]{2,1,0:T(8,128)(2,1)S(1)} collective-permute-done((bf16[2,128,1024]{2,1,0:T(8,128)(2,1)S(1)}, bf16[2,128,1024]{2,1,0:T(8,128)(2,1)S(1)}, u32[]{:S(2)}, u32[]{:S(2)}) %collective-permute-start.33) | collective-permute-done | bytes 524320 | tf_op jit(solution)/shard_map/ppermute | solution.py:29
  214.8 5.2 %finish.1 = bf16[1,128,8192]{2,1,0:T(8,128)(2,1)} custom-call(s32[1]{0:T(128)} %bitcast.z_ref, f32[128,128]{1,0:T(8,128)S(1)} %get-tuple-element.66.r_ref, bf16[1,8192]{1,0:T(2,128)(2,1)S(1)} %copy-done.9, bf16[128,8192]{1,0:T(8,128)(2,1)S(1)} %bitcast.24, bf16[1,128,8192]{2,1,0:T(8,128)(2,1)} %collective-permute-done.24.u_ref, ...), custom_call_target="tpu_custom_call" | custom-call | tf_op jit(solution)/shard_map/finish/pallas_call | solution.py:207
  (57 shorter events, 1.3 us)
Async XLA Ops:
  0.6 6.8 %copy-start.1 = (bf16[1,128,8192]{2,1,0:T(8,128)(2,1)S(1)}, bf16[1,128,8192]{2,1,0:T(8,128)(2,1)}, u32[]{:S(2)}) copy-start(bf16[1,128,8192]{2,1,0:T(8,128)(2,1)} %param.5) | copy-start | bytes 6291460
  0.6 6.8 %copy-start.9 = (bf16[1,8192]{1,0:T(2,128)(2,1)S(1)}, bf16[1,8192]{1,0:T(2,128)(2,1)}, u32[]{:S(2)}) copy-start(bf16[1,8192]{1,0:T(2,128)(2,1)} %g_ref.3) | copy-start | bytes 49156
  4.3 20.9 %collective-permute-start.18 = (bf16[4,128,768]{2,1,0:T(8,128)(2,1)}, bf16[4,128,768]{2,1,0:T(8,128)(2,1)S(1)}, u32[]{:S(2)}, u32[]{:S(2)}) collective-permute-start(bf16[4,128,768]{2,1,0:T(8,128)(2,1)} %pad_maximum_fusion.1), channel_id=1, source_target_pairs={{0,4},{1,5},{2,6},{3,7},{4,0},{5,1},{6,2},{7,3},{8,12},{9,13},{10,... | collective-permute-start | bytes 2359304 | tf_op jit(solution)/shard_map/ppermute | solution.py:41
  9.5 0.8 copy-start.11
  10.3 0.8 copy-start.13
  11.0 24.4 %collective-permute-start = (bf16[2048,128]{1,0:T(8,128)(2,1)S(1)}, bf16[2048,128]{1,0:T(8,128)(2,1)S(1)}, u32[]{:S(2)}, u32[]{:S(2)}) collective-permute-start(bf16[2048,128]{1,0:T(8,128)(2,1)S(1)} %get-tuple-element.44.refs_0_), channel_id=1, source_target_pairs={{1,0},{2,1},{3,2},{0,3},{5,4},{6,5},{7,6},{4,7},{9,8},{10,9},{11,1... | collective-permute-start | bytes 1572872 | tf_op jit(solution)/shard_map/ppermute | solution.py:33
  14.1 16.3 %collective-permute-start.2 = (bf16[2048,128]{1,0:T(8,128)(2,1)S(1)}, bf16[2048,128]{1,0:T(8,128)(2,1)S(1)}, u32[]{:S(2)}, u32[]{:S(2)}) collective-permute-start(bf16[2048,128]{1,0:T(8,128)(2,1)S(1)} %get-tuple-element.44.refs_0_), channel_id=1, source_target_pairs={{3,0},{0,1},{1,2},{2,3},{7,4},{4,5},{5,6},{6,7},{11,8},{8,9},{9,10... | collective-permute-start | bytes 1572872 | tf_op jit(solution)/shard_map/ppermute | solution.py:33
  14.1 19.8 %collective-permute-start.3 = (bf16[2048,128]{1,0:T(8,128)(2,1)}, bf16[2048,128]{1,0:T(8,128)(2,1)S(1)}, u32[]{:S(2)}, u32[]{:S(2)}) collective-permute-start(bf16[2048,128]{1,0:T(8,128)(2,1)} %get-tuple-element.46), channel_id=1, source_target_pairs={{8,0},{16,8},{24,16},{0,24},{9,1},{17,9},{25,17},{1,25},{10,2},{18... | collective-permute-start | bytes 1572872 | tf_op jit(solution)/shard_map/ppermute | solution.py:29
  18.1 10.3 %copy-start.14 = (bf16[2048,128]{1,0:T(8,128)(2,1)S(1)}, bf16[2048,128]{1,0:T(8,128)(2,1)}, u32[]{:S(2)}) copy-start(bf16[2048,128]{1,0:T(8,128)(2,1)} %copy-done.13) | copy-start | bytes 1572868
  18.1 12.2 %copy-start.12 = (bf16[2048,128]{1,0:T(8,128)(2,1)S(1)}, bf16[2048,128]{1,0:T(8,128)(2,1)}, u32[]{:S(2)}) copy-start(bf16[2048,128]{1,0:T(8,128)(2,1)} %copy-done.11) | copy-start | bytes 1572868
  18.1 19.0 %copy-start.16 = (bf16[1,128,768]{2,1,0:T(8,128)(2,1)S(1)}, bf16[1,128,768]{2,1,0:T(8,128)(2,1)}, u32[]{:S(2)}) copy-start(bf16[1,128,768]{2,1,0:T(8,128)(2,1)} %get-tuple-element.86) | copy-start | bytes 589828
  18.1 19.0 %copy-start.17 = (bf16[1,128,768]{2,1,0:T(8,128)(2,1)S(1)}, bf16[1,128,768]{2,1,0:T(8,128)(2,1)}, u32[]{:S(2)}) copy-start(bf16[1,128,768]{2,1,0:T(8,128)(2,1)} %get-tuple-element.91) | copy-start | bytes 589828
  18.1 19.0 %copy-start.18 = (bf16[1,128,768]{2,1,0:T(8,128)(2,1)S(1)}, bf16[1,128,768]{2,1,0:T(8,128)(2,1)}, u32[]{:S(2)}) copy-start(bf16[1,128,768]{2,1,0:T(8,128)(2,1)} %get-tuple-element.92) | copy-start | bytes 589828
  18.1 19.0 %copy-start.19 = (bf16[1,128,768]{2,1,0:T(8,128)(2,1)S(1)}, bf16[1,128,768]{2,1,0:T(8,128)(2,1)}, u32[]{:S(2)}) copy-start(bf16[1,128,768]{2,1,0:T(8,128)(2,1)} %get-tuple-element.93) | copy-start | bytes 589828
  20.4 123.5 %copy-start = (bf16[2048,768]{1,0:T(8,128)(2,1)}, bf16[2048,768]{1,0:T(8,128)(2,1)S(1)}, u32[]{:S(2)}) copy-start(bf16[2048,768]{1,0:T(8,128)(2,1)S(1)} %dynamic-slice_bitcast_fusion.refs_8_.refs_10_.refs_16_.refs_18_) | copy-start | bytes 9437188
  25.1 83.6 %collective-permute-start.22 = (bf16[2048,768]{1,0:T(8,128)(2,1)S(1)}, bf16[2048,768]{1,0:T(8,128)(2,1)}, u32[]{:S(2)}, u32[]{:S(2)}) collective-permute-start(bf16[2048,768]{1,0:T(8,128)(2,1)S(1)} %dynamic-slice_bitcast_fusion.refs_8_.refs_10_.refs_16_.refs_18_), channel_id=1, source_target_pairs={{0,4},{1,5},{2,6},{3,7},{4,0},{5,1},{6,2},{7,3},{8,12},{9,13},{10,... | collective-permute-start | bytes 9437192 | tf_op jit(solution)/shard_map/ppermute | solution.py:41
  28.4 16.0 %collective-permute-start.11 = (bf16[2048,128]{1,0:T(8,128)(2,1)S(1)}, bf16[2048,128]{1,0:T(8,128)(2,1)S(1)}, u32[]{:S(2)}, u32[]{:S(2)}) collective-permute-start(bf16[2048,128]{1,0:T(8,128)(2,1)S(1)} %copy-done.14), channel_id=1, source_target_pairs={{24,0},{0,8},{8,16},{16,24},{25,1},{1,9},{9,17},{17,25},{26,2},{2,... | collective-permute-start | bytes 1572872 | tf_op jit(solution)/shard_map/ppermute | solution.py:29
  30.3 26.5 %collective-permute-start.7 = (bf16[2048,128]{1,0:T(8,128)(2,1)S(1)}, bf16[2048,128]{1,0:T(8,128)(2,1)S(1)}, u32[]{:S(2)}, u32[]{:S(2)}) collective-permute-start(bf16[2048,128]{1,0:T(8,128)(2,1)S(1)} %copy-done.12), channel_id=1, source_target_pairs={{16,0},{24,8},{0,16},{8,24},{17,1},{25,9},{1,17},{9,25},{18,2},{26... | collective-permute-start | bytes 1572872 | tf_op jit(solution)/shard_map/ppermute | solution.py:29
  33.9 22.9 %collective-permute-start.6 = (bf16[2048,128]{1,0:T(8,128)(2,1)S(1)}, bf16[2048,128]{1,0:T(8,128)(2,1)S(1)}, u32[]{:S(2)}, u32[]{:S(2)}) collective-permute-start(bf16[2048,128]{1,0:T(8,128)(2,1)S(1)} %collective-permute-done.3.refs_4_), channel_id=1, source_target_pairs={{3,0},{0,1},{1,2},{2,3},{7,4},{4,5},{5,6},{6,7},{11,8},{8,9},{9,10... | collective-permute-start | bytes 1572872 | tf_op jit(solution)/shard_map/ppermute | solution.py:33
  35.5 22.9 %collective-permute-start.1 = (bf16[2048,128]{1,0:T(8,128)(2,1)S(1)}, bf16[2048,128]{1,0:T(8,128)(2,1)S(1)}, u32[]{:S(2)}, u32[]{:S(2)}) collective-permute-start(bf16[2048,128]{1,0:T(8,128)(2,1)S(1)} %collective-permute-done.refs_1_), channel_id=1, source_target_pairs={{1,0},{2,1},{3,2},{0,3},{5,4},{6,5},{7,6},{4,7},{9,8},{10,9},{11,1... | collective-permute-start | bytes 1572872 | tf_op jit(solution)/shard_map/ppermute | solution.py:33
  44.4 22.8 %collective-permute-start.15 = (bf16[4,128,768]{2,1,0:T(8,128)(2,1)S(1)}, bf16[4,128,768]{2,1,0:T(8,128)(2,1)S(1)}, u32[]{:S(2)}, u32[]{:S(2)}) collective-permute-start(bf16[4,128,768]{2,1,0:T(8,128)(2,1)S(1)} %pad_maximum_fusion.refs_16_.refs_0_.refs_8_), channel_id=1, source_target_pairs={{8,0},{16,8},{24,16},{0,24},{9,1},{17,9},{25,17},{1,25},{10,2},{18... | collective-permute-start | bytes 2359304 | tf_op jit(solution)/shard_map/ppermute | solution.py:29
  56.8 17.3 %collective-permute-start.17 = (bf16[4,128,768]{2,1,0:T(8,128)(2,1)S(1)}, bf16[4,128,768]{2,1,0:T(8,128)(2,1)S(1)}, u32[]{:S(2)}, u32[]{:S(2)}) collective-permute-start(bf16[4,128,768]{2,1,0:T(8,128)(2,1)S(1)} %pad_maximum_fusion.refs_16_.refs_0_.refs_8_), channel_id=1, source_target_pairs={{24,0},{0,8},{8,16},{16,24},{25,1},{1,9},{9,17},{17,25},{26,2},{2,... | collective-permute-start | bytes 2359304 | tf_op jit(solution)/shard_map/ppermute | solution.py:29
  56.8 17.3 %collective-permute-start.9 = (bf16[2048,128]{1,0:T(8,128)(2,1)S(1)}, bf16[2048,128]{1,0:T(8,128)(2,1)S(1)}, u32[]{:S(2)}, u32[]{:S(2)}) collective-permute-start(bf16[2048,128]{1,0:T(8,128)(2,1)S(1)} %collective-permute-done.7.refs_8_), channel_id=1, source_target_pairs={{3,0},{0,1},{1,2},{2,3},{7,4},{4,5},{5,6},{6,7},{11,8},{8,9},{9,10... | collective-permute-start | bytes 1572872 | tf_op jit(solution)/shard_map/ppermute | solution.py:33
  58.4 17.3 %collective-permute-start.4 = (bf16[2048,128]{1,0:T(8,128)(2,1)S(1)}, bf16[2048,128]{1,0:T(8,128)(2,1)S(1)}, u32[]{:S(2)}, u32[]{:S(2)}) collective-permute-start(bf16[2048,128]{1,0:T(8,128)(2,1)S(1)} %collective-permute-done.3.refs_4_), channel_id=1, source_target_pairs={{1,0},{2,1},{3,2},{0,3},{5,4},{6,5},{7,6},{4,7},{9,8},{10,9},{11,1... | collective-permute-start | bytes 1572872 | tf_op jit(solution)/shard_map/ppermute | solution.py:33
  60.1 0.8 copy-start.3
  67.2 51.0 %copy-start.4 = (bf16[2048,128]{1,0:T(8,128)(2,1)S(1)}, bf16[2048,128]{1,0:T(8,128)(2,1)}, u32[]{:S(2)}) copy-start(bf16[2048,128]{1,0:T(8,128)(2,1)} %copy-done.3) | copy-start | bytes 1572868
  67.2 22.2 %collective-permute-start.16 = (bf16[4,128,768]{2,1,0:T(8,128)(2,1)S(1)}, bf16[4,128,768]{2,1,0:T(8,128)(2,1)S(1)}, u32[]{:S(2)}, u32[]{:S(2)}) collective-permute-start(bf16[4,128,768]{2,1,0:T(8,128)(2,1)S(1)} %collective-permute-done.15.refs_17_.refs_1_.refs_9_), channel_id=1, source_target_pairs={{8,0},{16,8},{24,16},{0,24},{9,1},{17,9},{25,17},{1,25},{10,2},{18... | collective-permute-start | bytes 2359304 | tf_op jit(solution)/shard_map/ppermute | solution.py:29
  74.1 12.1 %collective-permute-start.10 = (bf16[2048,128]{1,0:T(8,128)(2,1)S(1)}, bf16[2048,128]{1,0:T(8,128)(2,1)S(1)}, u32[]{:S(2)}, u32[]{:S(2)}) collective-permute-start(bf16[2048,128]{1,0:T(8,128)(2,1)S(1)} %collective-permute-done.9.refs_11_), channel_id=1, source_target_pairs={{3,0},{0,1},{1,2},{2,3},{7,4},{4,5},{5,6},{6,7},{11,8},{8,9},{9,10... | collective-permute-start | bytes 1572872 | tf_op jit(solution)/shard_map/ppermute | solution.py:33
  75.7 17.6 %collective-permute-start.20 = (bf16[4,128,768]{2,1,0:T(8,128)(2,1)S(1)}, bf16[4,128,768]{2,1,0:T(8,128)(2,1)S(1)}, u32[]{:S(2)}, u32[]{:S(2)}) collective-permute-start(bf16[4,128,768]{2,1,0:T(8,128)(2,1)S(1)} %collective-permute-done.18.refs_16_.refs_4_.refs_12_), channel_id=1, source_target_pairs={{24,0},{0,8},{8,16},{16,24},{25,1},{1,9},{9,17},{17,25},{26,2},{2,... | collective-permute-start | bytes 2359304 | tf_op jit(solution)/shard_map/ppermute | solution.py:29
  75.7 12.0 %collective-permute-start.5 = (bf16[2048,128]{1,0:T(8,128)(2,1)S(1)}, bf16[2048,128]{1,0:T(8,128)(2,1)S(1)}, u32[]{:S(2)}, u32[]{:S(2)}) collective-permute-start(bf16[2048,128]{1,0:T(8,128)(2,1)S(1)} %collective-permute-done.4.refs_5_), channel_id=1, source_target_pairs={{1,0},{2,1},{3,2},{0,3},{5,4},{6,5},{7,6},{4,7},{9,8},{10,9},{11,1... | collective-permute-start | bytes 1572872 | tf_op jit(solution)/shard_map/ppermute | solution.py:33
  86.2 12.2 %collective-permute-start.13 = (bf16[2048,128]{1,0:T(8,128)(2,1)S(1)}, bf16[2048,128]{1,0:T(8,128)(2,1)S(1)}, u32[]{:S(2)}, u32[]{:S(2)}) collective-permute-start(bf16[2048,128]{1,0:T(8,128)(2,1)S(1)} %collective-permute-done.11.refs_12_), channel_id=1, source_target_pairs={{3,0},{0,1},{1,2},{2,3},{7,4},{4,5},{5,6},{6,7},{11,8},{8,9},{9,10... | collective-permute-start | bytes 1572872 | tf_op jit(solution)/shard_map/ppermute | solution.py:33
  87.7 12.5 %collective-permute-start.8 = (bf16[2048,128]{1,0:T(8,128)(2,1)S(1)}, bf16[2048,128]{1,0:T(8,128)(2,1)S(1)}, u32[]{:S(2)}, u32[]{:S(2)}) collective-permute-start(bf16[2048,128]{1,0:T(8,128)(2,1)S(1)} %collective-permute-done.7.refs_8_), channel_id=1, source_target_pairs={{1,0},{2,1},{3,2},{0,3},{5,4},{6,5},{7,6},{4,7},{9,8},{10,9},{11,1... | collective-permute-start | bytes 1572872 | tf_op jit(solution)/shard_map/ppermute | solution.py:33
  89.4 13.4 %collective-permute-start.19 = (bf16[4,128,768]{2,1,0:T(8,128)(2,1)S(1)}, bf16[4,128,768]{2,1,0:T(8,128)(2,1)S(1)}, u32[]{:S(2)}, u32[]{:S(2)}) collective-permute-start(bf16[4,128,768]{2,1,0:T(8,128)(2,1)S(1)} %collective-permute-done.18.refs_16_.refs_4_.refs_12_), channel_id=1, source_target_pairs={{8,0},{16,8},{24,16},{0,24},{9,1},{17,9},{25,17},{1,25},{10,2},{18... | collective-permute-start | bytes 2359304 | tf_op jit(solution)/shard_map/ppermute | solution.py:29
  93.3 15.5 %collective-permute-start.21 = (bf16[4,128,768]{2,1,0:T(8,128)(2,1)S(1)}, bf16[4,128,768]{2,1,0:T(8,128)(2,1)S(1)}, u32[]{:S(2)}, u32[]{:S(2)}) collective-permute-start(bf16[4,128,768]{2,1,0:T(8,128)(2,1)S(1)} %collective-permute-done.20.refs_19_.refs_7_.refs_15_), channel_id=1, source_target_pairs={{24,0},{0,8},{8,16},{16,24},{25,1},{1,9},{9,17},{17,25},{26,2},{2,... | collective-permute-start | bytes 2359304 | tf_op jit(solution)/shard_map/ppermute | solution.py:29
  98.4 16.6 %collective-permute-start.14 = (bf16[2048,128]{1,0:T(8,128)(2,1)S(1)}, bf16[2048,128]{1,0:T(8,128)(2,1)S(1)}, u32[]{:S(2)}, u32[]{:S(2)}) collective-permute-start(bf16[2048,128]{1,0:T(8,128)(2,1)S(1)} %collective-permute-done.13.refs_15_), channel_id=1, source_target_pairs={{3,0},{0,1},{1,2},{2,3},{7,4},{4,5},{5,6},{6,7},{11,8},{8,9},{9,10... | collective-permute-start | bytes 1572872 | tf_op jit(solution)/shard_map/ppermute | solution.py:33
  100.2 16.4 %collective-permute-start.12 = (bf16[2048,128]{1,0:T(8,128)(2,1)S(1)}, bf16[2048,128]{1,0:T(8,128)(2,1)S(1)}, u32[]{:S(2)}, u32[]{:S(2)}) collective-permute-start(bf16[2048,128]{1,0:T(8,128)(2,1)S(1)} %collective-permute-done.11.refs_12_), channel_id=1, source_target_pairs={{1,0},{2,1},{3,2},{0,3},{5,4},{6,5},{7,6},{4,7},{9,8},{10,9},{11,1... | collective-permute-start | bytes 1572872 | tf_op jit(solution)/shard_map/ppermute | solution.py:33
  115.0 22.4 %collective-permute-start.25 = (bf16[4,128,1024]{2,1,0:T(8,128)(2,1)}, bf16[4,128,1024]{2,1,0:T(8,128)(2,1)S(1)}, u32[]{:S(2)}, u32[]{:S(2)}) collective-permute-start(bf16[4,128,1024]{2,1,0:T(8,128)(2,1)} %get-tuple-element.68), channel_id=1, source_target_pairs={{3,0},{0,1},{1,2},{2,3},{7,4},{4,5},{5,6},{6,7},{11,8},{8,9},{9,10... | collective-permute-start | bytes 3145736 | tf_op jit(solution)/shard_map/ppermute | solution.py:33
  116.5 23.3 %collective-permute-start.26 = (bf16[4,128,1024]{2,1,0:T(8,128)(2,1)S(1)}, bf16[4,128,1024]{2,1,0:T(8,128)(2,1)S(1)}, u32[]{:S(2)}, u32[]{:S(2)}) collective-permute-start(bf16[4,128,1024]{2,1,0:T(8,128)(2,1)S(1)} %get-tuple-element.70), channel_id=1, source_target_pairs={{1,0},{2,1},{3,2},{0,3},{5,4},{6,5},{7,6},{4,7},{9,8},{10,9},{11,1... | collective-permute-start | bytes 3145736 | tf_op jit(solution)/shard_map/ppermute | solution.py:33
  126.9 67.1 %collective-permute-start.23 = (bf16[2048,768]{1,0:T(8,128)(2,1)}, bf16[2048,768]{1,0:T(8,128)(2,1)}, u32[]{:S(2)}, u32[]{:S(2)}) collective-permute-start(bf16[2048,768]{1,0:T(8,128)(2,1)} %weight_terms.3), channel_id=1, source_target_pairs={{0,4},{1,5},{2,6},{3,7},{4,0},{5,1},{6,2},{7,3},{8,12},{9,13},{10,... | collective-permute-start | bytes 9437192 | tf_op jit(solution)/shard_map/ppermute | solution.py:41
  137.3 1.0 copy-start.5
  138.3 19.5 %collective-permute-start.27 = (bf16[4,128,1024]{2,1,0:T(8,128)(2,1)}, bf16[4,128,1024]{2,1,0:T(8,128)(2,1)S(1)}, u32[]{:S(2)}, u32[]{:S(2)}) collective-permute-start(bf16[4,128,1024]{2,1,0:T(8,128)(2,1)} %get-tuple-element.73), channel_id=1, source_target_pairs={{3,0},{0,1},{1,2},{2,3},{7,4},{4,5},{5,6},{6,7},{11,8},{8,9},{9,10... | collective-permute-start | bytes 3145736 | tf_op jit(solution)/shard_map/ppermute | solution.py:33
  139.9 1.0 copy-start.7
  140.9 18.3 %collective-permute-start.29 = (bf16[4,128,1024]{2,1,0:T(8,128)(2,1)}, bf16[4,128,1024]{2,1,0:T(8,128)(2,1)}, u32[]{:S(2)}, u32[]{:S(2)}) collective-permute-start(bf16[4,128,1024]{2,1,0:T(8,128)(2,1)} %get-tuple-element.76), channel_id=1, source_target_pairs={{1,0},{2,1},{3,2},{0,3},{5,4},{6,5},{7,6},{4,7},{9,8},{10,9},{11,1... | collective-permute-start | bytes 3145736 | tf_op jit(solution)/shard_map/ppermute | solution.py:33
  142.6 55.8 %collective-permute-start.24 = (bf16[1,128,8192]{2,1,0:T(8,128)(2,1)}, bf16[1,128,8192]{2,1,0:T(8,128)(2,1)}, u32[]{:S(2)}, u32[]{:S(2)}) collective-permute-start(bf16[1,128,8192]{2,1,0:T(8,128)(2,1)} %param.9), channel_id=1, source_target_pairs={{32,0},{64,32},{96,64},{33,1},{65,33},{97,65},{34,2},{66,34},{98,6... | collective-permute-start | bytes 6291464 | tf_op jit(solution)/shard_map/ppermute | solution.py:256
  143.9 1.2 copy-start.6
  145.1 1.2 copy-start.8
  151.9 1.0 copy-start.10
  157.8 22.5 %collective-permute-start.28 = (bf16[4,128,1024]{2,1,0:T(8,128)(2,1)S(1)}, bf16[4,128,1024]{2,1,0:T(8,128)(2,1)S(1)}, u32[]{:S(2)}, u32[]{:S(2)}) collective-permute-start(bf16[4,128,1024]{2,1,0:T(8,128)(2,1)S(1)} %get-tuple-element.74), channel_id=1, source_target_pairs={{3,0},{0,1},{1,2},{2,3},{7,4},{4,5},{5,6},{6,7},{11,8},{8,9},{9,10... | collective-permute-start | bytes 3145736 | tf_op jit(solution)/shard_map/ppermute | solution.py:33
  159.2 21.1 %collective-permute-start.30 = (bf16[4,128,1024]{2,1,0:T(8,128)(2,1)}, bf16[4,128,1024]{2,1,0:T(8,128)(2,1)S(1)}, u32[]{:S(2)}, u32[]{:S(2)}) collective-permute-start(bf16[4,128,1024]{2,1,0:T(8,128)(2,1)} %copy-done.10), channel_id=1, source_target_pairs={{1,0},{2,1},{3,2},{0,3},{5,4},{6,5},{7,6},{4,7},{9,8},{10,9},{11,1... | collective-permute-start | bytes 3145736 | tf_op jit(solution)/shard_map/ppermute | solution.py:33
  169.8 24.2 %copy-start.15 = (bf16[2048,768]{1,0:T(8,128)(2,1)S(1)}, bf16[2048,768]{1,0:T(8,128)(2,1)}, u32[]{:S(2)}) copy-start(bf16[2048,768]{1,0:T(8,128)(2,1)} %weight_terms.2) | copy-start | bytes 9437188
  186.7 15.6 %collective-permute-start.31 = (bf16[2,128,1024]{2,1,0:T(8,128)(2,1)S(1)}, bf16[2,128,1024]{2,1,0:T(8,128)(2,1)S(1)}, u32[]{:S(2)}, u32[]{:S(2)}) collective-permute-start(bf16[2,128,1024]{2,1,0:T(8,128)(2,1)S(1)} %get-tuple-element.81), channel_id=1, source_target_pairs={{8,0},{16,8},{24,16},{0,24},{9,1},{17,9},{25,17},{1,25},{10,2},{18... | collective-permute-start | bytes 1572872 | tf_op jit(solution)/shard_map/ppermute | solution.py:29
  187.7 17.9 %collective-permute-start.32 = (bf16[2,128,1024]{2,1,0:T(8,128)(2,1)S(1)}, bf16[2,128,1024]{2,1,0:T(8,128)(2,1)S(1)}, u32[]{:S(2)}, u32[]{:S(2)}) collective-permute-start(bf16[2,128,1024]{2,1,0:T(8,128)(2,1)S(1)} %get-tuple-element.83), channel_id=1, source_target_pairs={{16,0},{24,8},{0,16},{8,24},{17,1},{25,9},{1,17},{9,25},{18,2},{26... | collective-permute-start | bytes 1572872 | tf_op jit(solution)/shard_map/ppermute | solution.py:29
  192.7 22.1 %copy-start.2 = (bf16[1,128,8192]{2,1,0:T(8,128)(2,1)S(1)}, bf16[1,128,8192]{2,1,0:T(8,128)(2,1)}, u32[]{:S(2)}) copy-start(bf16[1,128,8192]{2,1,0:T(8,128)(2,1)} %param.5) | copy-start | bytes 6291460
  192.7 22.1 %collective-permute-start.33 = (bf16[2,128,1024]{2,1,0:T(8,128)(2,1)S(1)}, bf16[2,128,1024]{2,1,0:T(8,128)(2,1)S(1)}, u32[]{:S(2)}, u32[]{:S(2)}) collective-permute-start(bf16[2,128,1024]{2,1,0:T(8,128)(2,1)S(1)} %get-tuple-element.85), channel_id=1, source_target_pairs={{24,0},{0,8},{8,16},{16,24},{25,1},{1,9},{9,17},{17,25},{26,2},{2,... | collective-permute-start | bytes 1572872 | tf_op jit(solution)/shard_map/ppermute | solution.py:29

commit v3 on v2

v3 whole, which is shorter than its diff:
```python
import functools

import jax
import jax.numpy as jnp
from jax import lax
from jax.experimental import pallas as pl
from jax.experimental.pallas import tpu as pltpu
from jax.sharding import PartitionSpec as P

N_Z = 4
N_Y = 4
F32 = jnp.float32
BF16 = jnp.bfloat16
VMEM_BYTES = 20 * 2**20


class Chains:
    def __init__(self):
        self.last = {}

    def __call__(self, key, block, send):
        block = self.after(block, key)
        self.last[key] = send(block)
        return self.last[key]

    def after(self, block, *keys):
        for key in keys:
            if key in self.last:
                block, _ = lax.optimization_barrier((block, self.last[key]))
        return block


def from_z(block, o):
    return lax.ppermute(block, "dp", [((i + o) % N_Z, i) for i in range(N_Z)])


def from_y(block, o):
    return lax.ppermute(
        block,
        "tensor",
        [(x * N_Y + (i + o) % N_Y, x * N_Y + i) for x in range(2) for i in range(N_Y)],
    )


def from_x(block):
    return lax.ppermute(block, "tensor", [(i, (i + N_Y) % (2 * N_Y)) for i in range(2 * N_Y)])


def dot_nt(a, b):
    return lax.dot_general(a, b, (((1,), (1,)), ((), ())), preferred_element_type=F32)


def dot_nn(a, b):
    return lax.dot_general(a, b, (((1,), (0,)), ((), ())), preferred_element_type=F32)


def call(kernel, grid, in_specs, out_specs, out_shape, flops=0, bytes_accessed=0, name=None):
    return pl.pallas_call(
        kernel,
        grid_spec=pltpu.PrefetchScalarGridSpec(
            num_scalar_prefetch=1, grid=grid, in_specs=in_specs, out_specs=out_specs
        ),
        out_shape=out_shape,
        name=name,
        compiler_params=pltpu.CompilerParams(vmem_limit_bytes=VMEM_BYTES),
        cost_estimate=pl.CostEstimate(
            flops=flops, bytes_accessed=bytes_accessed, transcendentals=0
        ),
    )


WHOLE = pl.BlockSpec(memory_space=pltpu.VMEM)


def normalize(place, hidden, gain):
    rows, width = hidden.shape
    part = width // N_Z

    def kernel(at_ref, h_ref, g_ref, r_ref, *out_refs):
        x = h_ref[...].astype(F32)
        r = lax.rsqrt(jnp.mean(x * x, axis=-1, keepdims=True) + 1e-06)
        r_ref[...] = jnp.broadcast_to(r, r_ref.shape)
        for d in range(N_Z):
            at = pl.multiple_of(lax.rem(at_ref[0] + d, N_Z) * part, part)
            x = h_ref[:, pl.ds(at, part)].astype(F32)
            g = g_ref[:, pl.ds(at, part)].astype(F32)
            out_refs[d][...] = ((x * r) * g).T.astype(BF16)

    return call(
        kernel,
        (),
        [WHOLE, WHOLE],
        [WHOLE] * (1 + N_Z),
        [jax.ShapeDtypeStruct((rows, 128), F32)]
        + [jax.ShapeDtypeStruct((part, rows), BF16)] * N_Z,
        bytes_accessed=4 * rows * width,
        name="normalize",
    )(place, hidden, gain)


def partial_sums(place, seqs, jobs, g_own, g_par, w_own, w_par, extras=(), per_sequence=False):
    _, rows, cols = g_own[0].shape
    part = w_own.shape[0]
    half = part // 2
    step = 256
    steps = half // step
    count = len(seqs)
    qs = sorted({q for q, _, _ in jobs})
    sides = sorted({side for _, side, _ in jobs})
    n_g, n_w, n_e = 2 * count * len(qs), 2 * len(sides), len(extras)

    def kernel(at_ref, *refs):
        g_refs, w_refs = refs[:n_g], refs[n_g : n_g + n_w]
        e_refs, outs = refs[n_g + n_w : n_g + n_w + n_e], refs[n_g + n_w + n_e :]
        for k, (q, side, adds) in enumerate(jobs):
            at = qs.index(q) * 2 * count
            left = jnp.concatenate([g_refs[at + o][0] for o in range(count)], 0)
            right = jnp.concatenate([g_refs[at + count + o][0] for o in range(count)], 0)
            s = sides.index(side) * 2
            total = dot_nt(left, w_refs[s][...]) + dot_nt(right, w_refs[s + 1][...])
            total = total.reshape(count, rows, step)
            for e in adds:
                total = total + e_refs[e][...].astype(F32)
            if per_sequence:
                for o in range(count):
                    outs[o][side] = total[o].astype(BF16)
            else:
                outs[k][...] = total.astype(BF16)

    def tokens_of(q):
        return pl.BlockSpec((1, rows, cols), lambda i, at: (lax.rem(at[1] + q, N_Y), 0, 0))

    def features_of(side):
        return pl.BlockSpec((step, cols), lambda i, at: (side * steps + i, 0))

    in_specs, operands = [], []
    for q in qs:
        for arrays in (g_own, g_par):
            for o in seqs:
                in_specs.append(tokens_of(q))
                operands.append(arrays[o])
    for side in sides:
        for w in (w_own, w_par):
            in_specs.append(features_of(side))
            operands.append(w)
    chunk = pl.BlockSpec((count, rows, step), lambda i, at: (0, 0, i))
    in_specs += [chunk] * n_e
    operands += list(extras)
    if per_sequence:
        out_specs = [pl.BlockSpec((2, rows, step), lambda i, at: (0, 0, i))] * count
        out_shape = [jax.ShapeDtypeStruct((2, rows, half), BF16)] * count
    else:
        out_specs = [chunk] * len(jobs)
        out_shape = [jax.ShapeDtypeStruct((count, rows, half), BF16)] * len(jobs)
    return call(
        kernel, (steps,), in_specs, out_specs, out_shape, name="partial_sums"
    )(place, *operands)


def weight_terms(place, n_pieces, g):
    part, rows = n_pieces[0][0].shape
    cols = g[0].shape[2]
    step = 256

    def kernel(at_ref, *refs):
        n_refs, g_refs, out_ref = refs[: N_Z * N_Y], refs[N_Z * N_Y : -1], refs[-1]
        total = None
        for o in range(N_Z):
            left = jnp.concatenate([n_refs[o * N_Y + q][...] for q in range(N_Y)], 1)
            right = jnp.concatenate(
                [g_refs[o][lax.rem(at_ref[1] + q, N_Y)] for q in range(N_Y)], 0
            )
            term = dot_nn(left, right)
            total = term if total is None else total + term
        out_ref[...] = total.astype(BF16)

    return call(
        kernel,
        (part // step,),
        [pl.BlockSpec((step, rows), lambda i, at: (i, 0))] * (N_Z * N_Y)
        + [pl.BlockSpec((N_Y, rows, cols), lambda i, at: (0, 0, 0))] * N_Z,
        pl.BlockSpec((step, cols), lambda i, at: (i, 0)),
        jax.ShapeDtypeStruct((part, cols), BF16),
        name="weight_terms",
    )(place, *[n_pieces[o][q] for o in range(N_Z) for q in range(N_Y)], *g)


def finish(place, deviation, gain, hidden, received, h):
    rows, width = hidden.shape
    part = width // N_Z
    half = part // 2
    step = 32

    def kernel(at_ref, r_ref, g_ref, x_ref, u_ref, *refs):
        h_refs, out_ref = refs[:-1], refs[-1]
        r = r_ref[:, :1]
        spots = [
            (o, s, pl.multiple_of(lax.rem(at_ref[0] + o, N_Z) * part + s * half, half))
            for o in range(N_Z)
            for s in range(2)
        ]

        def terms(o, s, at):
            xhat = x_ref[:, pl.ds(at, half)].astype(F32) * r
            scaled = g_ref[:, pl.ds(at, half)].astype(F32) * h_refs[o][s].astype(F32)
            return xhat, scaled

        total = jnp.zeros((step, 1), F32)
        for spot in spots:
            xhat, scaled = terms(*spot)
            total += jnp.sum(scaled * xhat, axis=-1, keepdims=True)
        mean = total / width
        for spot in spots:
            xhat, scaled = terms(*spot)
            at = spot[2]
            up = u_ref[0, :, pl.ds(at, half)].astype(F32)
            out_ref[0, :, pl.ds(at, half)] = (up + r * (scaled - xhat * mean)).astype(BF16)

    return call(
        kernel,
        (rows // step,),
        [
            pl.BlockSpec((step, 128), lambda i, at: (i, 0)),
            pl.BlockSpec((1, width), lambda i, at: (0, 0)),
            pl.BlockSpec((step, width), lambda i, at: (i, 0)),
            pl.BlockSpec((1, step, width), lambda i, at: (0, i, 0)),
        ]
        + [pl.BlockSpec((2, step, half), lambda i, at: (0, i, 0))] * N_Z,
        pl.BlockSpec((1, step, width), lambda i, at: (0, i, 0)),
        jax.ShapeDtypeStruct((1, rows, width), BF16),
        name="finish",
    )(place, deviation, gain, hidden, received, *h)


def shards(hidden_in, norm_gain, qkv_weight, qkv_grad, upper_grad):
    tensor = lax.axis_index("tensor")
    xh, y, z = tensor // N_Y, tensor % N_Y, lax.axis_index("dp")
    place = jnp.stack([z, y]).astype(jnp.int32)
    rows = hidden_in.shape[1]
    part = hidden_in.shape[2] // N_Z
    cols = qkv_grad.shape[2]
    layers = lax.axis_size("pipe")
    chains = Chains()

    def zz(block, o):
        return chains("z%d" % o, block, lambda b: from_z(b, o))

    def yy(block, o):
        return chains("y%d" % o, block, lambda b: from_y(b, o))

    def xx(block):
        return chains("x", block, from_x)

    grads = qkv_grad[0].reshape(2, N_Y, rows, cols)
    par0 = xx(lax.dynamic_index_in_dim(grads, 1 - xh, 0, keepdims=False))
    own0 = lax.dynamic_index_in_dim(grads, xh, 0, keepdims=False)
    w_own = lax.dynamic_slice_in_dim(qkv_weight[0], z * part, part, 0)
    w_par = xx(w_own)
    received = lax.ppermute(upper_grad, "pipe", [(i + 1, i) for i in range(layers - 1)])

    deviation, *n_to = normalize(place, hidden_in[0], norm_gain)
    n1, n3 = zz(n_to[3], 1), zz(n_to[1], 3)
    chains.last["z2"] = n2 = from_z(chains.after(n_to[2], "z1", "z3"), 2)
    n_near = [n_to[0], n1, n2, n3]
    order = (0, 1, 3, 2)
    n_up, n_down = {}, {}
    for o in order:
        n_up[o], n_down[o] = yy(n_near[o], 1), yy(n_near[o], 3)
    n_across = {}
    for one, other in ((0, 1), (3, 2)):
        n_across[one], n_across[other] = yy(n_up[one], 1), yy(n_down[other], 3)
    n_pieces = [[n_near[o], n_up[o], n_across[o], n_down[o]] for o in range(N_Z)]

    own0_sent = chains.after(own0, "z2")
    own1, own3 = zz(own0_sent, 1), zz(own0_sent, 3)
    par1, par3 = zz(par0, 1), zz(par0, 3)
    own2, par2 = zz(own1, 1), zz(par3, 3)
    g_own, g_par = [own0, own1, own2, own3], [par0, par1, par2, par3]

    def summed(seqs):
        sums = functools.partial(
            partial_sums, place, seqs, g_own=g_own, g_par=g_par, w_own=w_own, w_par=w_par
        )
        p2a, p2b = sums([(2, 0, ()), (2, 1, ())])
        p2a, p2b = chains.after(p2a, "h"), chains.after(p2b, "h")
        hop_up, hop_down = yy(p2a, 3), yy(p2b, 1)
        p1b, p3a = sums([(1, 1, ()), (3, 0, ())])
        up_b, down_a = yy(p1b, 3), yy(p3a, 1)
        hop_up, hop_down = chains.after(hop_up, "h2"), chains.after(hop_down, "h2")
        p1a, p3b = sums([(1, 0, (0,)), (3, 1, (1,))], extras=[hop_up, hop_down])
        up_a, down_b = yy(p1a, 3), yy(p3b, 1)
        up_a = chains.after(up_a, "dw", "h1", "h3")
        return sums(
            [(0, 0, (0, 1)), (0, 1, (2, 3))],
            extras=[up_a, down_a, down_b, up_b],
            per_sequence=True,
        )

    dw_got = xx(weight_terms(place, n_pieces, g_par))
    chains.last["dw"] = dw_own = weight_terms(place, n_pieces, g_own)
    h_to1, h_to2, h_to3 = summed([1, 2, 3])
    h2 = chains.last["h2"] = from_z(h_to2, 2)
    h1, h3 = from_z(chains.after(h_to3, "h2"), 1), from_z(chains.after(h_to1, "h2"), 3)
    chains.last.update(h=h_to2, h1=h1, h3=h3)
    (h0,) = summed([0])

    dw_got = chains.after(dw_got, "h1", "h3")
    weight_out = (dw_own.astype(F32) + dw_got.astype(F32)).astype(BF16)

    input_out = finish(place, deviation, norm_gain, hidden_in[0], received, [h0, h1, h2, h3])
    return (weight_out[None], input_out)


def solution(mesh):
    placed = (
        P("pipe", ("dp", "tensor"), None),
        P("pipe", None),
        P("pipe", None, "tensor"),
        P("pipe", "dp", "tensor"),
        P("pipe", ("dp", "tensor"), None),
    )
    return jax.shard_map(
        shards,
        mesh=mesh,
        in_specs=placed,
        out_specs=(P("pipe", "dp", "tensor"), P("pipe", ("dp", "tensor"), None)),
        check_vma=False,
    )
```

time: 223 us -> 213 us (0.955); the launches traced: 220 us -> 212 us
  starting transfers between devices: 64.3 us -> 54.9 us
  Pallas kernels: 49.3 us -> 56.4 us
  local copies, waits for them, and re-layouts: 12.6 us -> 6.94 us
  waiting for transfers between devices: 87.4 us -> 90.5 us
  other arithmetic: 5.42 us -> 2.65 us
    ppermute x18 -> x24, waiting for transfers between devices: 33.2 us -> 59.4 us  [from_y(): lax.ppermute(block, 'tensor', [(x * N_Y + (i + o) % N_Y, x * N_Y + i) for...]
    ppermute x12, waiting for transfers between devices: 49.4 us -> 28 us  [from_z(): return lax.ppermute(block, 'dp', [((i + o) % N_Z, i) for i in range(N_Z)])]
    ppermute x12, starting transfers between devices: 27.5 us -> 17.9 us  [from_z(): return lax.ppermute(block, 'dp', [((i + o) % N_Z, i) for i in range(N_Z)])]
    unnamed x40 -> x12, local copies, waits for them, and re-layouts: 7.83 us -> 2.42 us
    pallas_call x4 -> x8, Pallas kernels: 24.5 us -> 29.9 us  [partial_sums(): call(kernel, (steps,), in_specs, out_specs, out_shape, name='partial_sums')]
    dynamic_slice x1 -> x0, local copies, waits for them, and re-layouts: 2.54 us -> none  [turned(): lax.dynamic_slice_in_dim(side, (y + q) % N_Y, 1, 0)]
    squeeze x0 -> x1, local copies, waits for them, and re-layouts: none -> 2.36 us  [shards(): own0 = lax.dynamic_index_in_dim(grads, xh, 0, keepdims=False)]
    ppermute x18 -> x24, starting transfers between devices: 29.1 us -> 28.8 us  [from_y(): lax.ppermute(block, 'tensor', [(x * N_Y + (i + o) % N_Y, x * N_Y + i) for...]
  transfers between devices with their start and end apart: 34 -> 40, of which waited for: 17 -> 19; matrix products, arithmetic and copies ran while one was open for 3% -> 2% of each run, Pallas kernels for 20% -> 25%
where the time goes in v3:
time: 213 us; the launch traced here: 212 us
  waiting for transfers between devices  90.5 us (42%)
  Pallas kernels  56.4 us (26%)
  starting transfers between devices  54.9 us (26%)
  local copies, waits for them, and re-layouts  6.94 us (3%)
  other arithmetic  2.65 us (1%)
    ppermute x24, waiting for transfers between devices, from_y(): lax.ppermute(block, 'tensor', [(x * N_Y + (i + o) % N_Y, x * N_Y + i) for...  59.4 us
    pallas_call x8, Pallas kernels, partial_sums(): call(kernel, (steps,), in_specs, out_specs, out_shape, name='partial_sums')  29.9 us
    ppermute x24, starting transfers between devices, from_y(): lax.ppermute(block, 'tensor', [(x * N_Y + (i + o) % N_Y, x * N_Y + i) for...  28.8 us
    ppermute x12, waiting for transfers between devices, from_z(): return lax.ppermute(block, 'dp', [((i + o) % N_Z, i) for i in range(N_Z)])  28 us
    pallas_call x2, Pallas kernels, weight_terms(): call(kernel, (part // step,), [pl.BlockSpec((step, rows), lambda i, at: (...  19.4 us
    ppermute x12, starting transfers between devices, from_z(): return lax.ppermute(block, 'dp', [((i + o) % N_Z, i) for i in range(N_Z)])  17.9 us
    ppermute x3, starting transfers between devices, from_x(): lax.ppermute(block, 'tensor', [(i, (i + N_Y) % (2 * N_Y)) for i in range(...  6.94 us
    pallas_call x1, Pallas kernels, finish(): call(kernel, (rows // step,), [pl.BlockSpec((step, 128), lambda i, at: (i...  4.36 us
  transfers between devices with their start and end apart: 40, of which 19 were waited for; matrix products, arithmetic and copies ran while one was open for 2% of the time, Pallas kernels for 25%

profile of v3, /device:TPU:0, one launch (start us, length us, event | category | flops | bytes accessed | tf_op | source)
XLA Modules:
  0.0 212.2 jit_solution(3490319877229548202)
XLA Ops:
  0.7 2.4 %dynamic-slice_bitcast_fusion.2 = (bf16[4,128,768]{2,1,0:T(8,128)(2,1)S(1)}, bf16[4,128,768]{2,1,0:T(8,128)(2,1)}) fusion(bf16[2,4,128,768]{3,2,1,0:T(8,128)(2,1)} %bitcast.14, s32[]{:T(128)S(6)} %select_n.23, s32[]{:T(128)S(6)} %select_n.24), kind=kLoop, calls=%fused_computation.4 | loop fusion | bytes 3145736 | tf_op jit(solution)/shard_map/jit(dynamic_index_in_dim)/squeeze | solution.py:256
  3.0 3.1 %collective-permute-start.16 = (bf16[4,128,768]{2,1,0:T(8,128)(2,1)}, bf16[4,128,768]{2,1,0:T(8,128)(2,1)S(1)}, u32[]{:S(2)}, u32[]{:S(2)}) collective-permute-start(bf16[4,128,768]{2,1,0:T(8,128)(2,1)} %get-tuple-element.133), channel_id=1, source_target_pairs={{0,4},{1,5},{2,6},{3,7},{4,0},{5,1},{6,2},{7,3},{8,12},{9,13},{10,... | collective-permute-start | bytes 2359304 | tf_op jit(solution)/shard_map/ppermute | solution.py:46
  6.2 1.6 copy-done
  7.8 2.7 %normalize.1 = (f32[128,128]{1,0:T(8,128)S(1)}, bf16[2048,128]{1,0:T(8,128)(2,1)S(1)}, bf16[2048,128]{1,0:T(8,128)(2,1)}, bf16[2048,128]{1,0:T(8,128)(2,1)S(1)}, bf16[2048,128]{1,0:T(8,128)(2,1)}) custom-call(s32[2]{0:T(128)S(1)} %pad_add_fusion.at_ref, bf16[128,8192]{1,0:T(8,128)(2,1)S(1)} %bitcast.12, bf16[1,8192]{1,0:T(2,128)(2,1)S(1)} %copy-done.2), custom_call_target="tpu_custom_call" | custom-call | bytes 4194304 | tf_op jit(solution)/shard_map/normalize/pallas_call | solution.py:89
  10.5 0.8 copy-done.3
  11.3 1.6 collective-permute-start.8
  12.9 1.7 collective-permute-start
  14.6 4.0 %collective-permute-start.1 = (bf16[2048,128]{1,0:T(8,128)(2,1)}, bf16[2048,128]{1,0:T(8,128)(2,1)}, u32[]{:S(2)}, u32[]{:S(2)}) collective-permute-start(bf16[2048,128]{1,0:T(8,128)(2,1)} %get-tuple-element.69), channel_id=1, source_target_pairs={{8,0},{16,8},{24,16},{0,24},{9,1},{17,9},{25,17},{1,25},{10,2},{18... | collective-permute-start | bytes 1572872 | tf_op jit(solution)/shard_map/ppermute | solution.py:34
  18.6 2.2 %dynamic-slice_bitcast_fusion.refs_6_.refs_8_.refs_12_.refs_14_.refs_2_.refs_4_ = bf16[2048,768]{1,0:T(8,128)(2,1)S(1)} fusion(bf16[1,8192,768]{2,1,0:T(8,128)(2,1)} %param.7, s32[]{:T(128)S(6)} %select_n.25), kind=kLoop, calls=%fused_computation.2 | loop fusion | bytes 6291460 | tf_op jit(solution)/shard_map/dynamic_slice | solution.py:257
  20.8 3.1 %collective-permute-done.16.refs_16_.refs_1_.refs_3_ = bf16[4,128,768]{2,1,0:T(8,128)(2,1)S(1)} collective-permute-done((bf16[4,128,768]{2,1,0:T(8,128)(2,1)}, bf16[4,128,768]{2,1,0:T(8,128)(2,1)S(1)}, u32[]{:S(2)}, u32[]{:S(2)}) %collective-permute-start.16) | collective-permute-done | bytes 786464 | tf_op jit(solution)/shard_map/ppermute | solution.py:46
  23.9 3.2 %collective-permute-start.22 = (bf16[2048,768]{1,0:T(8,128)(2,1)S(1)}, bf16[2048,768]{1,0:T(8,128)(2,1)S(1)}, u32[]{:S(2)}, u32[]{:S(2)}) collective-permute-start(bf16[2048,768]{1,0:T(8,128)(2,1)S(1)} %dynamic-slice_bitcast_fusion.refs_6_.refs_8_.refs_12_.refs_14_.refs_2_.refs_4_), channel_id=1, source_target_pairs={{0,4},{1,5},{2,6},{3,7},{4,0},{5,1},{6,2},{7,3},{8,12},{9,13},{10,... | collective-permute-start | bytes 9437192 | tf_op jit(solution)/shard_map/ppermute | solution.py:46
  27.1 2.2 %collective-permute-done.1.refs_4_ = bf16[2048,128]{1,0:T(8,128)(2,1)} collective-permute-done((bf16[2048,128]{1,0:T(8,128)(2,1)}, bf16[2048,128]{1,0:T(8,128)(2,1)}, u32[]{:S(2)}, u32[]{:S(2)}) %collective-permute-start.1) | collective-permute-done | bytes 524320 | tf_op jit(solution)/shard_map/ppermute | solution.py:34
  29.3 3.4 %collective-permute-done.2.refs_12_ = bf16[2048,128]{1,0:T(8,128)(2,1)} collective-permute-done((bf16[2048,128]{1,0:T(8,128)(2,1)}, bf16[2048,128]{1,0:T(8,128)(2,1)}, u32[]{:S(2)}, u32[]{:S(2)}) %collective-permute-start.2) | collective-permute-done | bytes 524320 | tf_op jit(solution)/shard_map/ppermute | solution.py:34
  32.8 0.4 collective-permute-start.9
  33.1 2.9 %collective-permute-start.4 = (bf16[2048,128]{1,0:T(8,128)(2,1)}, bf16[2048,128]{1,0:T(8,128)(2,1)S(1)}, u32[]{:S(2)}, u32[]{:S(2)}) collective-permute-start(bf16[2048,128]{1,0:T(8,128)(2,1)} %collective-permute-done.1.refs_4_), channel_id=1, source_target_pairs={{1,0},{2,1},{3,2},{0,3},{5,4},{6,5},{7,6},{4,7},{9,8},{10,9},{11,1... | collective-permute-start | bytes 1572872 | tf_op jit(solution)/shard_map/ppermute | solution.py:38
  36.1 10.0 %collective-permute-done.3.refs_8_ = bf16[2048,128]{1,0:T(8,128)(2,1)S(1)} collective-permute-done((bf16[2048,128]{1,0:T(8,128)(2,1)S(1)}, bf16[2048,128]{1,0:T(8,128)(2,1)S(1)}, u32[]{:S(2)}, u32[]{:S(2)}) %collective-permute-start.3) | collective-permute-done | bytes 524320 | tf_op jit(solution)/shard_map/ppermute | solution.py:34
  46.1 0.4 collective-permute-start.15
  46.5 1.6 collective-permute-start.19
  48.2 3.1 %collective-permute-start.5 = (bf16[2048,128]{1,0:T(8,128)(2,1)}, bf16[2048,128]{1,0:T(8,128)(2,1)S(1)}, u32[]{:S(2)}, u32[]{:S(2)}) collective-permute-start(bf16[2048,128]{1,0:T(8,128)(2,1)} %collective-permute-done.2.refs_12_), channel_id=1, source_target_pairs={{1,0},{2,1},{3,2},{0,3},{5,4},{6,5},{7,6},{4,7},{9,8},{10,9},{11,1... | collective-permute-start | bytes 1572872 | tf_op jit(solution)/shard_map/ppermute | solution.py:38
  51.3 9.1 %collective-permute-done.10.refs_15_ = bf16[2048,128]{1,0:T(8,128)(2,1)S(1)} collective-permute-done((bf16[2048,128]{1,0:T(8,128)(2,1)}, bf16[2048,128]{1,0:T(8,128)(2,1)S(1)}, u32[]{:S(2)}, u32[]{:S(2)}) %collective-permute-start.10) | collective-permute-done | bytes 524320 | tf_op jit(solution)/shard_map/ppermute | solution.py:38
  60.4 3.4 %collective-permute-done.15.refs_17_.refs_0_.refs_6_ = bf16[4,128,768]{2,1,0:T(8,128)(2,1)S(1)} collective-permute-done((bf16[4,128,768]{2,1,0:T(8,128)(2,1)S(1)}, bf16[4,128,768]{2,1,0:T(8,128)(2,1)S(1)}, u32[]{:S(2)}, u32[]{:S(2)}) %collective-permute-start.15) | collective-permute-done | bytes 786464 | tf_op jit(solution)/shard_map/ppermute | solution.py:34
  63.8 0.6 collective-permute-start.17
  64.4 1.4 collective-permute-start.20
  65.8 1.6 collective-permute-start.6
  67.4 5.1 %collective-permute-done.11.refs_11_ = bf16[2048,128]{1,0:T(8,128)(2,1)S(1)} collective-permute-done((bf16[2048,128]{1,0:T(8,128)(2,1)S(1)}, bf16[2048,128]{1,0:T(8,128)(2,1)S(1)}, u32[]{:S(2)}, u32[]{:S(2)}) %collective-permute-start.11) | collective-permute-done | bytes 524320 | tf_op jit(solution)/shard_map/ppermute | solution.py:38
  72.5 6.1 %collective-permute-done.6.refs_9_ = bf16[2048,128]{1,0:T(8,128)(2,1)S(1)} collective-permute-done((bf16[2048,128]{1,0:T(8,128)(2,1)S(1)}, bf16[2048,128]{1,0:T(8,128)(2,1)S(1)}, u32[]{:S(2)}, u32[]{:S(2)}) %collective-permute-start.6) | collective-permute-done | bytes 524320 | tf_op jit(solution)/shard_map/ppermute | solution.py:38
  78.5 0.9 collective-permute-start.7
  79.4 2.0 collective-permute-done.17.refs_17_.refs_3_.refs_9_
  81.5 0.6 collective-permute-start.18
  82.1 1.4 collective-permute-start.21
  83.5 1.7 collective-permute-done.12.refs_6_
  85.3 6.8 %collective-permute-done.7.refs_2_ = bf16[2048,128]{1,0:T(8,128)(2,1)S(1)} collective-permute-done((bf16[2048,128]{1,0:T(8,128)(2,1)S(1)}, bf16[2048,128]{1,0:T(8,128)(2,1)S(1)}, u32[]{:S(2)}, u32[]{:S(2)}) %collective-permute-start.7) | collective-permute-done | bytes 524320 | tf_op jit(solution)/shard_map/ppermute | solution.py:38
  92.1 0.2 collective-permute-start.14
  92.3 3.7 %collective-permute-done.18.refs_18_.refs_1_.refs_7_ = bf16[4,128,768]{2,1,0:T(8,128)(2,1)S(1)} collective-permute-done((bf16[4,128,768]{2,1,0:T(8,128)(2,1)S(1)}, bf16[4,128,768]{2,1,0:T(8,128)(2,1)S(1)}, u32[]{:S(2)}, u32[]{:S(2)}) %collective-permute-start.18) | collective-permute-done | bytes 786464 | tf_op jit(solution)/shard_map/ppermute | solution.py:34
  96.0 1.9 collective-permute-done.21.refs_18_.refs_4_.refs_10_
  97.9 4.0 %partial_sums.8 = (bf16[3,128,1024]{2,1,0:T(8,128)(2,1)S(1)}, bf16[3,128,1024]{2,1,0:T(8,128)(2,1)S(1)}) custom-call(s32[2]{0:T(128)S(1)} %pad_add_fusion.at_ref, bf16[4,128,768]{2,1,0:T(8,128)(2,1)S(1)} %collective-permute-done.15.refs_17_.refs_0_.refs_6_, bf16[4,128,768]{2,1,0:T(8,128)(2,1)S(1)} %collective-permute-done.18.refs_18_.refs_1_.refs_7_, ...), custom_call_target="tpu_custom_call" | custom-call | tf_op jit(solution)/shard_map/partial_sums/pallas_call | solution.py:155
  101.9 0.8 collective-permute-start.24
  102.7 2.5 %collective-permute-start.25 = (bf16[3,128,1024]{2,1,0:T(8,128)(2,1)S(1)}, bf16[3,128,1024]{2,1,0:T(8,128)(2,1)S(1)}, u32[]{:S(2)}, u32[]{:S(2)}) collective-permute-start(bf16[3,128,1024]{2,1,0:T(8,128)(2,1)S(1)} %get-tuple-element.95), channel_id=1, source_target_pairs={{1,0},{2,1},{3,2},{0,3},{5,4},{6,5},{7,6},{4,7},{9,8},{10,9},{11,1... | collective-permute-start | bytes 2359304 | tf_op jit(solution)/shard_map/ppermute | solution.py:38
  105.2 9.7 %weight_terms.3 = bf16[2048,768]{1,0:T(8,128)(2,1)S(1)} custom-call(s32[2]{0:T(128)S(1)} %pad_add_fusion.at_ref, bf16[2048,128]{1,0:T(8,128)(2,1)S(1)} %get-tuple-element.67.refs_0_, bf16[2048,128]{1,0:T(8,128)(2,1)S(1)} %collective-permute-done.refs_1_, bf16[2048,128]{1,0:T(8,128)(2,1)S(1)} %collective-permute-done.7.refs_2_, ...), custom_call_target="tpu_custom_call" | custom-call | tf_op jit(solution)/shard_map/weight_terms/pallas_call | solution.py:177
  114.9 0.6 collective-permute-start.23
  115.5 4.0 %partial_sums.10 = (bf16[3,128,1024]{2,1,0:T(8,128)(2,1)S(1)}, bf16[3,128,1024]{2,1,0:T(8,128)(2,1)S(1)}) custom-call(s32[2]{0:T(128)S(1)} %pad_add_fusion.at_ref, bf16[4,128,768]{2,1,0:T(8,128)(2,1)S(1)} %collective-permute-done.15.refs_17_.refs_0_.refs_6_, bf16[4,128,768]{2,1,0:T(8,128)(2,1)S(1)} %collective-permute-done.18.refs_18_.refs_1_.refs_7_, ...), custom_call_target="tpu_custom_call" | custom-call | tf_op jit(solution)/shard_map/partial_sums/pallas_call | solution.py:155
  119.5 3.2 %collective-permute-start.28 = (bf16[3,128,1024]{2,1,0:T(8,128)(2,1)S(1)}, bf16[3,128,1024]{2,1,0:T(8,128)(2,1)S(1)}, u32[]{:S(2)}, u32[]{:S(2)}) collective-permute-start(bf16[3,128,1024]{2,1,0:T(8,128)(2,1)S(1)} %get-tuple-element.102), channel_id=1, source_target_pairs={{1,0},{2,1},{3,2},{0,3},{5,4},{6,5},{7,6},{4,7},{9,8},{10,9},{11,1... | collective-permute-start | bytes 2359304 | tf_op jit(solution)/shard_map/ppermute | solution.py:38
  122.8 4.2 %partial_sums.9 = (bf16[3,128,1024]{2,1,0:T(8,128)(2,1)S(1)}, bf16[3,128,1024]{2,1,0:T(8,128)(2,1)S(1)}) custom-call(s32[2]{0:T(128)S(1)} %pad_add_fusion.at_ref, bf16[4,128,768]{2,1,0:T(8,128)(2,1)S(1)} %collective-permute-done.15.refs_17_.refs_0_.refs_6_, bf16[4,128,768]{2,1,0:T(8,128)(2,1)S(1)} %collective-permute-done.18.refs_18_.refs_1_.refs_7_, ...), custom_call_target="tpu_custom_call" | custom-call | tf_op jit(solution)/shard_map/partial_sums/pallas_call | solution.py:155
  127.0 10.2 %collective-permute-done.26.refs_13_ = bf16[3,128,1024]{2,1,0:T(8,128)(2,1)S(1)} collective-permute-done((bf16[3,128,1024]{2,1,0:T(8,128)(2,1)S(1)}, bf16[3,128,1024]{2,1,0:T(8,128)(2,1)S(1)}, u32[]{:S(2)}, u32[]{:S(2)}) %collective-permute-start.26) | collective-permute-done | bytes 786464 | tf_op jit(solution)/shard_map/ppermute | solution.py:38
  137.2 3.2 %collective-permute-start.29 = (bf16[3,128,1024]{2,1,0:T(8,128)(2,1)S(1)}, bf16[3,128,1024]{2,1,0:T(8,128)(2,1)S(1)}, u32[]{:S(2)}, u32[]{:S(2)}) collective-permute-start(bf16[3,128,1024]{2,1,0:T(8,128)(2,1)S(1)} %get-tuple-element.104), channel_id=1, source_target_pairs={{1,0},{2,1},{3,2},{0,3},{5,4},{6,5},{7,6},{4,7},{9,8},{10,9},{11,1... | collective-permute-start | bytes 2359304 | tf_op jit(solution)/shard_map/ppermute | solution.py:38
  140.5 1.3 collective-permute-start.33
  141.8 9.7 %weight_terms.2 = bf16[2048,768]{1,0:T(8,128)(2,1)S(1)} custom-call(s32[2]{0:T(128)S(1)} %pad_add_fusion.at_ref, bf16[2048,128]{1,0:T(8,128)(2,1)S(1)} %get-tuple-element.67.refs_0_, bf16[2048,128]{1,0:T(8,128)(2,1)S(1)} %collective-permute-done.refs_1_, bf16[2048,128]{1,0:T(8,128)(2,1)S(1)} %collective-permute-done.7.refs_2_, ...), custom_call_target="tpu_custom_call" | custom-call | tf_op jit(solution)/shard_map/weight_terms/pallas_call | solution.py:177
  151.5 3.3 %partial_sums.12 = (bf16[1,128,1024]{2,1,0:T(8,128)(2,1)S(1)}, bf16[1,128,1024]{2,1,0:T(8,128)(2,1)S(1)}) custom-call(s32[2]{0:T(128)S(1)} %pad_add_fusion.at_ref, bf16[4,128,768]{2,1,0:T(8,128)(2,1)S(1)} %get-tuple-element.87.refs_16_.refs_0_.refs_2_, bf16[4,128,768]{2,1,0:T(8,128)(2,1)S(1)} %collective-permute-done.16.refs_16_.refs_1_.refs_3_, ...), custom_call_target="tpu_custom_call" | custom-call | tf_op jit(solution)/shard_map/partial_sums/pallas_call | solution.py:155
  154.7 4.5 %partial_sums.11 = (bf16[2,128,1024]{2,1,0:T(8,128)(2,1)S(1)}, bf16[2,128,1024]{2,1,0:T(8,128)(2,1)S(1)}, bf16[2,128,1024]{2,1,0:T(8,128)(2,1)S(1)}) custom-call(s32[2]{0:T(128)S(1)} %pad_add_fusion.at_ref, bf16[4,128,768]{2,1,0:T(8,128)(2,1)S(1)} %collective-permute-done.15.refs_17_.refs_0_.refs_6_, ...), custom_call_target="tpu_custom_call" | custom-call | tf_op jit(solution)/shard_map/partial_sums/pallas_call | solution.py:155
  159.3 3.6 %collective-permute-start.30 = (bf16[2,128,1024]{2,1,0:T(8,128)(2,1)S(1)}, bf16[2,128,1024]{2,1,0:T(8,128)(2,1)S(1)}, u32[]{:S(2)}, u32[]{:S(2)}) collective-permute-start(bf16[2,128,1024]{2,1,0:T(8,128)(2,1)S(1)} %get-tuple-element.106), channel_id=1, source_target_pairs={{16,0},{24,8},{0,16},{8,24},{17,1},{25,9},{1,17},{9,25},{18,2},{26... | collective-permute-start | bytes 1572872 | tf_op jit(solution)/shard_map/ppermute | solution.py:34
  162.9 3.2 %collective-permute-start.35 = (bf16[1,128,1024]{2,1,0:T(8,128)(2,1)S(1)}, bf16[1,128,1024]{2,1,0:T(8,128)(2,1)S(1)}, u32[]{:S(2)}, u32[]{:S(2)}) collective-permute-start(bf16[1,128,1024]{2,1,0:T(8,128)(2,1)S(1)} %get-tuple-element.119), channel_id=1, source_target_pairs={{1,0},{2,1},{3,2},{0,3},{5,4},{6,5},{7,6},{4,7},{9,8},{10,9},{11,1... | collective-permute-start | bytes 786440 | tf_op jit(solution)/shard_map/ppermute | solution.py:38
  166.1 3.3 %partial_sums.14 = (bf16[1,128,1024]{2,1,0:T(8,128)(2,1)S(1)}, bf16[1,128,1024]{2,1,0:T(8,128)(2,1)S(1)}) custom-call(s32[2]{0:T(128)S(1)} %pad_add_fusion.at_ref, bf16[4,128,768]{2,1,0:T(8,128)(2,1)S(1)} %get-tuple-element.87.refs_16_.refs_0_.refs_2_, bf16[4,128,768]{2,1,0:T(8,128)(2,1)S(1)} %collective-permute-done.16.refs_16_.refs_1_.refs_3_, ...), custom_call_target="tpu_custom_call" | custom-call | tf_op jit(solution)/shard_map/partial_sums/pallas_call | solution.py:155
  169.4 3.8 %collective-permute-done.34.refs_8_ = bf16[1,128,1024]{2,1,0:T(8,128)(2,1)S(1)} collective-permute-done((bf16[1,128,1024]{2,1,0:T(8,128)(2,1)S(1)}, bf16[1,128,1024]{2,1,0:T(8,128)(2,1)S(1)}, u32[]{:S(2)}, u32[]{:S(2)}) %collective-permute-start.34) | collective-permute-done | bytes 262176 | tf_op jit(solution)/shard_map/ppermute | solution.py:38
  173.2 3.2 %collective-permute-start.38 = (bf16[1,128,1024]{2,1,0:T(8,128)(2,1)S(1)}, bf16[1,128,1024]{2,1,0:T(8,128)(2,1)S(1)}, u32[]{:S(2)}, u32[]{:S(2)}) collective-permute-start(bf16[1,128,1024]{2,1,0:T(8,128)(2,1)S(1)} %get-tuple-element.129), channel_id=1, source_target_pairs={{1,0},{2,1},{3,2},{0,3},{5,4},{6,5},{7,6},{4,7},{9,8},{10,9},{11,1... | collective-permute-start | bytes 786440 | tf_op jit(solution)/shard_map/ppermute | solution.py:38
  176.4 3.0 %collective-permute-start.31 = (bf16[2,128,1024]{2,1,0:T(8,128)(2,1)S(1)}, bf16[2,128,1024]{2,1,0:T(8,128)(2,1)S(1)}, u32[]{:S(2)}, u32[]{:S(2)}) collective-permute-start(bf16[2,128,1024]{2,1,0:T(8,128)(2,1)S(1)} %get-tuple-element.107), channel_id=1, source_target_pairs={{8,0},{16,8},{24,16},{0,24},{9,1},{17,9},{25,17},{1,25},{10,2},{18... | collective-permute-start | bytes 1572872 | tf_op jit(solution)/shard_map/ppermute | solution.py:34
  179.4 3.2 %collective-permute-done.36.refs_9_ = bf16[1,128,1024]{2,1,0:T(8,128)(2,1)S(1)} collective-permute-done((bf16[1,128,1024]{2,1,0:T(8,128)(2,1)S(1)}, bf16[1,128,1024]{2,1,0:T(8,128)(2,1)S(1)}, u32[]{:S(2)}, u32[]{:S(2)}) %collective-permute-start.36) | collective-permute-done | bytes 262176 | tf_op jit(solution)/shard_map/ppermute | solution.py:38
  182.6 1.2 collective-permute-start.32
  183.8 3.3 %partial_sums.13 = (bf16[1,128,1024]{2,1,0:T(8,128)(2,1)S(1)}, bf16[1,128,1024]{2,1,0:T(8,128)(2,1)S(1)}) custom-call(s32[2]{0:T(128)S(1)} %pad_add_fusion.at_ref, bf16[4,128,768]{2,1,0:T(8,128)(2,1)S(1)} %get-tuple-element.87.refs_16_.refs_0_.refs_2_, bf16[4,128,768]{2,1,0:T(8,128)(2,1)S(1)} %collective-permute-done.16.refs_16_.refs_1_.refs_3_, ...), custom_call_target="tpu_custom_call" | custom-call | tf_op jit(solution)/shard_map/partial_sums/pallas_call | solution.py:155
  187.2 8.3 %collective-permute-done.37.refs_6_ = bf16[1,128,1024]{2,1,0:T(8,128)(2,1)S(1)} collective-permute-done((bf16[1,128,1024]{2,1,0:T(8,128)(2,1)S(1)}, bf16[1,128,1024]{2,1,0:T(8,128)(2,1)S(1)}, u32[]{:S(2)}, u32[]{:S(2)}) %collective-permute-start.37) | collective-permute-done | bytes 262176 | tf_op jit(solution)/shard_map/ppermute | solution.py:38
  195.5 1.4 collective-permute-done.32.refs_3_
  196.9 5.0 %collective-permute-done.39.refs_8_ = bf16[1,128,1024]{2,1,0:T(8,128)(2,1)S(1)} collective-permute-done((bf16[1,128,1024]{2,1,0:T(8,128)(2,1)S(1)}, bf16[1,128,1024]{2,1,0:T(8,128)(2,1)S(1)}, u32[]{:S(2)}, u32[]{:S(2)}) %collective-permute-start.39) | collective-permute-done | bytes 262176 | tf_op jit(solution)/shard_map/ppermute | solution.py:38
  201.9 3.4 %partial_sums.15.refs_0_ = bf16[2,128,1024]{2,1,0:T(8,128)(2,1)S(1)} custom-call(s32[2]{0:T(128)S(1)} %pad_add_fusion.at_ref, bf16[4,128,768]{2,1,0:T(8,128)(2,1)S(1)} %get-tuple-element.87.refs_16_.refs_0_.refs_2_, bf16[4,128,768]{2,1,0:T(8,128)(2,1)S(1)} %collective-permute-done.16.refs_16_.refs_1_.refs_3_, ...), custom_call_target="tpu_custom_call" | custom-call | tf_op jit(solution)/shard_map/partial_sums/pallas_call | solution.py:155
  205.3 2.6 %fusion = bf16[1,2048,768]{2,1,0:T(8,128)(2,1)} fusion(bf16[2048,768]{1,0:T(8,128)(2,1)S(1)} %collective-permute-done.23, bf16[2048,768]{1,0:T(8,128)(2,1)S(1)} %weight_terms.2), kind=kLoop, calls=%fused_computation.1 | loop fusion | flops 6291456 | bytes 9437184 | tf_op jit(solution)/shard_map/broadcast_in_dim | solution.py:311
  207.9 4.4 %finish.1 = bf16[1,128,8192]{2,1,0:T(8,128)(2,1)} custom-call(s32[2]{0:T(128)S(1)} %pad_add_fusion.at_ref, f32[128,128]{1,0:T(8,128)S(1)} %get-tuple-element.112.r_ref, bf16[1,8192]{1,0:T(2,128)(2,1)S(1)} %copy-done.2, bf16[128,8192]{1,0:T(8,128)(2,1)S(1)} %bitcast.13, bf16[1,128,8192]{2,1,0:T(8,128)(2,1)S(1)} %collective-permute-done.33.u_ref, ...), custom_call_target="tpu_custom_call" | custom-call | tf_op jit(solution)/shard_map/finish/pallas_call | solution.py:219
  (44 shorter events, 0.4 us)
Async XLA Ops:
  0.6 5.6 %copy-start.2 = (bf16[1,8192]{1,0:T(2,128)(2,1)S(1)}, bf16[1,8192]{1,0:T(2,128)(2,1)}, u32[]{:S(2)}) copy-start(bf16[1,8192]{1,0:T(2,128)(2,1)} %g_ref.3) | copy-start | bytes 49156
  3.0 20.9 %collective-permute-start.16 = (bf16[4,128,768]{2,1,0:T(8,128)(2,1)}, bf16[4,128,768]{2,1,0:T(8,128)(2,1)S(1)}, u32[]{:S(2)}, u32[]{:S(2)}) collective-permute-start(bf16[4,128,768]{2,1,0:T(8,128)(2,1)} %get-tuple-element.133), channel_id=1, source_target_pairs={{0,4},{1,5},{2,6},{3,7},{4,0},{5,1},{6,2},{7,3},{8,12},{9,13},{10,... | collective-permute-start | bytes 2359304 | tf_op jit(solution)/shard_map/ppermute | solution.py:46
  6.2 1.6 copy-start
  10.5 0.8 copy-start.3
  11.3 21.4 %collective-permute-start.8 = (bf16[2048,128]{1,0:T(8,128)(2,1)S(1)}, bf16[2048,128]{1,0:T(8,128)(2,1)S(1)}, u32[]{:S(2)}, u32[]{:S(2)}) collective-permute-start(bf16[2048,128]{1,0:T(8,128)(2,1)S(1)} %get-tuple-element.67.refs_0_), channel_id=1, source_target_pairs={{3,0},{0,1},{1,2},{2,3},{7,4},{4,5},{5,6},{6,7},{11,8},{8,9},{9,10... | collective-permute-start | bytes 1572872 | tf_op jit(solution)/shard_map/ppermute | solution.py:38
  12.9 20.2 %collective-permute-start = (bf16[2048,128]{1,0:T(8,128)(2,1)S(1)}, bf16[2048,128]{1,0:T(8,128)(2,1)S(1)}, u32[]{:S(2)}, u32[]{:S(2)}) collective-permute-start(bf16[2048,128]{1,0:T(8,128)(2,1)S(1)} %get-tuple-element.67.refs_0_), channel_id=1, source_target_pairs={{1,0},{2,1},{3,2},{0,3},{5,4},{6,5},{7,6},{4,7},{9,8},{10,9},{11,1... | collective-permute-start | bytes 1572872 | tf_op jit(solution)/shard_map/ppermute | solution.py:38
  14.6 14.8 %collective-permute-start.1 = (bf16[2048,128]{1,0:T(8,128)(2,1)}, bf16[2048,128]{1,0:T(8,128)(2,1)}, u32[]{:S(2)}, u32[]{:S(2)}) collective-permute-start(bf16[2048,128]{1,0:T(8,128)(2,1)} %get-tuple-element.69), channel_id=1, source_target_pairs={{8,0},{16,8},{24,16},{0,24},{9,1},{17,9},{25,17},{1,25},{10,2},{18... | collective-permute-start | bytes 1572872 | tf_op jit(solution)/shard_map/ppermute | solution.py:34
  18.6 14.1 %collective-permute-start.2 = (bf16[2048,128]{1,0:T(8,128)(2,1)}, bf16[2048,128]{1,0:T(8,128)(2,1)}, u32[]{:S(2)}, u32[]{:S(2)}) collective-permute-start(bf16[2048,128]{1,0:T(8,128)(2,1)} %get-tuple-element.71), channel_id=1, source_target_pairs={{24,0},{0,8},{8,16},{16,24},{25,1},{1,9},{9,17},{17,25},{26,2},{2,... | collective-permute-start | bytes 1572872 | tf_op jit(solution)/shard_map/ppermute | solution.py:34
  18.6 14.1 %copy-start.4 = (bf16[2048,128]{1,0:T(8,128)(2,1)S(1)}, bf16[2048,128]{1,0:T(8,128)(2,1)}, u32[]{:S(2)}) copy-start(bf16[2048,128]{1,0:T(8,128)(2,1)} %copy-done.3) | copy-start | bytes 1572868
  23.9 74.0 %collective-permute-start.22 = (bf16[2048,768]{1,0:T(8,128)(2,1)S(1)}, bf16[2048,768]{1,0:T(8,128)(2,1)S(1)}, u32[]{:S(2)}, u32[]{:S(2)}) collective-permute-start(bf16[2048,768]{1,0:T(8,128)(2,1)S(1)} %dynamic-slice_bitcast_fusion.refs_6_.refs_8_.refs_12_.refs_14_.refs_2_.refs_4_), channel_id=1, source_target_pairs={{0,4},{1,5},{2,6},{3,7},{4,0},{5,1},{6,2},{7,3},{8,12},{9,13},{10,... | collective-permute-start | bytes 9437192 | tf_op jit(solution)/shard_map/ppermute | solution.py:46
  32.8 13.3 %collective-permute-start.3 = (bf16[2048,128]{1,0:T(8,128)(2,1)S(1)}, bf16[2048,128]{1,0:T(8,128)(2,1)S(1)}, u32[]{:S(2)}, u32[]{:S(2)}) collective-permute-start(bf16[2048,128]{1,0:T(8,128)(2,1)S(1)} %copy-done.4), channel_id=1, source_target_pairs={{16,0},{24,8},{0,16},{8,24},{17,1},{25,9},{1,17},{9,25},{18,2},{26... | collective-permute-start | bytes 1572872 | tf_op jit(solution)/shard_map/ppermute | solution.py:34
  32.8 15.3 %collective-permute-start.9 = (bf16[2048,128]{1,0:T(8,128)(2,1)}, bf16[2048,128]{1,0:T(8,128)(2,1)S(1)}, u32[]{:S(2)}, u32[]{:S(2)}) collective-permute-start(bf16[2048,128]{1,0:T(8,128)(2,1)} %collective-permute-done.1.refs_4_), channel_id=1, source_target_pairs={{3,0},{0,1},{1,2},{2,3},{7,4},{4,5},{5,6},{6,7},{11,8},{8,9},{9,10... | collective-permute-start | bytes 1572872 | tf_op jit(solution)/shard_map/ppermute | solution.py:38
  33.1 15.1 %collective-permute-start.4 = (bf16[2048,128]{1,0:T(8,128)(2,1)}, bf16[2048,128]{1,0:T(8,128)(2,1)S(1)}, u32[]{:S(2)}, u32[]{:S(2)}) collective-permute-start(bf16[2048,128]{1,0:T(8,128)(2,1)} %collective-permute-done.1.refs_4_), channel_id=1, source_target_pairs={{1,0},{2,1},{3,2},{0,3},{5,4},{6,5},{7,6},{4,7},{9,8},{10,9},{11,1... | collective-permute-start | bytes 1572872 | tf_op jit(solution)/shard_map/ppermute | solution.py:38
  46.1 17.7 %collective-permute-start.15 = (bf16[4,128,768]{2,1,0:T(8,128)(2,1)S(1)}, bf16[4,128,768]{2,1,0:T(8,128)(2,1)S(1)}, u32[]{:S(2)}, u32[]{:S(2)}) collective-permute-start(bf16[4,128,768]{2,1,0:T(8,128)(2,1)S(1)} %get-tuple-element.87.refs_16_.refs_0_.refs_2_), channel_id=1, source_target_pairs={{8,0},{16,8},{24,16},{0,24},{9,1},{17,9},{25,17},{1,25},{10,2},{18... | collective-permute-start | bytes 2359304 | tf_op jit(solution)/shard_map/ppermute | solution.py:34
  46.5 17.9 %collective-permute-start.19 = (bf16[4,128,768]{2,1,0:T(8,128)(2,1)S(1)}, bf16[4,128,768]{2,1,0:T(8,128)(2,1)S(1)}, u32[]{:S(2)}, u32[]{:S(2)}) collective-permute-start(bf16[4,128,768]{2,1,0:T(8,128)(2,1)S(1)} %get-tuple-element.87.refs_16_.refs_0_.refs_2_), channel_id=1, source_target_pairs={{24,0},{0,8},{8,16},{16,24},{25,1},{1,9},{9,17},{17,25},{26,2},{2,... | collective-permute-start | bytes 2359304 | tf_op jit(solution)/shard_map/ppermute | solution.py:34
  48.1 12.3 %collective-permute-start.10 = (bf16[2048,128]{1,0:T(8,128)(2,1)}, bf16[2048,128]{1,0:T(8,128)(2,1)S(1)}, u32[]{:S(2)}, u32[]{:S(2)}) collective-permute-start(bf16[2048,128]{1,0:T(8,128)(2,1)} %collective-permute-done.2.refs_12_), channel_id=1, source_target_pairs={{3,0},{0,1},{1,2},{2,3},{7,4},{4,5},{5,6},{6,7},{11,8},{8,9},{9,10... | collective-permute-start | bytes 1572872 | tf_op jit(solution)/shard_map/ppermute | solution.py:38
  48.2 17.6 %collective-permute-start.5 = (bf16[2048,128]{1,0:T(8,128)(2,1)}, bf16[2048,128]{1,0:T(8,128)(2,1)S(1)}, u32[]{:S(2)}, u32[]{:S(2)}) collective-permute-start(bf16[2048,128]{1,0:T(8,128)(2,1)} %collective-permute-done.2.refs_12_), channel_id=1, source_target_pairs={{1,0},{2,1},{3,2},{0,3},{5,4},{6,5},{7,6},{4,7},{9,8},{10,9},{11,1... | collective-permute-start | bytes 1572872 | tf_op jit(solution)/shard_map/ppermute | solution.py:38
  60.4 12.1 %collective-permute-start.11 = (bf16[2048,128]{1,0:T(8,128)(2,1)S(1)}, bf16[2048,128]{1,0:T(8,128)(2,1)S(1)}, u32[]{:S(2)}, u32[]{:S(2)}) collective-permute-start(bf16[2048,128]{1,0:T(8,128)(2,1)S(1)} %collective-permute-done.3.refs_8_), channel_id=1, source_target_pairs={{3,0},{0,1},{1,2},{2,3},{7,4},{4,5},{5,6},{6,7},{11,8},{8,9},{9,10... | collective-permute-start | bytes 1572872 | tf_op jit(solution)/shard_map/ppermute | solution.py:38
  63.8 17.7 %collective-permute-start.17 = (bf16[4,128,768]{2,1,0:T(8,128)(2,1)S(1)}, bf16[4,128,768]{2,1,0:T(8,128)(2,1)S(1)}, u32[]{:S(2)}, u32[]{:S(2)}) collective-permute-start(bf16[4,128,768]{2,1,0:T(8,128)(2,1)S(1)} %collective-permute-done.16.refs_16_.refs_1_.refs_3_), channel_id=1, source_target_pairs={{8,0},{16,8},{24,16},{0,24},{9,1},{17,9},{25,17},{1,25},{10,2},{18... | collective-permute-start | bytes 2359304 | tf_op jit(solution)/shard_map/ppermute | solution.py:34
  64.4 17.7 %collective-permute-start.20 = (bf16[4,128,768]{2,1,0:T(8,128)(2,1)S(1)}, bf16[4,128,768]{2,1,0:T(8,128)(2,1)S(1)}, u32[]{:S(2)}, u32[]{:S(2)}) collective-permute-start(bf16[4,128,768]{2,1,0:T(8,128)(2,1)S(1)} %collective-permute-done.16.refs_16_.refs_1_.refs_3_), channel_id=1, source_target_pairs={{24,0},{0,8},{8,16},{16,24},{25,1},{1,9},{9,17},{17,25},{26,2},{2,... | collective-permute-start | bytes 2359304 | tf_op jit(solution)/shard_map/ppermute | solution.py:34
  65.8 12.7 %collective-permute-start.6 = (bf16[2048,128]{1,0:T(8,128)(2,1)S(1)}, bf16[2048,128]{1,0:T(8,128)(2,1)S(1)}, u32[]{:S(2)}, u32[]{:S(2)}) collective-permute-start(bf16[2048,128]{1,0:T(8,128)(2,1)S(1)} %collective-permute-done.3.refs_8_), channel_id=1, source_target_pairs={{1,0},{2,1},{3,2},{0,3},{5,4},{6,5},{7,6},{4,7},{9,8},{10,9},{11,1... | collective-permute-start | bytes 1572872 | tf_op jit(solution)/shard_map/ppermute | solution.py:38
  72.4 12.8 %collective-permute-start.12 = (bf16[2048,128]{1,0:T(8,128)(2,1)S(1)}, bf16[2048,128]{1,0:T(8,128)(2,1)S(1)}, u32[]{:S(2)}, u32[]{:S(2)}) collective-permute-start(bf16[2048,128]{1,0:T(8,128)(2,1)S(1)} %collective-permute-done.9.refs_7_), channel_id=1, source_target_pairs={{3,0},{0,1},{1,2},{2,3},{7,4},{4,5},{5,6},{6,7},{11,8},{8,9},{9,10... | collective-permute-start | bytes 1572872 | tf_op jit(solution)/shard_map/ppermute | solution.py:38
  78.5 13.5 %collective-permute-start.7 = (bf16[2048,128]{1,0:T(8,128)(2,1)S(1)}, bf16[2048,128]{1,0:T(8,128)(2,1)S(1)}, u32[]{:S(2)}, u32[]{:S(2)}) collective-permute-start(bf16[2048,128]{1,0:T(8,128)(2,1)S(1)} %collective-permute-done.refs_1_), channel_id=1, source_target_pairs={{1,0},{2,1},{3,2},{0,3},{5,4},{6,5},{7,6},{4,7},{9,8},{10,9},{11,1... | collective-permute-start | bytes 1572872 | tf_op jit(solution)/shard_map/ppermute | solution.py:38
  81.5 14.5 %collective-permute-start.18 = (bf16[4,128,768]{2,1,0:T(8,128)(2,1)S(1)}, bf16[4,128,768]{2,1,0:T(8,128)(2,1)S(1)}, u32[]{:S(2)}, u32[]{:S(2)}) collective-permute-start(bf16[4,128,768]{2,1,0:T(8,128)(2,1)S(1)} %collective-permute-done.15.refs_17_.refs_0_.refs_6_), channel_id=1, source_target_pairs={{8,0},{16,8},{24,16},{0,24},{9,1},{17,9},{25,17},{1,25},{10,2},{18... | collective-permute-start | bytes 2359304 | tf_op jit(solution)/shard_map/ppermute | solution.py:34
  82.1 15.8 %collective-permute-start.21 = (bf16[4,128,768]{2,1,0:T(8,128)(2,1)S(1)}, bf16[4,128,768]{2,1,0:T(8,128)(2,1)S(1)}, u32[]{:S(2)}, u32[]{:S(2)}) collective-permute-start(bf16[4,128,768]{2,1,0:T(8,128)(2,1)S(1)} %collective-permute-done.20.refs_19_.refs_5_.refs_11_), channel_id=1, source_target_pairs={{24,0},{0,8},{8,16},{16,24},{25,1},{1,9},{9,17},{17,25},{26,2},{2,... | collective-permute-start | bytes 2359304 | tf_op jit(solution)/shard_map/ppermute | solution.py:34
  85.3 16.6 %collective-permute-start.13 = (bf16[2048,128]{1,0:T(8,128)(2,1)S(1)}, bf16[2048,128]{1,0:T(8,128)(2,1)S(1)}, u32[]{:S(2)}, u32[]{:S(2)}) collective-permute-start(bf16[2048,128]{1,0:T(8,128)(2,1)S(1)} %collective-permute-done.11.refs_11_), channel_id=1, source_target_pairs={{3,0},{0,1},{1,2},{2,3},{7,4},{4,5},{5,6},{6,7},{11,8},{8,9},{9,10... | collective-permute-start | bytes 1572872 | tf_op jit(solution)/shard_map/ppermute | solution.py:38
  92.1 10.6 %collective-permute-start.14 = (bf16[2048,128]{1,0:T(8,128)(2,1)S(1)}, bf16[2048,128]{1,0:T(8,128)(2,1)S(1)}, u32[]{:S(2)}, u32[]{:S(2)}) collective-permute-start(bf16[2048,128]{1,0:T(8,128)(2,1)S(1)} %collective-permute-done.5.refs_13_), channel_id=1, source_target_pairs={{1,0},{2,1},{3,2},{0,3},{5,4},{6,5},{7,6},{4,7},{9,8},{10,9},{11,1... | collective-permute-start | bytes 1572872 | tf_op jit(solution)/shard_map/ppermute | solution.py:38
  101.9 17.6 %collective-permute-start.24 = (bf16[3,128,1024]{2,1,0:T(8,128)(2,1)S(1)}, bf16[3,128,1024]{2,1,0:T(8,128)(2,1)S(1)}, u32[]{:S(2)}, u32[]{:S(2)}) collective-permute-start(bf16[3,128,1024]{2,1,0:T(8,128)(2,1)S(1)} %get-tuple-element.93), channel_id=1, source_target_pairs={{3,0},{0,1},{1,2},{2,3},{7,4},{4,5},{5,6},{6,7},{11,8},{8,9},{9,10... | collective-permute-start | bytes 2359304 | tf_op jit(solution)/shard_map/ppermute | solution.py:38
  102.7 16.8 %collective-permute-start.25 = (bf16[3,128,1024]{2,1,0:T(8,128)(2,1)S(1)}, bf16[3,128,1024]{2,1,0:T(8,128)(2,1)S(1)}, u32[]{:S(2)}, u32[]{:S(2)}) collective-permute-start(bf16[3,128,1024]{2,1,0:T(8,128)(2,1)S(1)} %get-tuple-element.95), channel_id=1, source_target_pairs={{1,0},{2,1},{3,2},{0,3},{5,4},{6,5},{7,6},{4,7},{9,8},{10,9},{11,1... | collective-permute-start | bytes 2359304 | tf_op jit(solution)/shard_map/ppermute | solution.py:38
  114.9 82.0 %collective-permute-start.23 = (bf16[2048,768]{1,0:T(8,128)(2,1)S(1)}, bf16[2048,768]{1,0:T(8,128)(2,1)S(1)}, u32[]{:S(2)}, u32[]{:S(2)}) collective-permute-start(bf16[2048,768]{1,0:T(8,128)(2,1)S(1)} %weight_terms.3), channel_id=1, source_target_pairs={{0,4},{1,5},{2,6},{3,7},{4,0},{5,1},{6,2},{7,3},{8,12},{9,13},{10,... | collective-permute-start | bytes 9437192 | tf_op jit(solution)/shard_map/ppermute | solution.py:46
  119.4 17.8 %collective-permute-start.26 = (bf16[3,128,1024]{2,1,0:T(8,128)(2,1)S(1)}, bf16[3,128,1024]{2,1,0:T(8,128)(2,1)S(1)}, u32[]{:S(2)}, u32[]{:S(2)}) collective-permute-start(bf16[3,128,1024]{2,1,0:T(8,128)(2,1)S(1)} %get-tuple-element.98), channel_id=1, source_target_pairs={{3,0},{0,1},{1,2},{2,3},{7,4},{4,5},{5,6},{6,7},{11,8},{8,9},{9,10... | collective-permute-start | bytes 2359304 | tf_op jit(solution)/shard_map/ppermute | solution.py:38
  119.5 20.9 %copy-start.5 = (bf16[1,128,8192]{2,1,0:T(8,128)(2,1)S(1)}, bf16[1,128,8192]{2,1,0:T(8,128)(2,1)}, u32[]{:S(2)}) copy-start(bf16[1,128,8192]{2,1,0:T(8,128)(2,1)} %param.9) | copy-start | bytes 6291460
  119.5 17.7 %collective-permute-start.28 = (bf16[3,128,1024]{2,1,0:T(8,128)(2,1)S(1)}, bf16[3,128,1024]{2,1,0:T(8,128)(2,1)S(1)}, u32[]{:S(2)}, u32[]{:S(2)}) collective-permute-start(bf16[3,128,1024]{2,1,0:T(8,128)(2,1)S(1)} %get-tuple-element.102), channel_id=1, source_target_pairs={{1,0},{2,1},{3,2},{0,3},{5,4},{6,5},{7,6},{4,7},{9,8},{10,9},{11,1... | collective-permute-start | bytes 2359304 | tf_op jit(solution)/shard_map/ppermute | solution.py:38
  137.2 17.5 %collective-permute-start.27 = (bf16[3,128,1024]{2,1,0:T(8,128)(2,1)S(1)}, bf16[3,128,1024]{2,1,0:T(8,128)(2,1)S(1)}, u32[]{:S(2)}, u32[]{:S(2)}) collective-permute-start(bf16[3,128,1024]{2,1,0:T(8,128)(2,1)S(1)} %get-tuple-element.99), channel_id=1, source_target_pairs={{3,0},{0,1},{1,2},{2,3},{7,4},{4,5},{5,6},{6,7},{11,8},{8,9},{9,10... | collective-permute-start | bytes 2359304 | tf_op jit(solution)/shard_map/ppermute | solution.py:38
  137.2 17.5 %collective-permute-start.29 = (bf16[3,128,1024]{2,1,0:T(8,128)(2,1)S(1)}, bf16[3,128,1024]{2,1,0:T(8,128)(2,1)S(1)}, u32[]{:S(2)}, u32[]{:S(2)}) collective-permute-start(bf16[3,128,1024]{2,1,0:T(8,128)(2,1)S(1)} %get-tuple-element.104), channel_id=1, source_target_pairs={{1,0},{2,1},{3,2},{0,3},{5,4},{6,5},{7,6},{4,7},{9,8},{10,9},{11,1... | collective-permute-start | bytes 2359304 | tf_op jit(solution)/shard_map/ppermute | solution.py:38
  140.5 67.4 %collective-permute-start.33 = (bf16[1,128,8192]{2,1,0:T(8,128)(2,1)S(1)}, bf16[1,128,8192]{2,1,0:T(8,128)(2,1)S(1)}, u32[]{:S(2)}, u32[]{:S(2)}) collective-permute-start(bf16[1,128,8192]{2,1,0:T(8,128)(2,1)S(1)} %copy-done.5), channel_id=1, source_target_pairs={{32,0},{64,32},{96,64},{33,1},{65,33},{97,65},{34,2},{66,34},{98,6... | collective-permute-start | bytes 6291464 | tf_op jit(solution)/shard_map/ppermute | solution.py:259
  159.3 17.2 %collective-permute-start.30 = (bf16[2,128,1024]{2,1,0:T(8,128)(2,1)S(1)}, bf16[2,128,1024]{2,1,0:T(8,128)(2,1)S(1)}, u32[]{:S(2)}, u32[]{:S(2)}) collective-permute-start(bf16[2,128,1024]{2,1,0:T(8,128)(2,1)S(1)} %get-tuple-element.106), channel_id=1, source_target_pairs={{16,0},{24,8},{0,16},{8,24},{17,1},{25,9},{1,17},{9,25},{18,2},{26... | collective-permute-start | bytes 1572872 | tf_op jit(solution)/shard_map/ppermute | solution.py:34
  162.9 10.3 %collective-permute-start.34 = (bf16[1,128,1024]{2,1,0:T(8,128)(2,1)S(1)}, bf16[1,128,1024]{2,1,0:T(8,128)(2,1)S(1)}, u32[]{:S(2)}, u32[]{:S(2)}) collective-permute-start(bf16[1,128,1024]{2,1,0:T(8,128)(2,1)S(1)} %get-tuple-element.115), channel_id=1, source_target_pairs={{3,0},{0,1},{1,2},{2,3},{7,4},{4,5},{5,6},{6,7},{11,8},{8,9},{9,10... | collective-permute-start | bytes 786440 | tf_op jit(solution)/shard_map/ppermute | solution.py:38
  162.9 10.3 %collective-permute-start.35 = (bf16[1,128,1024]{2,1,0:T(8,128)(2,1)S(1)}, bf16[1,128,1024]{2,1,0:T(8,128)(2,1)S(1)}, u32[]{:S(2)}, u32[]{:S(2)}) collective-permute-start(bf16[1,128,1024]{2,1,0:T(8,128)(2,1)S(1)} %get-tuple-element.119), channel_id=1, source_target_pairs={{1,0},{2,1},{3,2},{0,3},{5,4},{6,5},{7,6},{4,7},{9,8},{10,9},{11,1... | collective-permute-start | bytes 786440 | tf_op jit(solution)/shard_map/ppermute | solution.py:38
  173.2 9.4 %collective-permute-start.36 = (bf16[1,128,1024]{2,1,0:T(8,128)(2,1)S(1)}, bf16[1,128,1024]{2,1,0:T(8,128)(2,1)S(1)}, u32[]{:S(2)}, u32[]{:S(2)}) collective-permute-start(bf16[1,128,1024]{2,1,0:T(8,128)(2,1)S(1)} %get-tuple-element.123), channel_id=1, source_target_pairs={{3,0},{0,1},{1,2},{2,3},{7,4},{4,5},{5,6},{6,7},{11,8},{8,9},{9,10... | collective-permute-start | bytes 786440 | tf_op jit(solution)/shard_map/ppermute | solution.py:38
  173.2 13.9 %collective-permute-start.38 = (bf16[1,128,1024]{2,1,0:T(8,128)(2,1)S(1)}, bf16[1,128,1024]{2,1,0:T(8,128)(2,1)S(1)}, u32[]{:S(2)}, u32[]{:S(2)}) collective-permute-start(bf16[1,128,1024]{2,1,0:T(8,128)(2,1)S(1)} %get-tuple-element.129), channel_id=1, source_target_pairs={{1,0},{2,1},{3,2},{0,3},{5,4},{6,5},{7,6},{4,7},{9,8},{10,9},{11,1... | collective-permute-start | bytes 786440 | tf_op jit(solution)/shard_map/ppermute | solution.py:38
  176.4 19.1 %collective-permute-start.31 = (bf16[2,128,1024]{2,1,0:T(8,128)(2,1)S(1)}, bf16[2,128,1024]{2,1,0:T(8,128)(2,1)S(1)}, u32[]{:S(2)}, u32[]{:S(2)}) collective-permute-start(bf16[2,128,1024]{2,1,0:T(8,128)(2,1)S(1)} %get-tuple-element.107), channel_id=1, source_target_pairs={{8,0},{16,8},{24,16},{0,24},{9,1},{17,9},{25,17},{1,25},{10,2},{18... | collective-permute-start | bytes 1572872 | tf_op jit(solution)/shard_map/ppermute | solution.py:34
  182.6 14.2 %collective-permute-start.32 = (bf16[2,128,1024]{2,1,0:T(8,128)(2,1)S(1)}, bf16[2,128,1024]{2,1,0:T(8,128)(2,1)S(1)}, u32[]{:S(2)}, u32[]{:S(2)}) collective-permute-start(bf16[2,128,1024]{2,1,0:T(8,128)(2,1)S(1)} %get-tuple-element.110), channel_id=1, source_target_pairs={{24,0},{0,8},{8,16},{16,24},{25,1},{1,9},{9,17},{17,25},{26,2},{2,... | collective-permute-start | bytes 1572872 | tf_op jit(solution)/shard_map/ppermute | solution.py:34
  187.1 8.4 %collective-permute-start.37 = (bf16[1,128,1024]{2,1,0:T(8,128)(2,1)S(1)}, bf16[1,128,1024]{2,1,0:T(8,128)(2,1)S(1)}, u32[]{:S(2)}, u32[]{:S(2)}) collective-permute-start(bf16[1,128,1024]{2,1,0:T(8,128)(2,1)S(1)} %get-tuple-element.124), channel_id=1, source_target_pairs={{3,0},{0,1},{1,2},{2,3},{7,4},{4,5},{5,6},{6,7},{11,8},{8,9},{9,10... | collective-permute-start | bytes 786440 | tf_op jit(solution)/shard_map/ppermute | solution.py:38
  195.5 6.4 %collective-permute-start.39 = (bf16[1,128,1024]{2,1,0:T(8,128)(2,1)S(1)}, bf16[1,128,1024]{2,1,0:T(8,128)(2,1)S(1)}, u32[]{:S(2)}, u32[]{:S(2)}) collective-permute-start(bf16[1,128,1024]{2,1,0:T(8,128)(2,1)S(1)} %get-tuple-element.131), channel_id=1, source_target_pairs={{1,0},{2,1},{3,2},{0,3},{5,4},{6,5},{7,6},{4,7},{9,8},{10,9},{11,1... | collective-permute-start | bytes 786440 | tf_op jit(solution)/shard_map/ppermute | solution.py:38
  205.3 2.6 %copy-start.1 = (bf16[1,128,8192]{2,1,0:T(8,128)(2,1)S(1)}, bf16[1,128,8192]{2,1,0:T(8,128)(2,1)}, u32[]{:S(2)}) copy-start(bf16[1,128,8192]{2,1,0:T(8,128)(2,1)} %param.5) | copy-start | bytes 6291460

commit v4 on v3

v4 whole, which is shorter than its diff:
```python
import functools

import jax
import jax.numpy as jnp
from jax import lax
from jax.experimental import pallas as pl
from jax.experimental.pallas import tpu as pltpu
from jax.sharding import PartitionSpec as P

N_Z = 4
N_Y = 4
F32 = jnp.float32
BF16 = jnp.bfloat16
VMEM_BYTES = 20 * 2**20


class Chains:
    def __init__(self):
        self.sent = {}

    def __call__(self, key, block, send, depth=1):
        sent = self.sent.setdefault(key, [])
        if len(sent) >= depth:
            block, _ = lax.optimization_barrier((block, sent[-depth]))
        sent.append(send(block))
        return sent[-1]


def after(block, *others):
    return lax.optimization_barrier((block, *others))[0]


def from_z(block, o):
    return lax.ppermute(block, "dp", [((i + o) % N_Z, i) for i in range(N_Z)])


def from_y(block, o):
    return lax.ppermute(
        block,
        "tensor",
        [(x * N_Y + (i + o) % N_Y, x * N_Y + i) for x in range(2) for i in range(N_Y)],
    )


def from_x(block):
    return lax.ppermute(block, "tensor", [(i, (i + N_Y) % (2 * N_Y)) for i in range(2 * N_Y)])


def dot_nt(a, b):
    return lax.dot_general(a, b, (((1,), (1,)), ((), ())), preferred_element_type=F32)


def dot_nn(a, b):
    return lax.dot_general(a, b, (((1,), (0,)), ((), ())), preferred_element_type=F32)


def call(kernel, grid, in_specs, out_specs, out_shape, flops=0, bytes_accessed=0, name=None):
    return pl.pallas_call(
        kernel,
        grid_spec=pltpu.PrefetchScalarGridSpec(
            num_scalar_prefetch=1, grid=grid, in_specs=in_specs, out_specs=out_specs
        ),
        out_shape=out_shape,
        name=name,
        compiler_params=pltpu.CompilerParams(vmem_limit_bytes=VMEM_BYTES),
        cost_estimate=pl.CostEstimate(
            flops=flops, bytes_accessed=bytes_accessed, transcendentals=0
        ),
    )


WHOLE = pl.BlockSpec(memory_space=pltpu.VMEM)


def normalize(place, hidden, gain):
    rows, width = hidden.shape
    part = width // N_Z

    def kernel(at_ref, h_ref, g_ref, r_ref, *out_refs):
        x = h_ref[...].astype(F32)
        r = lax.rsqrt(jnp.mean(x * x, axis=-1, keepdims=True) + 1e-06)
        r_ref[...] = jnp.broadcast_to(r, r_ref.shape)
        for d in range(N_Z):
            at = pl.multiple_of(lax.rem(at_ref[0] + d, N_Z) * part, part)
            x = h_ref[:, pl.ds(at, part)].astype(F32)
            g = g_ref[:, pl.ds(at, part)].astype(F32)
            out_refs[d][...] = ((x * r) * g).T.astype(BF16)

    return call(
        kernel,
        (),
        [WHOLE, WHOLE],
        [WHOLE] * (1 + N_Z),
        [jax.ShapeDtypeStruct((rows, 128), F32)]
        + [jax.ShapeDtypeStruct((part, rows), BF16)] * N_Z,
        bytes_accessed=4 * rows * width,
        name="normalize",
    )(place, hidden, gain)


def partial_sums(place, seqs, groups, g_own, g_par, w_own, w_par, extras=(), per_sequence=False):
    _, _, rows, cols = g_own.shape
    part = w_own.shape[0]
    half = part // 2
    step = 256
    steps = half // step
    count = len(seqs)
    jobs = [job for group in groups for job in group]
    qs = sorted({q for q, _, _ in jobs})
    sides = sorted({side for _, side, _ in jobs})
    n_g, n_w, n_e = 2 * count * len(qs), 2 * len(sides), len(extras)

    def kernel(at_ref, *refs):
        g_refs, w_refs = refs[:n_g], refs[n_g : n_g + n_w]
        e_refs, outs = refs[n_g + n_w : n_g + n_w + n_e], refs[n_g + n_w + n_e :]
        for k, group in enumerate(groups):
            for j, (q, side, adds) in enumerate(group):
                at = qs.index(q) * 2 * count
                left = jnp.concatenate([g_refs[at + o][0, 0] for o in range(count)], 0)
                right = jnp.concatenate([g_refs[at + count + o][0, 0] for o in range(count)], 0)
                s = sides.index(side) * 2
                total = dot_nt(left, w_refs[s][...]) + dot_nt(right, w_refs[s + 1][...])
                total = total.reshape(count, rows, step)
                for e, i in adds:
                    total = total + e_refs[e][i].astype(F32)
                if per_sequence:
                    for o in range(count):
                        outs[o][side] = total[o].astype(BF16)
                else:
                    outs[k][j] = total.astype(BF16)

    def tokens_of(o, q):
        return pl.BlockSpec(
            (1, 1, rows, cols),
            lambda i, at: (lax.rem(at[0] + o, N_Z), lax.rem(at[1] + q, N_Y), 0, 0),
        )

    def features_of(side):
        return pl.BlockSpec((step, cols), lambda i, at: (side * steps + i, 0))

    def chunk(n):
        return pl.BlockSpec((n, count, rows, step), lambda i, at: (0, 0, 0, i))

    in_specs, operands = [], []
    for q in qs:
        for array in (g_own, g_par):
            for o in seqs:
                in_specs.append(tokens_of(o, q))
                operands.append(array)
    for side in sides:
        for w in (w_own, w_par):
            in_specs.append(features_of(side))
            operands.append(w)
    in_specs += [chunk(e.shape[0]) for e in extras]
    operands += list(extras)
    if per_sequence:
        out_specs = [pl.BlockSpec((2, rows, step), lambda i, at: (0, 0, i))] * count
        out_shape = [jax.ShapeDtypeStruct((2, rows, half), BF16)] * count
    else:
        out_specs = [chunk(len(group)) for group in groups]
        out_shape = [
            jax.ShapeDtypeStruct((len(group), count, rows, half), BF16) for group in groups
        ]
    return call(
        kernel, (steps,), in_specs, out_specs, out_shape, name="partial_sums"
    )(place, *operands)


def weight_terms(place, n_pieces, g):
    part, rows = n_pieces[0][0].shape
    cols = g.shape[3]
    step = 512

    def kernel(at_ref, *refs):
        n_refs, (g_ref, out_ref) = refs[: N_Z * N_Y], refs[N_Z * N_Y :]
        total = None
        for o in range(N_Z):
            left = jnp.concatenate([n_refs[o * N_Y + q][...] for q in range(N_Y)], 1)
            z = lax.rem(at_ref[0] + o, N_Z)
            right = jnp.concatenate(
                [g_ref[z, lax.rem(at_ref[1] + q, N_Y)] for q in range(N_Y)], 0
            )
            term = dot_nn(left, right)
            total = term if total is None else total + term
        out_ref[...] = total.astype(BF16)

    return call(
        kernel,
        (part // step,),
        [pl.BlockSpec((step, rows), lambda i, at: (i, 0))] * (N_Z * N_Y)
        + [pl.BlockSpec((N_Z, N_Y, rows, cols), lambda i, at: (0, 0, 0, 0))],
        pl.BlockSpec((step, cols), lambda i, at: (i, 0)),
        jax.ShapeDtypeStruct((part, cols), BF16),
        name="weight_terms",
    )(place, *[n_pieces[o][q] for o in range(N_Z) for q in range(N_Y)], g)


def finish(place, deviation, gain, hidden, received, h):
    rows, width = hidden.shape
    part = width // N_Z
    half = part // 2
    step = 32

    def kernel(at_ref, r_ref, g_ref, x_ref, u_ref, *refs):
        h_refs, out_ref = refs[:-1], refs[-1]
        r = r_ref[:, :1]
        spots = [
            (o, s, pl.multiple_of(lax.rem(at_ref[0] + o, N_Z) * part + s * half, half))
            for o in range(N_Z)
            for s in range(2)
        ]

        def terms(o, s, at):
            xhat = x_ref[:, pl.ds(at, half)].astype(F32) * r
            scaled = g_ref[:, pl.ds(at, half)].astype(F32) * h_refs[o][s].astype(F32)
            return xhat, scaled

        total = jnp.zeros((step, 1), F32)
        for spot in spots:
            xhat, scaled = terms(*spot)
            total += jnp.sum(scaled * xhat, axis=-1, keepdims=True)
        mean = total / width
        for spot in spots:
            xhat, scaled = terms(*spot)
            at = spot[2]
            up = u_ref[0, :, pl.ds(at, half)].astype(F32)
            out_ref[0, :, pl.ds(at, half)] = (up + r * (scaled - xhat * mean)).astype(BF16)

    return call(
        kernel,
        (rows // step,),
        [
            pl.BlockSpec((step, 128), lambda i, at: (i, 0)),
            pl.BlockSpec((1, width), lambda i, at: (0, 0)),
            pl.BlockSpec((step, width), lambda i, at: (i, 0)),
            pl.BlockSpec((1, step, width), lambda i, at: (0, i, 0)),
        ]
        + [pl.BlockSpec((2, step, half), lambda i, at: (0, i, 0))] * N_Z,
        pl.BlockSpec((1, step, width), lambda i, at: (0, i, 0)),
        jax.ShapeDtypeStruct((1, rows, width), BF16),
        name="finish",
    )(place, deviation, gain, hidden, received, *h)


def shards(hidden_in, norm_gain, qkv_weight, qkv_grad, upper_grad):
    tensor = lax.axis_index("tensor")
    xh, y, z = tensor // N_Y, tensor % N_Y, lax.axis_index("dp")
    place = jnp.stack([z, y]).astype(jnp.int32)
    rows = hidden_in.shape[1]
    part = hidden_in.shape[2] // N_Z
    cols = qkv_grad.shape[2]
    layers = lax.axis_size("pipe")
    chains = Chains()

    def yy(block, o, depth=1):
        return chains("y%d" % o, block, lambda b: from_y(b, o), depth)

    def xx(block):
        return chains("x", block, from_x)

    grads = qkv_grad[0].reshape(2, N_Y, rows, cols)
    par0 = xx(lax.dynamic_index_in_dim(grads, 1 - xh, 0, keepdims=False))
    g_own = lax.all_gather(lax.dynamic_index_in_dim(grads, xh, 0, keepdims=False), "dp")

    deviation, *n_to = normalize(place, hidden_in[0], norm_gain)
    n1, n3 = from_z(n_to[3], 1), from_z(n_to[1], 3)
    n_up, n_down = {0: yy(n_to[0], 1, 2)}, {0: yy(n_to[0], 3, 2)}
    n2 = from_z(after(n_to[2], n1, n3), 2)
    n_near = [n_to[0], n1, n2, n3]

    g_par = lax.all_gather(after(par0, n1, n3), "dp")
    w_own = lax.dynamic_slice_in_dim(qkv_weight[0], z * part, part, 0)
    w_par = xx(after(w_own, n1, n3, n_up[0], n_down[0]))
    received = lax.ppermute(
        after(upper_grad, w_par), "pipe", [(i + 1, i) for i in range(layers - 1)]
    )
    for o in (1, 3, 2):
        n_up[o], n_down[o] = yy(n_near[o], 1, 2), yy(n_near[o], 3, 2)
    n_across = {}
    for one, other in ((0, 1), (3, 2)):
        n_across[one], n_across[other] = yy(n_up[one], 1, 2), yy(n_down[other], 3, 2)
    n_pieces = [[n_near[o], n_up[o], n_across[o], n_down[o]] for o in range(N_Z)]

    dw_got = xx(weight_terms(place, n_pieces, g_par))
    dw_own = weight_terms(place, n_pieces, g_own)

    sums = functools.partial(partial_sums, place, g_own=g_own, g_par=g_par, w_own=w_own, w_par=w_par)

    def first(seqs):
        up, down = sums(seqs, [[(2, 0, ()), (1, 1, ())], [(2, 1, ()), (3, 0, ())]])
        return yy(up, 3), yy(down, 1)

    def second(seqs, up, down):
        up2, down2 = sums(seqs, [[(1, 0, [(0, 0)])], [(3, 1, [(1, 0)])]], extras=[up, down])
        return yy(up2, 3), yy(down2, 1)

    def third(seqs, up, down, up2, down2):
        return sums(
            seqs,
            [[(0, 0, [(1, 1), (2, 0)]), (0, 1, [(0, 1), (3, 0)])]],
            extras=[up, down, up2, down2],
            per_sequence=True,
        )

    here, there = [2, 3], [1, 0]
    one = first(here)
    two = first(there)
    one = one + second(here, after(one[0], received), one[1])
    two = two + second(there, *two)
    h_to2, h_to3 = third(here, after(one[0], dw_own), *one[1:])
    h2, h1 = from_z(h_to2, 2), from_z(h_to3, 1)
    h_to1, h0 = third(there, *two)
    h3 = from_z(h_to1, 3)

    weight_out = (dw_own.astype(F32) + after(dw_got, h1, h2).astype(F32)).astype(BF16)
    input_out = finish(place, deviation, norm_gain, hidden_in[0], received, [h0, h1, h2, h3])
    return (weight_out[None], input_out)


def solution(mesh):
    placed = (
        P("pipe", ("dp", "tensor"), None),
        P("pipe", None),
        P("pipe", None, "tensor"),
        P("pipe", "dp", "tensor"),
        P("pipe", ("dp", "tensor"), None),
    )
    return jax.shard_map(
        shards,
        mesh=mesh,
        in_specs=placed,
        out_specs=(P("pipe", "dp", "tensor"), P("pipe", ("dp", "tensor"), None)),
        check_vma=False,
    )
```

time: 213 us -> 251 us (1.18)
  waiting for transfers between devices: 90.5 us -> 117 us
  between operations: 0.88 us -> 14.3 us
  local copies, waits for them, and re-layouts: 6.94 us -> 17.3 us
  starting transfers between devices: 54.9 us -> 48.5 us
  Pallas kernels: 56.4 us -> 51.6 us
    ppermute x12 -> x6, waiting for transfers between devices: 28 us -> 40.4 us  [from_z(): return lax.ppermute(block, 'dp', [((i + o) % N_Z, i) for i in range(N_Z)])]
    ppermute x3, waiting for transfers between devices: 3.11 us -> 14.2 us  [from_x(): lax.ppermute(block, 'tensor', [(i, (i + N_Y) % (2 * N_Y)) for i in range(...]
    unnamed x12 -> x42, local copies, waits for them, and re-layouts: 2.42 us -> 12.3 us
    ppermute x12 -> x6, starting transfers between devices: 17.9 us -> 11.3 us  [from_z(): return lax.ppermute(block, 'dp', [((i + o) % N_Z, i) for i in range(N_Z)])]
    pallas_call x8 -> x6, Pallas kernels: 29.9 us -> 23.8 us  [partial_sums(): call(kernel, (steps,), in_specs, out_specs, out_shape, name='partial_sums')]
    ppermute x24 -> x20, starting transfers between devices: 28.8 us -> 32.1 us  [from_y(): lax.ppermute(block, 'tensor', [(x * N_Y + (i + o) % N_Y, x * N_Y + i) for...]
    ppermute x3, starting transfers between devices: 6.94 us -> 3.73 us  [from_x(): lax.ppermute(block, 'tensor', [(i, (i + N_Y) % (2 * N_Y)) for i in range(...]
    dynamic_slice x0 -> x1, local copies, waits for them, and re-layouts: none -> 2.75 us  [shards(): lax.dynamic_index_in_dim(grads, xh, 0, keepdims=False)]
  transfers between devices with their start and end apart: 40 -> 32, of which waited for: 19 -> 16; matrix products, arithmetic and copies ran while one was open for 2% -> 2% of each run, Pallas kernels for 25% -> 18%
where the time goes in v4:
time: 251 us
  waiting for transfers between devices  117 us (47%)
  Pallas kernels  51.6 us (21%)
  starting transfers between devices  48.5 us (19%)
  local copies, waits for them, and re-layouts  17.3 us (7%)
  between operations  14.3 us (6%)
  other arithmetic  2.67 us (1%)
    ppermute x20, waiting for transfers between devices, from_y(): lax.ppermute(block, 'tensor', [(x * N_Y + (i + o) % N_Y, x * N_Y + i) for...  61.9 us
    ppermute x6, waiting for transfers between devices, from_z(): return lax.ppermute(block, 'dp', [((i + o) % N_Z, i) for i in range(N_Z)])  40.4 us
    ppermute x20, starting transfers between devices, from_y(): lax.ppermute(block, 'tensor', [(x * N_Y + (i + o) % N_Y, x * N_Y + i) for...  32.1 us
    pallas_call x6, Pallas kernels, partial_sums(): call(kernel, (steps,), in_specs, out_specs, out_shape, name='partial_sums')  23.8 us
    pallas_call x2, Pallas kernels, weight_terms(): call(kernel, (part // step,), [pl.BlockSpec((step, rows), lambda i, at: (...  19.4 us
    ppermute x3, waiting for transfers between devices, from_x(): lax.ppermute(block, 'tensor', [(i, (i + N_Y) % (2 * N_Y)) for i in range(...  14.2 us
    unnamed x42, local copies, waits for them, and re-layouts  12.3 us
    ppermute x6, starting transfers between devices, from_z(): return lax.ppermute(block, 'dp', [((i + o) % N_Z, i) for i in range(N_Z)])  11.3 us
  transfers between devices with their start and end apart: 32, of which 16 were waited for; matrix products, arithmetic and copies ran while one was open for 2% of the time, Pallas kernels for 18%

profile of v4, /device:TPU:0, one launch (start us, length us, event | category | flops | bytes accessed | tf_op | source)
XLA Modules:
  0.0 250.9 jit_solution(6428470615147177459)
XLA Ops:
  7.2 0.0 all-gather.4.cloned.1.call-start
  7.3 2.7 %constant_dynamic-slice_fusion = (bf16[1,4,128,768]{3,2,1,0:T(8,128)(2,1)}, bf16[4,128,768]{2,1,0:T(8,128)(2,1)}) fusion(bf16[2,4,128,768]{3,2,1,0:T(8,128)(2,1)} %bitcast.38, s32[]{:T(128)S(6)} %select_n.23, s32[]{:T(128)S(6)} %select_n.24), kind=kLoop, calls=%fused_computation.4 | loop fusion | bytes 3145736 | tf_op jit(solution)/shard_map/jit(dynamic_index_in_dim)/dynamic_slice | solution.py:263
  10.0 0.0 all-gather.6.cloned.1.call-start
  10.1 3.2 %collective-permute-start.15 = (bf16[4,128,768]{2,1,0:T(8,128)(2,1)}, bf16[4,128,768]{2,1,0:T(8,128)(2,1)S(1)}, u32[]{:S(2)}, u32[]{:S(2)}) collective-permute-start(bf16[4,128,768]{2,1,0:T(8,128)(2,1)} %get-tuple-element.87), channel_id=1, source_target_pairs={{0,4},{1,5},{2,6},{3,7},{4,0},{5,1},{6,2},{7,3},{8,12},{9,13},{10,... | collective-permute-start | bytes 2359304 | tf_op jit(solution)/shard_map/ppermute | solution.py:46
  13.3 0.1 pad_add_fusion.at_ref
  13.3 2.5 %normalize.1 = (f32[128,128]{1,0:T(8,128)S(1)}, bf16[2048,128]{1,0:T(8,128)(2,1)}, bf16[2048,128]{1,0:T(8,128)(2,1)S(1)}, bf16[2048,128]{1,0:T(8,128)(2,1)S(1)}, bf16[2048,128]{1,0:T(8,128)(2,1)S(1)}) custom-call(s32[2]{0:T(128)S(1)} %pad_add_fusion.at_ref, bf16[128,8192]{1,0:T(8,128)(2,1)S(1)} %bitcast.36, bf16[1,8192]{1,0:T(2,128)(2,1)S(1)} %copy-done.17), custom_call_target="tpu_custom_call" | custom-call | bytes 4194304 | tf_op jit(solution)/shard_map/normalize/pallas_call | solution.py:89
  15.9 0.8 copy-done.18
  16.7 1.9 collective-permute-start.1
  18.6 2.1 collective-permute-start.5
  20.7 18.3 %collective-permute-done.1.refs_12_ = bf16[2048,128]{1,0:T(8,128)(2,1)} collective-permute-done((bf16[2048,128]{1,0:T(8,128)(2,1)S(1)}, bf16[2048,128]{1,0:T(8,128)(2,1)}, u32[]{:S(2)}, u32[]{:S(2)}) %collective-permute-start.1) | collective-permute-done | bytes 524320 | tf_op jit(solution)/shard_map/ppermute | solution.py:34
  39.0 1.9 collective-permute-done.5.refs_4_
  40.9 0.9 copy-done.20
  41.8 1.5 collective-permute-start.4
  43.3 1.8 collective-permute-start
  45.1 2.2 dynamic-slice_bitcast_fusion.refs_12_.refs_14_.refs_8_.refs_10_.refs_4_.refs_6_
  47.3 5.7 %collective-permute-done.4.refs_3_ = bf16[2048,128]{1,0:T(8,128)(2,1)} collective-permute-done((bf16[2048,128]{1,0:T(8,128)(2,1)}, bf16[2048,128]{1,0:T(8,128)(2,1)}, u32[]{:S(2)}, u32[]{:S(2)}) %collective-permute-start.4) | collective-permute-done | bytes 524320 | tf_op jit(solution)/shard_map/ppermute | solution.py:38
  53.1 0.7 collective-permute-done.refs_1_
  53.7 3.4 %collective-permute-start.10 = (bf16[2048,128]{1,0:T(8,128)(2,1)S(1)}, bf16[2048,128]{1,0:T(8,128)(2,1)S(1)}, u32[]{:S(2)}, u32[]{:S(2)}) collective-permute-start(bf16[2048,128]{1,0:T(8,128)(2,1)S(1)} %copy-done.19), channel_id=1, source_target_pairs={{16,0},{24,8},{0,16},{8,24},{17,1},{25,9},{1,17},{9,25},{18,2},{26... | collective-permute-start | bytes 1572872 | tf_op jit(solution)/shard_map/ppermute | solution.py:34
  57.1 1.9 collective-permute-start.6
  59.0 0.4 collective-permute-start.7
  59.4 2.8 %collective-permute-start.2 = (bf16[2048,128]{1,0:T(8,128)(2,1)}, bf16[2048,128]{1,0:T(8,128)(2,1)}, u32[]{:S(2)}, u32[]{:S(2)}) collective-permute-start(bf16[2048,128]{1,0:T(8,128)(2,1)} %collective-permute-done.1.refs_12_), channel_id=1, source_target_pairs={{1,0},{2,1},{3,2},{0,3},{5,4},{6,5},{7,6},{4,7},{9,8},{10,9},{11,1... | collective-permute-start | bytes 1572872 | tf_op jit(solution)/shard_map/ppermute | solution.py:38
  62.2 7.8 %collective-permute-done.10.refs_8_ = bf16[2048,128]{1,0:T(8,128)(2,1)S(1)} collective-permute-done((bf16[2048,128]{1,0:T(8,128)(2,1)S(1)}, bf16[2048,128]{1,0:T(8,128)(2,1)S(1)}, u32[]{:S(2)}, u32[]{:S(2)}) %collective-permute-start.10) | collective-permute-done | bytes 524320 | tf_op jit(solution)/shard_map/ppermute | solution.py:34
  70.1 0.8 copy-done.11
  70.9 3.0 %collective-permute-start.11 = (bf16[2048,128]{1,0:T(8,128)(2,1)S(1)}, bf16[2048,128]{1,0:T(8,128)(2,1)S(1)}, u32[]{:S(2)}, u32[]{:S(2)}) collective-permute-start(bf16[2048,128]{1,0:T(8,128)(2,1)S(1)} %collective-permute-done.10.refs_8_), channel_id=1, source_target_pairs={{1,0},{2,1},{3,2},{0,3},{5,4},{6,5},{7,6},{4,7},{9,8},{10,9},{11,1... | collective-permute-start | bytes 1572872 | tf_op jit(solution)/shard_map/ppermute | solution.py:38
  73.9 0.8 copy-done.9
  74.7 0.6 collective-permute-start.8
  75.3 3.9 %collective-permute-done.2.refs_13_ = bf16[2048,128]{1,0:T(8,128)(2,1)} collective-permute-done((bf16[2048,128]{1,0:T(8,128)(2,1)}, bf16[2048,128]{1,0:T(8,128)(2,1)}, u32[]{:S(2)}, u32[]{:S(2)}) %collective-permute-start.2) | collective-permute-done | bytes 524320 | tf_op jit(solution)/shard_map/ppermute | solution.py:38
  79.2 7.3 %collective-permute-done.11.refs_9_ = bf16[2048,128]{1,0:T(8,128)(2,1)S(1)} collective-permute-done((bf16[2048,128]{1,0:T(8,128)(2,1)S(1)}, bf16[2048,128]{1,0:T(8,128)(2,1)S(1)}, u32[]{:S(2)}, u32[]{:S(2)}) %collective-permute-start.11) | collective-permute-done | bytes 524320 | tf_op jit(solution)/shard_map/ppermute | solution.py:38
  86.5 0.8 copy-done.13
  87.3 3.2 %collective-permute-start.14 = (bf16[2048,128]{1,0:T(8,128)(2,1)}, bf16[2048,128]{1,0:T(8,128)(2,1)}, u32[]{:S(2)}, u32[]{:S(2)}) collective-permute-start(bf16[2048,128]{1,0:T(8,128)(2,1)} %collective-permute-done.2.refs_13_), channel_id=1, source_target_pairs={{1,0},{2,1},{3,2},{0,3},{5,4},{6,5},{7,6},{4,7},{9,8},{10,9},{11,1... | collective-permute-start | bytes 1572872 | tf_op jit(solution)/shard_map/ppermute | solution.py:38
  90.5 10.7 %collective-permute-done.8.refs_15_ = bf16[2048,128]{1,0:T(8,128)(2,1)S(1)} collective-permute-done((bf16[2048,128]{1,0:T(8,128)(2,1)}, bf16[2048,128]{1,0:T(8,128)(2,1)S(1)}, u32[]{:S(2)}, u32[]{:S(2)}) %collective-permute-start.8) | collective-permute-done | bytes 524320 | tf_op jit(solution)/shard_map/ppermute | solution.py:38
  101.2 0.8 copy-done.15
  102.0 3.2 %collective-permute-start.3 = (bf16[2048,128]{1,0:T(8,128)(2,1)}, bf16[2048,128]{1,0:T(8,128)(2,1)}, u32[]{:S(2)}, u32[]{:S(2)}) collective-permute-start(bf16[2048,128]{1,0:T(8,128)(2,1)} %collective-permute-done.refs_1_), channel_id=1, source_target_pairs={{1,0},{2,1},{3,2},{0,3},{5,4},{6,5},{7,6},{4,7},{9,8},{10,9},{11,1... | collective-permute-start | bytes 1572872 | tf_op jit(solution)/shard_map/ppermute | solution.py:38
  105.3 14.2 %collective-permute-done.16.refs_13_.refs_15_.refs_9_.refs_11_.refs_5_.refs_7_ = bf16[2048,768]{1,0:T(8,128)(2,1)S(1)} collective-permute-done((bf16[2048,768]{1,0:T(8,128)(2,1)S(1)}, bf16[2048,768]{1,0:T(8,128)(2,1)S(1)}, u32[]{:S(2)}, u32[]{:S(2)}) %collective-permute-start.16) | collective-permute-done | bytes 3145760 | tf_op jit(solution)/shard_map/ppermute | solution.py:46
  119.5 1.7 copy-done.4
  121.1 1.3 collective-permute-start.20
  122.4 0.0 all-gather.4.cloned.1.call-done.refs_16_.refs_0_.refs_1_.refs_4_.refs_5_.refs_8_.refs_9_
  122.5 1.9 copy-done
  124.4 1.9 copy-done.2
  126.2 1.9 copy-done.5
  128.2 4.9 %partial_sums.6 = (bf16[2,2,128,1024]{3,2,1,0:T(8,128)(2,1)S(1)}, bf16[2,2,128,1024]{3,2,1,0:T(8,128)(2,1)S(1)}) custom-call(s32[2]{0:T(128)S(1)} %pad_add_fusion.at_ref, bf16[4,4,128,768]{3,2,1,0:T(8,128)(2,1)S(1)} %copy-done, bf16[4,4,128,768]{3,2,1,0:T(8,128)(2,1)S(1)} %copy-done, bf16[4,4,128,768]{3,2,1,0:T(8,128)(2,1)S(1)} %bitcast.11, ...), custom_call_target="tpu_custom_call" | custom-call | tf_op jit(solution)/shard_map/partial_sums/pallas_call | solution.py:164
  133.0 2.9 %collective-permute-start.19 = (bf16[2,2,128,1024]{3,2,1,0:T(8,128)(2,1)S(1)}, bf16[2,2,128,1024]{3,2,1,0:T(8,128)(2,1)S(1)}, u32[]{:S(2)}, u32[]{:S(2)}) collective-permute-start(bf16[2,2,128,1024]{3,2,1,0:T(8,128)(2,1)S(1)} %get-tuple-element.65), channel_id=1, source_target_pairs={{1,0},{2,1},{3,2},{0,3},{5,4},{6,5},{7,6},{4,7},{9,8},{10,9},{11,1... | collective-permute-start | bytes 3145736 | tf_op jit(solution)/shard_map/ppermute | solution.py:38
  136.0 9.9 %weight_terms.3 = bf16[2048,768]{1,0:T(8,128)(2,1)S(1)} custom-call(s32[2]{0:T(128)S(1)} %pad_add_fusion.at_ref, bf16[2048,128]{1,0:T(8,128)(2,1)} %get-tuple-element.44.refs_0_, bf16[2048,128]{1,0:T(8,128)(2,1)} %collective-permute-done.refs_1_, bf16[2048,128]{1,0:T(8,128)(2,1)} %collective-permute-done.3.refs_2_, ...), custom_call_target="tpu_custom_call" | custom-call | tf_op jit(solution)/shard_map/weight_terms/pallas_call | solution.py:187
  145.9 0.5 collective-permute-start.17
  146.5 4.9 %partial_sums.8 = (bf16[2,2,128,1024]{3,2,1,0:T(8,128)(2,1)S(1)}, bf16[2,2,128,1024]{3,2,1,0:T(8,128)(2,1)S(1)}) custom-call(s32[2]{0:T(128)S(1)} %pad_add_fusion.at_ref, bf16[4,4,128,768]{3,2,1,0:T(8,128)(2,1)S(1)} %copy-done.1, bf16[4,4,128,768]{3,2,1,0:T(8,128)(2,1)S(1)} %copy-done.1, bf16[4,4,128,768]{3,2,1,0:T(8,128)(2,1)S(1)} %bitcast.23, ...), custom_call_target="tpu_custom_call" | custom-call | tf_op jit(solution)/shard_map/partial_sums/pallas_call | solution.py:164
  151.3 8.0 %collective-permute-done.19.refs_13_.refs_9_ = bf16[2,2,128,1024]{3,2,1,0:T(8,128)(2,1)S(1)} collective-permute-done((bf16[2,2,128,1024]{3,2,1,0:T(8,128)(2,1)S(1)}, bf16[2,2,128,1024]{3,2,1,0:T(8,128)(2,1)S(1)}, u32[]{:S(2)}, u32[]{:S(2)}) %collective-permute-start.19) | collective-permute-done | bytes 1048608 | tf_op jit(solution)/shard_map/ppermute | solution.py:38
  159.3 3.7 %collective-permute-start.23 = (bf16[2,2,128,1024]{3,2,1,0:T(8,128)(2,1)S(1)}, bf16[2,2,128,1024]{3,2,1,0:T(8,128)(2,1)S(1)}, u32[]{:S(2)}, u32[]{:S(2)}) collective-permute-start(bf16[2,2,128,1024]{3,2,1,0:T(8,128)(2,1)S(1)} %get-tuple-element.74), channel_id=1, source_target_pairs={{1,0},{2,1},{3,2},{0,3},{5,4},{6,5},{7,6},{4,7},{9,8},{10,9},{11,1... | collective-permute-start | bytes 3145736 | tf_op jit(solution)/shard_map/ppermute | solution.py:38
  163.0 0.1 collective-permute-done.18.refs_12_.refs_8_
  163.1 3.4 %partial_sums.7 = (bf16[1,2,128,1024]{3,2,1,0:T(8,128)(2,1)S(1)}, bf16[1,2,128,1024]{3,2,1,0:T(8,128)(2,1)S(1)}) custom-call(s32[2]{0:T(128)S(1)} %pad_add_fusion.at_ref, bf16[4,4,128,768]{3,2,1,0:T(8,128)(2,1)S(1)} %copy-done.1, bf16[4,4,128,768]{3,2,1,0:T(8,128)(2,1)S(1)} %copy-done.1, bf16[4,4,128,768]{3,2,1,0:T(8,128)(2,1)S(1)} %bitcast.24, ...), custom_call_target="tpu_custom_call" | custom-call | tf_op jit(solution)/shard_map/partial_sums/pallas_call | solution.py:164
  166.5 19.4 %collective-permute-done.23.refs_13_.refs_9_ = bf16[2,2,128,1024]{3,2,1,0:T(8,128)(2,1)S(1)} collective-permute-done((bf16[2,2,128,1024]{3,2,1,0:T(8,128)(2,1)S(1)}, bf16[2,2,128,1024]{3,2,1,0:T(8,128)(2,1)S(1)}, u32[]{:S(2)}, u32[]{:S(2)}) %collective-permute-start.23) | collective-permute-done | bytes 1048608 | tf_op jit(solution)/shard_map/ppermute | solution.py:38
  185.9 3.7 %collective-permute-start.24 = (bf16[1,2,128,1024]{3,2,1,0:T(8,128)(2,1)S(1)}, bf16[1,2,128,1024]{3,2,1,0:T(8,128)(2,1)S(1)}, u32[]{:S(2)}, u32[]{:S(2)}) collective-permute-start(bf16[1,2,128,1024]{3,2,1,0:T(8,128)(2,1)S(1)} %get-tuple-element.75), channel_id=1, source_target_pairs={{1,0},{2,1},{3,2},{0,3},{5,4},{6,5},{7,6},{4,7},{9,8},{10,9},{11,1... | collective-permute-start | bytes 1572872 | tf_op jit(solution)/shard_map/ppermute | solution.py:38
  189.6 9.6 %weight_terms.2 = bf16[2048,768]{1,0:T(8,128)(2,1)S(1)} custom-call(s32[2]{0:T(128)S(1)} %pad_add_fusion.at_ref, bf16[2048,128]{1,0:T(8,128)(2,1)} %get-tuple-element.44.refs_0_, bf16[2048,128]{1,0:T(8,128)(2,1)} %collective-permute-done.refs_1_, bf16[2048,128]{1,0:T(8,128)(2,1)} %collective-permute-done.3.refs_2_, ...), custom_call_target="tpu_custom_call" | custom-call | tf_op jit(solution)/shard_map/weight_terms/pallas_call | solution.py:187
  199.1 3.4 %partial_sums.10 = (bf16[1,2,128,1024]{3,2,1,0:T(8,128)(2,1)S(1)}, bf16[1,2,128,1024]{3,2,1,0:T(8,128)(2,1)S(1)}) custom-call(s32[2]{0:T(128)S(1)} %pad_add_fusion.at_ref, bf16[4,4,128,768]{3,2,1,0:T(8,128)(2,1)S(1)} %copy-done.1, bf16[4,4,128,768]{3,2,1,0:T(8,128)(2,1)S(1)} %copy-done.1, bf16[4,4,128,768]{3,2,1,0:T(8,128)(2,1)S(1)} %bitcast.28, ...), custom_call_target="tpu_custom_call" | custom-call | tf_op jit(solution)/shard_map/partial_sums/pallas_call | solution.py:164
  202.6 3.3 %collective-permute-start.28 = (bf16[1,2,128,1024]{3,2,1,0:T(8,128)(2,1)S(1)}, bf16[1,2,128,1024]{3,2,1,0:T(8,128)(2,1)S(1)}, u32[]{:S(2)}, u32[]{:S(2)}) collective-permute-start(bf16[1,2,128,1024]{3,2,1,0:T(8,128)(2,1)S(1)} %get-tuple-element.83), channel_id=1, source_target_pairs={{1,0},{2,1},{3,2},{0,3},{5,4},{6,5},{7,6},{4,7},{9,8},{10,9},{11,1... | collective-permute-start | bytes 1572872 | tf_op jit(solution)/shard_map/ppermute | solution.py:38
  205.9 3.6 %partial_sums.9 = (bf16[2,128,1024]{2,1,0:T(8,128)(2,1)S(1)}, bf16[2,128,1024]{2,1,0:T(8,128)(2,1)S(1)}) custom-call(s32[2]{0:T(128)S(1)} %pad_add_fusion.at_ref, bf16[4,4,128,768]{3,2,1,0:T(8,128)(2,1)S(1)} %copy-done.1, bf16[4,4,128,768]{3,2,1,0:T(8,128)(2,1)S(1)} %copy-done.1, bf16[4,4,128,768]{3,2,1,0:T(8,128)(2,1)S(1)} %bitcast.32, ...), custom_call_target="tpu_custom_call" | custom-call | tf_op jit(solution)/shard_map/partial_sums/pallas_call | solution.py:164
  209.5 3.9 %collective-permute-start.25 = (bf16[2,128,1024]{2,1,0:T(8,128)(2,1)S(1)}, bf16[2,128,1024]{2,1,0:T(8,128)(2,1)S(1)}, u32[]{:S(2)}, u32[]{:S(2)}) collective-permute-start(bf16[2,128,1024]{2,1,0:T(8,128)(2,1)S(1)} %get-tuple-element.76), channel_id=1, source_target_pairs={{8,0},{16,8},{24,16},{0,24},{9,1},{17,9},{25,17},{1,25},{10,2},{18... | collective-permute-start | bytes 1572872 | tf_op jit(solution)/shard_map/ppermute | solution.py:34
  213.4 2.8 %collective-permute-done.28.refs_11_ = bf16[1,2,128,1024]{3,2,1,0:T(8,128)(2,1)S(1)} collective-permute-done((bf16[1,2,128,1024]{3,2,1,0:T(8,128)(2,1)S(1)}, bf16[1,2,128,1024]{3,2,1,0:T(8,128)(2,1)S(1)}, u32[]{:S(2)}, u32[]{:S(2)}) %collective-permute-start.28) | collective-permute-done | bytes 524320 | tf_op jit(solution)/shard_map/ppermute | solution.py:38
  216.2 3.4 %collective-permute-done.27.refs_10_ = bf16[1,2,128,1024]{3,2,1,0:T(8,128)(2,1)S(1)} collective-permute-done((bf16[1,2,128,1024]{3,2,1,0:T(8,128)(2,1)S(1)}, bf16[1,2,128,1024]{3,2,1,0:T(8,128)(2,1)S(1)}, u32[]{:S(2)}, u32[]{:S(2)}) %collective-permute-start.27) | collective-permute-done | bytes 524320 | tf_op jit(solution)/shard_map/ppermute | solution.py:38
  219.6 3.6 %partial_sums.11 = (bf16[2,128,1024]{2,1,0:T(8,128)(2,1)S(1)}, bf16[2,128,1024]{2,1,0:T(8,128)(2,1)S(1)}) custom-call(s32[2]{0:T(128)S(1)} %pad_add_fusion.at_ref, bf16[4,4,128,768]{3,2,1,0:T(8,128)(2,1)S(1)} %copy-done.1, bf16[4,4,128,768]{3,2,1,0:T(8,128)(2,1)S(1)} %copy-done.1, bf16[4,4,128,768]{3,2,1,0:T(8,128)(2,1)S(1)} %bitcast.34, ...), custom_call_target="tpu_custom_call" | custom-call | tf_op jit(solution)/shard_map/partial_sums/pallas_call | solution.py:164
  223.2 0.1 collective-permute-start.29
  223.3 11.3 %collective-permute-done.25.refs_1_ = bf16[2,128,1024]{2,1,0:T(8,128)(2,1)S(1)} collective-permute-done((bf16[2,128,1024]{2,1,0:T(8,128)(2,1)S(1)}, bf16[2,128,1024]{2,1,0:T(8,128)(2,1)S(1)}, u32[]{:S(2)}, u32[]{:S(2)}) %collective-permute-start.25) | collective-permute-done | bytes 524320 | tf_op jit(solution)/shard_map/ppermute | solution.py:34
  234.6 2.6 %fusion = bf16[1,2048,768]{2,1,0:T(8,128)(2,1)} fusion(bf16[2048,768]{1,0:T(8,128)(2,1)S(1)} %collective-permute-done.17, bf16[2048,768]{1,0:T(8,128)(2,1)S(1)} %weight_terms.2), kind=kLoop, calls=%fused_computation.1 | loop fusion | flops 6291456 | bytes 9437184 | tf_op jit(solution)/shard_map/broadcast_in_dim | solution.py:317
  237.2 1.1 collective-permute-done.29.refs_3_
  238.3 5.8 %finish.1 = bf16[1,128,8192]{2,1,0:T(8,128)(2,1)} custom-call(s32[2]{0:T(128)S(1)} %pad_add_fusion.at_ref, f32[128,128]{1,0:T(8,128)S(1)} %get-tuple-element.79.r_ref, bf16[1,8192]{1,0:T(2,128)(2,1)S(1)} %copy-done.17, bf16[128,8192]{1,0:T(8,128)(2,1)S(1)} %bitcast.37, bf16[1,128,8192]{2,1,0:T(8,128)(2,1)} %collective-permute-done.20.u_ref, ...), custom_call_target="tpu_custom_call" | custom-call | tf_op jit(solution)/shard_map/finish/pallas_call | solution.py:229
  (58 shorter events, 0.2 us)
Async XLA Ops:
  7.2 6.2 %copy-start.17 = (bf16[1,8192]{1,0:T(2,128)(2,1)S(1)}, bf16[1,8192]{1,0:T(2,128)(2,1)}, u32[]{:S(2)}) copy-start(bf16[1,8192]{1,0:T(2,128)(2,1)} %g_ref.3) | copy-start | bytes 49156
  7.2 6.2 %copy-start.7 = (bf16[1,128,8192]{2,1,0:T(8,128)(2,1)S(1)}, bf16[1,128,8192]{2,1,0:T(8,128)(2,1)}, u32[]{:S(2)}) copy-start(bf16[1,128,8192]{2,1,0:T(8,128)(2,1)} %param.5) | copy-start | bytes 6291460
  7.2 115.2 %all-gather.4.cloned.1.call-start = ((), (), s32[]{:S(2)}) async-start(), calls=%async_computation | async-start | bytes 3932160 | tf_op jit(solution)/shard_map/all_gather | solution.py:263
  10.0 112.4 %all-gather.6.cloned.1.call-start = ((), (), s32[]{:S(2)}) async-start(), calls=%async_computation.1 | async-start | bytes 3932160 | tf_op jit(solution)/shard_map/all_gather | solution.py:271
  10.1 30.8 %collective-permute-start.15 = (bf16[4,128,768]{2,1,0:T(8,128)(2,1)}, bf16[4,128,768]{2,1,0:T(8,128)(2,1)S(1)}, u32[]{:S(2)}, u32[]{:S(2)}) collective-permute-start(bf16[4,128,768]{2,1,0:T(8,128)(2,1)} %get-tuple-element.87), channel_id=1, source_target_pairs={{0,4},{1,5},{2,6},{3,7},{4,0},{5,1},{6,2},{7,3},{8,12},{9,13},{10,... | collective-permute-start | bytes 2359304 | tf_op jit(solution)/shard_map/ppermute | solution.py:46
  15.9 0.8 copy-start.18
  16.7 22.3 %collective-permute-start.1 = (bf16[2048,128]{1,0:T(8,128)(2,1)S(1)}, bf16[2048,128]{1,0:T(8,128)(2,1)}, u32[]{:S(2)}, u32[]{:S(2)}) collective-permute-start(bf16[2048,128]{1,0:T(8,128)(2,1)S(1)} %get-tuple-element.45), channel_id=1, source_target_pairs={{24,0},{0,8},{8,16},{16,24},{25,1},{1,9},{9,17},{17,25},{26,2},{2,... | collective-permute-start | bytes 1572872 | tf_op jit(solution)/shard_map/ppermute | solution.py:34
  18.6 22.3 %collective-permute-start.5 = (bf16[2048,128]{1,0:T(8,128)(2,1)S(1)}, bf16[2048,128]{1,0:T(8,128)(2,1)}, u32[]{:S(2)}, u32[]{:S(2)}) collective-permute-start(bf16[2048,128]{1,0:T(8,128)(2,1)S(1)} %get-tuple-element.48), channel_id=1, source_target_pairs={{8,0},{16,8},{24,16},{0,24},{9,1},{17,9},{25,17},{1,25},{10,2},{18... | collective-permute-start | bytes 1572872 | tf_op jit(solution)/shard_map/ppermute | solution.py:34
  40.9 0.9 copy-start.20
  41.8 11.2 %collective-permute-start.4 = (bf16[2048,128]{1,0:T(8,128)(2,1)}, bf16[2048,128]{1,0:T(8,128)(2,1)}, u32[]{:S(2)}, u32[]{:S(2)}) collective-permute-start(bf16[2048,128]{1,0:T(8,128)(2,1)} %get-tuple-element.44.refs_0_), channel_id=1, source_target_pairs={{3,0},{0,1},{1,2},{2,3},{7,4},{4,5},{5,6},{6,7},{11,8},{8,9},{9,10... | collective-permute-start | bytes 1572872 | tf_op jit(solution)/shard_map/ppermute | solution.py:38
  43.3 10.4 %collective-permute-start = (bf16[2048,128]{1,0:T(8,128)(2,1)}, bf16[2048,128]{1,0:T(8,128)(2,1)}, u32[]{:S(2)}, u32[]{:S(2)}) collective-permute-start(bf16[2048,128]{1,0:T(8,128)(2,1)} %get-tuple-element.44.refs_0_), channel_id=1, source_target_pairs={{1,0},{2,1},{3,2},{0,3},{5,4},{6,5},{7,6},{4,7},{9,8},{10,9},{11,1... | collective-permute-start | bytes 1572872 | tf_op jit(solution)/shard_map/ppermute | solution.py:38
  45.1 8.6 %copy-start.19 = (bf16[2048,128]{1,0:T(8,128)(2,1)S(1)}, bf16[2048,128]{1,0:T(8,128)(2,1)}, u32[]{:S(2)}) copy-start(bf16[2048,128]{1,0:T(8,128)(2,1)} %copy-done.18) | copy-start | bytes 1572868
  53.7 65.7 %collective-permute-start.16 = (bf16[2048,768]{1,0:T(8,128)(2,1)S(1)}, bf16[2048,768]{1,0:T(8,128)(2,1)S(1)}, u32[]{:S(2)}, u32[]{:S(2)}) collective-permute-start(bf16[2048,768]{1,0:T(8,128)(2,1)S(1)} %dynamic-slice_bitcast_fusion.refs_12_.refs_14_.refs_8_.refs_10_.refs_4_.refs_6_), channel_id=1, source_target_pairs={{0,4},{1,5},{2,6},{3,7},{4,0},{5,1},{6,2},{7,3},{8,12},{9,13},{10,... | collective-permute-start | bytes 9437192 | tf_op jit(solution)/shard_map/ppermute | solution.py:46
  53.7 16.3 %collective-permute-start.10 = (bf16[2048,128]{1,0:T(8,128)(2,1)S(1)}, bf16[2048,128]{1,0:T(8,128)(2,1)S(1)}, u32[]{:S(2)}, u32[]{:S(2)}) collective-permute-start(bf16[2048,128]{1,0:T(8,128)(2,1)S(1)} %copy-done.19), channel_id=1, source_target_pairs={{16,0},{24,8},{0,16},{8,24},{17,1},{25,9},{1,17},{9,25},{18,2},{26... | collective-permute-start | bytes 1572872 | tf_op jit(solution)/shard_map/ppermute | solution.py:34
  57.1 13.0 %collective-permute-start.6 = (bf16[2048,128]{1,0:T(8,128)(2,1)}, bf16[2048,128]{1,0:T(8,128)(2,1)S(1)}, u32[]{:S(2)}, u32[]{:S(2)}) collective-permute-start(bf16[2048,128]{1,0:T(8,128)(2,1)} %collective-permute-done.5.refs_4_), channel_id=1, source_target_pairs={{1,0},{2,1},{3,2},{0,3},{5,4},{6,5},{7,6},{4,7},{9,8},{10,9},{11,1... | collective-permute-start | bytes 1572872 | tf_op jit(solution)/shard_map/ppermute | solution.py:38
  59.0 14.9 %collective-permute-start.7 = (bf16[2048,128]{1,0:T(8,128)(2,1)}, bf16[2048,128]{1,0:T(8,128)(2,1)}, u32[]{:S(2)}, u32[]{:S(2)}) collective-permute-start(bf16[2048,128]{1,0:T(8,128)(2,1)} %collective-permute-done.5.refs_4_), channel_id=1, source_target_pairs={{3,0},{0,1},{1,2},{2,3},{7,4},{4,5},{5,6},{6,7},{11,8},{8,9},{9,10... | collective-permute-start | bytes 1572872 | tf_op jit(solution)/shard_map/ppermute | solution.py:38
  59.4 19.8 %collective-permute-start.2 = (bf16[2048,128]{1,0:T(8,128)(2,1)}, bf16[2048,128]{1,0:T(8,128)(2,1)}, u32[]{:S(2)}, u32[]{:S(2)}) collective-permute-start(bf16[2048,128]{1,0:T(8,128)(2,1)} %collective-permute-done.1.refs_12_), channel_id=1, source_target_pairs={{1,0},{2,1},{3,2},{0,3},{5,4},{6,5},{7,6},{4,7},{9,8},{10,9},{11,1... | collective-permute-start | bytes 1572872 | tf_op jit(solution)/shard_map/ppermute | solution.py:38
  70.0 0.8 copy-start.11
  70.9 15.6 %collective-permute-start.11 = (bf16[2048,128]{1,0:T(8,128)(2,1)S(1)}, bf16[2048,128]{1,0:T(8,128)(2,1)S(1)}, u32[]{:S(2)}, u32[]{:S(2)}) collective-permute-start(bf16[2048,128]{1,0:T(8,128)(2,1)S(1)} %collective-permute-done.10.refs_8_), channel_id=1, source_target_pairs={{1,0},{2,1},{3,2},{0,3},{5,4},{6,5},{7,6},{4,7},{9,8},{10,9},{11,1... | collective-permute-start | bytes 1572872 | tf_op jit(solution)/shard_map/ppermute | solution.py:38
  73.9 16.6 %collective-permute-start.12 = (bf16[2048,128]{1,0:T(8,128)(2,1)S(1)}, bf16[2048,128]{1,0:T(8,128)(2,1)}, u32[]{:S(2)}, u32[]{:S(2)}) collective-permute-start(bf16[2048,128]{1,0:T(8,128)(2,1)S(1)} %collective-permute-done.10.refs_8_), channel_id=1, source_target_pairs={{3,0},{0,1},{1,2},{2,3},{7,4},{4,5},{5,6},{6,7},{11,8},{8,9},{9,10... | collective-permute-start | bytes 1572872 | tf_op jit(solution)/shard_map/ppermute | solution.py:38
  73.9 0.8 copy-start.9
  74.7 26.5 %collective-permute-start.8 = (bf16[2048,128]{1,0:T(8,128)(2,1)}, bf16[2048,128]{1,0:T(8,128)(2,1)S(1)}, u32[]{:S(2)}, u32[]{:S(2)}) collective-permute-start(bf16[2048,128]{1,0:T(8,128)(2,1)} %collective-permute-done.1.refs_12_), channel_id=1, source_target_pairs={{3,0},{0,1},{1,2},{2,3},{7,4},{4,5},{5,6},{6,7},{11,8},{8,9},{9,10... | collective-permute-start | bytes 1572872 | tf_op jit(solution)/shard_map/ppermute | solution.py:38
  86.5 0.8 copy-start.13
  87.3 45.7 %collective-permute-start.14 = (bf16[2048,128]{1,0:T(8,128)(2,1)}, bf16[2048,128]{1,0:T(8,128)(2,1)}, u32[]{:S(2)}, u32[]{:S(2)}) collective-permute-start(bf16[2048,128]{1,0:T(8,128)(2,1)} %collective-permute-done.2.refs_13_), channel_id=1, source_target_pairs={{1,0},{2,1},{3,2},{0,3},{5,4},{6,5},{7,6},{4,7},{9,8},{10,9},{11,1... | collective-permute-start | bytes 1572872 | tf_op jit(solution)/shard_map/ppermute | solution.py:38
  90.5 45.4 %collective-permute-start.13 = (bf16[2048,128]{1,0:T(8,128)(2,1)}, bf16[2048,128]{1,0:T(8,128)(2,1)}, u32[]{:S(2)}, u32[]{:S(2)}) collective-permute-start(bf16[2048,128]{1,0:T(8,128)(2,1)} %collective-permute-done.12.refs_11_), channel_id=1, source_target_pairs={{3,0},{0,1},{1,2},{2,3},{7,4},{4,5},{5,6},{6,7},{11,8},{8,9},{9,10... | collective-permute-start | bytes 1572872 | tf_op jit(solution)/shard_map/ppermute | solution.py:38
  101.2 0.8 copy-start.15
  102.0 33.9 %collective-permute-start.9 = (bf16[2048,128]{1,0:T(8,128)(2,1)}, bf16[2048,128]{1,0:T(8,128)(2,1)}, u32[]{:S(2)}, u32[]{:S(2)}) collective-permute-start(bf16[2048,128]{1,0:T(8,128)(2,1)} %collective-permute-done.7.refs_7_), channel_id=1, source_target_pairs={{3,0},{0,1},{1,2},{2,3},{7,4},{4,5},{5,6},{6,7},{11,8},{8,9},{9,10... | collective-permute-start | bytes 1572872 | tf_op jit(solution)/shard_map/ppermute | solution.py:38
  102.0 33.9 %collective-permute-start.3 = (bf16[2048,128]{1,0:T(8,128)(2,1)}, bf16[2048,128]{1,0:T(8,128)(2,1)}, u32[]{:S(2)}, u32[]{:S(2)}) collective-permute-start(bf16[2048,128]{1,0:T(8,128)(2,1)} %collective-permute-done.refs_1_), channel_id=1, source_target_pairs={{1,0},{2,1},{3,2},{0,3},{5,4},{6,5},{7,6},{4,7},{9,8},{10,9},{11,1... | collective-permute-start | bytes 1572872 | tf_op jit(solution)/shard_map/ppermute | solution.py:38
  119.5 1.7 copy-start.4
  121.1 42.0 %collective-permute-start.20 = (bf16[1,128,8192]{2,1,0:T(8,128)(2,1)}, bf16[1,128,8192]{2,1,0:T(8,128)(2,1)}, u32[]{:S(2)}, u32[]{:S(2)}) collective-permute-start(bf16[1,128,8192]{2,1,0:T(8,128)(2,1)} %param.9), channel_id=1, source_target_pairs={{32,0},{64,32},{96,64},{33,1},{65,33},{97,65},{34,2},{66,34},{98,6... | collective-permute-start | bytes 6291464 | tf_op jit(solution)/shard_map/ppermute | solution.py:274
  122.5 1.9 copy-start
  124.3 1.9 copy-start.2
  126.2 1.9 copy-start.5
  128.1 7.8 %copy-start.3 = (bf16[16,128,768]{2,1,0:T(8,128)(2,1)S(1)}, bf16[16,128,768]{2,1,0:T(8,128)(2,1)}, u32[]{:S(2)}) copy-start(bf16[16,128,768]{2,1,0:T(8,128)(2,1)} %all-gather.6.cloned.1.call-done) | copy-start | bytes 9437188
  128.1 7.9 %copy-start.10 = (bf16[2048,128]{1,0:T(8,128)(2,1)S(1)}, bf16[2048,128]{1,0:T(8,128)(2,1)}, u32[]{:S(2)}) copy-start(bf16[2048,128]{1,0:T(8,128)(2,1)} %copy-done.9) | copy-start | bytes 1572868
  128.1 7.9 %copy-start.12 = (bf16[2048,128]{1,0:T(8,128)(2,1)S(1)}, bf16[2048,128]{1,0:T(8,128)(2,1)}, u32[]{:S(2)}) copy-start(bf16[2048,128]{1,0:T(8,128)(2,1)} %copy-done.11) | copy-start | bytes 1572868
  128.1 7.9 %copy-start.14 = (bf16[2048,128]{1,0:T(8,128)(2,1)S(1)}, bf16[2048,128]{1,0:T(8,128)(2,1)}, u32[]{:S(2)}) copy-start(bf16[2048,128]{1,0:T(8,128)(2,1)} %copy-done.13) | copy-start | bytes 1572868
  128.1 7.9 %copy-start.16 = (bf16[2048,128]{1,0:T(8,128)(2,1)S(1)}, bf16[2048,128]{1,0:T(8,128)(2,1)}, u32[]{:S(2)}) copy-start(bf16[2048,128]{1,0:T(8,128)(2,1)} %copy-done.15) | copy-start | bytes 1572868
  133.0 26.3 %collective-permute-start.19 = (bf16[2,2,128,1024]{3,2,1,0:T(8,128)(2,1)S(1)}, bf16[2,2,128,1024]{3,2,1,0:T(8,128)(2,1)S(1)}, u32[]{:S(2)}, u32[]{:S(2)}) collective-permute-start(bf16[2,2,128,1024]{3,2,1,0:T(8,128)(2,1)S(1)} %get-tuple-element.65), channel_id=1, source_target_pairs={{1,0},{2,1},{3,2},{0,3},{5,4},{6,5},{7,6},{4,7},{9,8},{10,9},{11,1... | collective-permute-start | bytes 3145736 | tf_op jit(solution)/shard_map/ppermute | solution.py:38
  135.9 10.5 %copy-start.1 = (bf16[4,4,128,768]{3,2,1,0:T(8,128)(2,1)S(1)}, bf16[4,4,128,768]{3,2,1,0:T(8,128)(2,1)}, u32[]{:S(2)}) copy-start(bf16[4,4,128,768]{3,2,1,0:T(8,128)(2,1)} %all-gather.4.cloned.1.call-done.refs_16_.refs_0_.refs_1_.refs_4_.refs_5_.refs_8_.refs_9_) | copy-start | bytes 9437188
  135.9 10.5 %copy-start.6 = (bf16[2048,768]{1,0:T(8,128)(2,1)S(1)}, bf16[2048,768]{1,0:T(8,128)(2,1)}, u32[]{:S(2)}) copy-start(bf16[2048,768]{1,0:T(8,128)(2,1)} %copy-done.4) | copy-start | bytes 9437188
  135.9 27.1 %collective-permute-start.18 = (bf16[2,2,128,1024]{3,2,1,0:T(8,128)(2,1)S(1)}, bf16[2,2,128,1024]{3,2,1,0:T(8,128)(2,1)S(1)}, u32[]{:S(2)}, u32[]{:S(2)}) collective-permute-start(bf16[2,2,128,1024]{3,2,1,0:T(8,128)(2,1)S(1)} %get-tuple-element.62), channel_id=1, source_target_pairs={{3,0},{0,1},{1,2},{2,3},{7,4},{4,5},{5,6},{6,7},{11,8},{8,9},{9,10... | collective-permute-start | bytes 3145736 | tf_op jit(solution)/shard_map/ppermute | solution.py:38
  145.9 88.7 %collective-permute-start.17 = (bf16[2048,768]{1,0:T(8,128)(2,1)S(1)}, bf16[2048,768]{1,0:T(8,128)(2,1)S(1)}, u32[]{:S(2)}, u32[]{:S(2)}) collective-permute-start(bf16[2048,768]{1,0:T(8,128)(2,1)S(1)} %weight_terms.3), channel_id=1, source_target_pairs={{0,4},{1,5},{2,6},{3,7},{4,0},{5,1},{6,2},{7,3},{8,12},{9,13},{10,... | collective-permute-start | bytes 9437192 | tf_op jit(solution)/shard_map/ppermute | solution.py:46
  159.3 26.6 %collective-permute-start.23 = (bf16[2,2,128,1024]{3,2,1,0:T(8,128)(2,1)S(1)}, bf16[2,2,128,1024]{3,2,1,0:T(8,128)(2,1)S(1)}, u32[]{:S(2)}, u32[]{:S(2)}) collective-permute-start(bf16[2,2,128,1024]{3,2,1,0:T(8,128)(2,1)S(1)} %get-tuple-element.74), channel_id=1, source_target_pairs={{1,0},{2,1},{3,2},{0,3},{5,4},{6,5},{7,6},{4,7},{9,8},{10,9},{11,1... | collective-permute-start | bytes 3145736 | tf_op jit(solution)/shard_map/ppermute | solution.py:38
  163.1 26.5 %collective-permute-start.21 = (bf16[2,2,128,1024]{3,2,1,0:T(8,128)(2,1)S(1)}, bf16[2,2,128,1024]{3,2,1,0:T(8,128)(2,1)S(1)}, u32[]{:S(2)}, u32[]{:S(2)}) collective-permute-start(bf16[2,2,128,1024]{3,2,1,0:T(8,128)(2,1)S(1)} %get-tuple-element.70), channel_id=1, source_target_pairs={{3,0},{0,1},{1,2},{2,3},{7,4},{4,5},{5,6},{6,7},{11,8},{8,9},{9,10... | collective-permute-start | bytes 3145736 | tf_op jit(solution)/shard_map/ppermute | solution.py:38
  185.9 16.7 %collective-permute-start.24 = (bf16[1,2,128,1024]{3,2,1,0:T(8,128)(2,1)S(1)}, bf16[1,2,128,1024]{3,2,1,0:T(8,128)(2,1)S(1)}, u32[]{:S(2)}, u32[]{:S(2)}) collective-permute-start(bf16[1,2,128,1024]{3,2,1,0:T(8,128)(2,1)S(1)} %get-tuple-element.75), channel_id=1, source_target_pairs={{1,0},{2,1},{3,2},{0,3},{5,4},{6,5},{7,6},{4,7},{9,8},{10,9},{11,1... | collective-permute-start | bytes 1572872 | tf_op jit(solution)/shard_map/ppermute | solution.py:38
  189.6 16.3 %collective-permute-start.22 = (bf16[1,2,128,1024]{3,2,1,0:T(8,128)(2,1)S(1)}, bf16[1,2,128,1024]{3,2,1,0:T(8,128)(2,1)S(1)}, u32[]{:S(2)}, u32[]{:S(2)}) collective-permute-start(bf16[1,2,128,1024]{3,2,1,0:T(8,128)(2,1)S(1)} %get-tuple-element.71), channel_id=1, source_target_pairs={{3,0},{0,1},{1,2},{2,3},{7,4},{4,5},{5,6},{6,7},{11,8},{8,9},{9,10... | collective-permute-start | bytes 1572872 | tf_op jit(solution)/shard_map/ppermute | solution.py:38
  202.6 13.6 %collective-permute-start.28 = (bf16[1,2,128,1024]{3,2,1,0:T(8,128)(2,1)S(1)}, bf16[1,2,128,1024]{3,2,1,0:T(8,128)(2,1)S(1)}, u32[]{:S(2)}, u32[]{:S(2)}) collective-permute-start(bf16[1,2,128,1024]{3,2,1,0:T(8,128)(2,1)S(1)} %get-tuple-element.83), channel_id=1, source_target_pairs={{1,0},{2,1},{3,2},{0,3},{5,4},{6,5},{7,6},{4,7},{9,8},{10,9},{11,1... | collective-permute-start | bytes 1572872 | tf_op jit(solution)/shard_map/ppermute | solution.py:38
  205.9 13.7 %collective-permute-start.27 = (bf16[1,2,128,1024]{3,2,1,0:T(8,128)(2,1)S(1)}, bf16[1,2,128,1024]{3,2,1,0:T(8,128)(2,1)S(1)}, u32[]{:S(2)}, u32[]{:S(2)}) collective-permute-start(bf16[1,2,128,1024]{3,2,1,0:T(8,128)(2,1)S(1)} %get-tuple-element.81), channel_id=1, source_target_pairs={{3,0},{0,1},{1,2},{2,3},{7,4},{4,5},{5,6},{6,7},{11,8},{8,9},{9,10... | collective-permute-start | bytes 1572872 | tf_op jit(solution)/shard_map/ppermute | solution.py:38
  209.5 25.1 %collective-permute-start.25 = (bf16[2,128,1024]{2,1,0:T(8,128)(2,1)S(1)}, bf16[2,128,1024]{2,1,0:T(8,128)(2,1)S(1)}, u32[]{:S(2)}, u32[]{:S(2)}) collective-permute-start(bf16[2,128,1024]{2,1,0:T(8,128)(2,1)S(1)} %get-tuple-element.76), channel_id=1, source_target_pairs={{8,0},{16,8},{24,16},{0,24},{9,1},{17,9},{25,17},{1,25},{10,2},{18... | collective-permute-start | bytes 1572872 | tf_op jit(solution)/shard_map/ppermute | solution.py:34
  213.4 21.2 %collective-permute-start.26 = (bf16[2,128,1024]{2,1,0:T(8,128)(2,1)S(1)}, bf16[2,128,1024]{2,1,0:T(8,128)(2,1)S(1)}, u32[]{:S(2)}, u32[]{:S(2)}) collective-permute-start(bf16[2,128,1024]{2,1,0:T(8,128)(2,1)S(1)} %get-tuple-element.77), channel_id=1, source_target_pairs={{16,0},{24,8},{0,16},{8,24},{17,1},{25,9},{1,17},{9,25},{18,2},{26... | collective-permute-start | bytes 1572872 | tf_op jit(solution)/shard_map/ppermute | solution.py:34
  223.2 15.1 %copy-start.8 = (bf16[1,128,8192]{2,1,0:T(8,128)(2,1)S(1)}, bf16[1,128,8192]{2,1,0:T(8,128)(2,1)}, u32[]{:S(2)}) copy-start(bf16[1,128,8192]{2,1,0:T(8,128)(2,1)} %param.5) | copy-start | bytes 6291460
  223.2 15.1 %collective-permute-start.29 = (bf16[2,128,1024]{2,1,0:T(8,128)(2,1)S(1)}, bf16[2,128,1024]{2,1,0:T(8,128)(2,1)S(1)}, u32[]{:S(2)}, u32[]{:S(2)}) collective-permute-start(bf16[2,128,1024]{2,1,0:T(8,128)(2,1)S(1)} %get-tuple-element.85), channel_id=1, source_target_pairs={{24,0},{0,8},{8,16},{16,24},{25,1},{1,9},{9,17},{17,25},{26,2},{2,... | collective-permute-start | bytes 1572872 | tf_op jit(solution)/shard_map/ppermute | solution.py:34
Sparse Core Ops, SparseCore 0:
  10.3 58.0 all-gather.3
  70.0 40.1 all-gather.5

commit v5 on v4

--- a/solution.py
+++ b/solution.py
@@ -16,14 +16,17 @@
 
 class Chains:
     def __init__(self):
-        self.sent = {}
-
-    def __call__(self, key, block, send, depth=1):
-        sent = self.sent.setdefault(key, [])
-        if len(sent) >= depth:
-            block, _ = lax.optimization_barrier((block, sent[-depth]))
-        sent.append(send(block))
-        return sent[-1]
+        self.last = {}
+
+    def __call__(self, key, block, send):
+        if key in self.last:
+            block = after(block, self.last[key])
+        return self.hold(key, send(block))
+
+    def hold(self, *keys_and_sent):
+        for key in keys_and_sent[:-1]:
+            self.last[key] = keys_and_sent[-1]
+        return keys_and_sent[-1]
 
 
 def after(block, *others):
@@ -84,7 +87,7 @@
             at = pl.multiple_of(lax.rem(at_ref[0] + d, N_Z) * part, part)
             x = h_ref[:, pl.ds(at, part)].astype(F32)
             g = g_ref[:, pl.ds(at, part)].astype(F32)
-            out_refs[d][...] = ((x * r) * g).T.astype(BF16)
+            out_refs[d][0] = ((x * r) * g).T.astype(BF16)
 
     return call(
         kernel,
@@ -92,14 +95,14 @@
         [WHOLE, WHOLE],
         [WHOLE] * (1 + N_Z),
         [jax.ShapeDtypeStruct((rows, 128), F32)]
-        + [jax.ShapeDtypeStruct((part, rows), BF16)] * N_Z,
+        + [jax.ShapeDtypeStruct((1, part, rows), BF16)] * N_Z,
         bytes_accessed=4 * rows * width,
         name="normalize",
     )(place, hidden, gain)
 
 
 def partial_sums(place, seqs, groups, g_own, g_par, w_own, w_par, extras=(), per_sequence=False):
-    _, _, rows, cols = g_own.shape
+    _, _, rows, cols = g_own[0][0].shape
     part = w_own.shape[0]
     half = part // 2
     step = 256
@@ -122,31 +125,30 @@
                 total = dot_nt(left, w_refs[s][...]) + dot_nt(right, w_refs[s + 1][...])
                 total = total.reshape(count, rows, step)
                 for e, i in adds:
-                    total = total + e_refs[e][i].astype(F32)
+                    total = total + e_refs[e][i * count : (i + 1) * count].astype(F32)
                 if per_sequence:
                     for o in range(count):
                         outs[o][side] = total[o].astype(BF16)
                 else:
-                    outs[k][j] = total.astype(BF16)
-
-    def tokens_of(o, q):
+                    outs[k][j * count : (j + 1) * count] = total.astype(BF16)
+
+    def tokens_of(index, q):
         return pl.BlockSpec(
-            (1, 1, rows, cols),
-            lambda i, at: (lax.rem(at[0] + o, N_Z), lax.rem(at[1] + q, N_Y), 0, 0),
+            (1, 1, rows, cols), lambda i, at: (index, lax.rem(at[1] + q, N_Y), 0, 0)
         )
 
     def features_of(side):
         return pl.BlockSpec((step, cols), lambda i, at: (side * steps + i, 0))
 
     def chunk(n):
-        return pl.BlockSpec((n, count, rows, step), lambda i, at: (0, 0, 0, i))
+        return pl.BlockSpec((n, rows, step), lambda i, at: (0, 0, i))
 
     in_specs, operands = [], []
     for q in qs:
-        for array in (g_own, g_par):
+        for g in (g_own, g_par):
             for o in seqs:
-                in_specs.append(tokens_of(o, q))
-                operands.append(array)
+                in_specs.append(tokens_of(g[o][1], q))
+                operands.append(g[o][0])
     for side in sides:
         for w in (w_own, w_par):
             in_specs.append(features_of(side))
@@ -157,9 +159,9 @@
         out_specs = [pl.BlockSpec((2, rows, step), lambda i, at: (0, 0, i))] * count
         out_shape = [jax.ShapeDtypeStruct((2, rows, half), BF16)] * count
     else:
-        out_specs = [chunk(len(group)) for group in groups]
+        out_specs = [chunk(len(group) * count) for group in groups]
         out_shape = [
-            jax.ShapeDtypeStruct((len(group), count, rows, half), BF16) for group in groups
+            jax.ShapeDtypeStruct((len(group) * count, rows, half), BF16) for group in groups
         ]
     return call(
         kernel, (steps,), in_specs, out_specs, out_shape, name="partial_sums"
@@ -167,32 +169,37 @@
 
 
 def weight_terms(place, n_pieces, g):
-    part, rows = n_pieces[0][0].shape
-    cols = g.shape[3]
-    step = 512
+    _, part, rows = n_pieces[0][0][0].shape
+    cols = g[0][0].shape[3]
+    step = 256
 
     def kernel(at_ref, *refs):
-        n_refs, (g_ref, out_ref) = refs[: N_Z * N_Y], refs[N_Z * N_Y :]
+        n_refs, g_refs, out_ref = refs[: N_Z * N_Y], refs[N_Z * N_Y : -1], refs[-1]
         total = None
         for o in range(N_Z):
-            left = jnp.concatenate([n_refs[o * N_Y + q][...] for q in range(N_Y)], 1)
-            z = lax.rem(at_ref[0] + o, N_Z)
+            left = jnp.concatenate([n_refs[o * N_Y + q][0] for q in range(N_Y)], 1)
             right = jnp.concatenate(
-                [g_ref[z, lax.rem(at_ref[1] + q, N_Y)] for q in range(N_Y)], 0
+                [g_refs[o][0, lax.rem(at_ref[1] + q, N_Y)] for q in range(N_Y)], 0
             )
             term = dot_nn(left, right)
             total = term if total is None else total + term
         out_ref[...] = total.astype(BF16)
 
+    def piece(index):
+        return pl.BlockSpec((1, step, rows), lambda i, at: (index, i, 0))
+
+    def tokens(index):
+        return pl.BlockSpec((1, N_Y, rows, cols), lambda i, at: (index, 0, 0, 0))
+
+    flat = [n_pieces[o][q] for o in range(N_Z) for q in range(N_Y)]
     return call(
         kernel,
         (part // step,),
-        [pl.BlockSpec((step, rows), lambda i, at: (i, 0))] * (N_Z * N_Y)
-        + [pl.BlockSpec((N_Z, N_Y, rows, cols), lambda i, at: (0, 0, 0, 0))],
+        [piece(index) for _, index in flat] + [tokens(index) for _, index in g],
         pl.BlockSpec((step, cols), lambda i, at: (i, 0)),
         jax.ShapeDtypeStruct((part, cols), BF16),
         name="weight_terms",
-    )(place, *[n_pieces[o][q] for o in range(N_Z) for q in range(N_Y)], g)
+    )(place, *[array for array, _ in flat], *[array for array, _ in g])
 
 
 def finish(place, deviation, gain, hidden, received, h):
@@ -252,67 +259,87 @@
     layers = lax.axis_size("pipe")
     chains = Chains()
 
-    def yy(block, o, depth=1):
-        return chains("y%d" % o, block, lambda b: from_y(b, o), depth)
+    def zz(block, o):
+        return chains("z%d" % o, block, lambda b: from_z(b, o))
+
+    def yy(block, o):
+        return chains("y%d" % o, block, lambda b: from_y(b, o))
 
     def xx(block):
         return chains("x", block, from_x)
 
     grads = qkv_grad[0].reshape(2, N_Y, rows, cols)
-    par0 = xx(lax.dynamic_index_in_dim(grads, 1 - xh, 0, keepdims=False))
-    g_own = lax.all_gather(lax.dynamic_index_in_dim(grads, xh, 0, keepdims=False), "dp")
+    par0 = xx(lax.dynamic_slice_in_dim(grads, 1 - xh, 1, 0))
 
     deviation, *n_to = normalize(place, hidden_in[0], norm_gain)
-    n1, n3 = from_z(n_to[3], 1), from_z(n_to[1], 3)
-    n_up, n_down = {0: yy(n_to[0], 1, 2)}, {0: yy(n_to[0], 3, 2)}
-    n2 = from_z(after(n_to[2], n1, n3), 2)
-    n_near = [n_to[0], n1, n2, n3]
-
-    g_par = lax.all_gather(after(par0, n1, n3), "dp")
+    n1, n3 = zz(n_to[3], 1), zz(n_to[1], 3)
+    n2 = chains.hold("z1", "z3", from_z(after(n_to[2], n1, n3), 2))
     w_own = lax.dynamic_slice_in_dim(qkv_weight[0], z * part, part, 0)
-    w_par = xx(after(w_own, n1, n3, n_up[0], n_down[0]))
-    received = lax.ppermute(
-        after(upper_grad, w_par), "pipe", [(i + 1, i) for i in range(layers - 1)]
-    )
-    for o in (1, 3, 2):
-        n_up[o], n_down[o] = yy(n_near[o], 1, 2), yy(n_near[o], 3, 2)
-    n_across = {}
+    n_near = [after(n_to[0], w_own), n1, n2, n3]
+    n_up, n_down, n_across = {}, {}, {}
+    for o in (0, 1, 3, 2):
+        n_up[o], n_down[o] = yy(n_near[o], 1), yy(n_near[o], 3)
     for one, other in ((0, 1), (3, 2)):
-        n_across[one], n_across[other] = yy(n_up[one], 1, 2), yy(n_down[other], 3, 2)
-    n_pieces = [[n_near[o], n_up[o], n_across[o], n_down[o]] for o in range(N_Z)]
-
-    dw_got = xx(weight_terms(place, n_pieces, g_par))
+        n_across[one], n_across[other] = yy(n_up[one], 1), yy(n_down[other], 3)
+    n_pieces = [
+        [(n_near[o], 0), (n_up[o], 0), (n_across[o], 0), (n_down[o], 0)] for o in range(N_Z)
+    ]
+
+    own0 = lax.dynamic_slice_in_dim(grads, xh, 1, 0)
+    own1, own3 = zz(own0, 1), zz(own0, 3)
+    par1, par3 = zz(par0, 1), zz(par0, 3)
+    own2, par2 = zz(own1, 1), zz(par3, 3)
+    g_own = [(own0, 0), (own1, 0), (own2, 0), (own3, 0)]
+    g_par = [(par0, 0), (par1, 0), (par2, 0), (par3, 0)]
+
+    w_par = xx(w_own)
+    moved = (n_near, n_up, n_down, n_across, own0, own1, own2, own3, par0, par1, par2, par3)
+    moved, w_own, w_par, upper_grad = lax.optimization_barrier((moved, w_own, w_par, upper_grad))
+    n_near, n_up, n_down, n_across, own0, own1, own2, own3, par0, par1, par2, par3 = moved
+    n_pieces = [
+        [(n_near[o], 0), (n_up[o], 0), (n_across[o], 0), (n_down[o], 0)] for o in range(N_Z)
+    ]
+    g_own = [(own0, 0), (own1, 0), (own2, 0), (own3, 0)]
+    g_par = [(par0, 0), (par1, 0), (par2, 0), (par3, 0)]
+
+    dw_partner = weight_terms(place, n_pieces, g_par)
+    dw_got = xx(dw_partner)
+
+    sums = functools.partial(partial_sums, place, g_own=g_own, g_par=g_par, w_own=w_own, w_par=w_par)
+    far = [1, 2, 3]
+    p2a, p2b = sums(far, [[(2, 0, ())], [(2, 1, ())]])
+    hop_up, hop_down = yy(p2a, 3), yy(p2b, 1)
     dw_own = weight_terms(place, n_pieces, g_own)
-
-    sums = functools.partial(partial_sums, place, g_own=g_own, g_par=g_par, w_own=w_own, w_par=w_par)
-
-    def first(seqs):
-        up, down = sums(seqs, [[(2, 0, ()), (1, 1, ())], [(2, 1, ()), (3, 0, ())]])
-        return yy(up, 3), yy(down, 1)
-
-    def second(seqs, up, down):
-        up2, down2 = sums(seqs, [[(1, 0, [(0, 0)])], [(3, 1, [(1, 0)])]], extras=[up, down])
-        return yy(up2, 3), yy(down2, 1)
-
-    def third(seqs, up, down, up2, down2):
-        return sums(
-            seqs,
-            [[(0, 0, [(1, 1), (2, 0)]), (0, 1, [(0, 1), (3, 0)])]],
-            extras=[up, down, up2, down2],
-            per_sequence=True,
-        )
-
-    here, there = [2, 3], [1, 0]
-    one = first(here)
-    two = first(there)
-    one = one + second(here, after(one[0], received), one[1])
-    two = two + second(there, *two)
-    h_to2, h_to3 = third(here, after(one[0], dw_own), *one[1:])
-    h2, h1 = from_z(h_to2, 2), from_z(h_to3, 1)
-    h_to1, h0 = third(there, *two)
-    h3 = from_z(h_to1, 3)
-
-    weight_out = (dw_own.astype(F32) + after(dw_got, h1, h2).astype(F32)).astype(BF16)
+    p1b, p3a = sums(far, [[(1, 1, ())], [(3, 0, ())]], w_par=after(w_par, dw_partner))
+    up_b, down_a = yy(p1b, 3), yy(p3a, 1)
+    p1a, p3b = sums(
+        far,
+        [[(1, 0, [(0, 0)])], [(3, 1, [(1, 0)])]],
+        extras=[hop_up, hop_down],
+    )
+    up_a, down_b = yy(p1a, 3), yy(p3b, 1)
+    up, down = sums([0], [[(2, 0, ()), (1, 1, ())], [(2, 1, ()), (3, 0, ())]])
+    h_to1, h_to2, h_to3 = sums(
+        far,
+        [[(0, 0, [(0, 0), (1, 0)]), (0, 1, [(2, 0), (3, 0)])]],
+        extras=[after(up_a, dw_own, up), down_a, down_b, up_b],
+        per_sequence=True,
+    )
+    received = lax.ppermute(after(upper_grad, p1a), "pipe", [(i + 1, i) for i in range(layers - 1)])
+    h2 = from_z(h_to2, 2)
+    h1, h3 = from_z(after(h_to3, h2), 1), from_z(after(h_to1, h2), 3)
+
+    up, down = yy(after(up, h_to2), 3), yy(after(down, h_to2), 1)
+    p1a, p3b = sums([0], [[(1, 0, [(0, 0)])], [(3, 1, [(1, 0)])]], extras=[after(up, h2), down])
+    up2, down2 = yy(p1a, 3), yy(p3b, 1)
+    (h0,) = sums(
+        [0],
+        [[(0, 0, [(1, 1), (2, 0)]), (0, 1, [(0, 1), (3, 0)])]],
+        extras=[after(up, h1, h3), down, up2, down2],
+        per_sequence=True,
+    )
+
+    weight_out = (dw_own.astype(F32) + dw_got.astype(F32)).astype(BF16)
     input_out = finish(place, deviation, norm_gain, hidden_in[0], received, [h0, h1, h2, h3])
     return (weight_out[None], input_out)
 

time: 251 us -> 206 us (0.82)
  waiting for transfers between devices: 117 us -> 74.8 us
  starting transfers between devices: 48.5 us -> 67.7 us
  between operations: 14.3 us -> 0.84 us
  local copies, waits for them, and re-layouts: 17.3 us -> 6.93 us
    ppermute x20 -> x22, waiting for transfers between devices: 61.9 us -> 45.1 us  [from_y(): lax.ppermute(block, 'tensor', [(x * N_Y + (i + o) % N_Y, x * N_Y + i) for...]
    ppermute x6 -> x12, waiting for transfers between devices: 40.4 us -> 26.5 us  [from_z(): return lax.ppermute(block, 'dp', [((i + o) % N_Z, i) for i in range(N_Z)])]
    ppermute x6 -> x12, starting transfers between devices: 11.3 us -> 23.2 us  [from_z(): return lax.ppermute(block, 'dp', [((i + o) % N_Z, i) for i in range(N_Z)])]
    ppermute x3, waiting for transfers between devices: 14.2 us -> 3.25 us  [from_x(): lax.ppermute(block, 'tensor', [(i, (i + N_Y) % (2 * N_Y)) for i in range(...]
    unnamed x42 -> x12, local copies, waits for them, and re-layouts: 12.3 us -> 2.42 us
    pallas_call x6 -> x7, Pallas kernels: 23.8 us -> 28.8 us  [partial_sums(): call(kernel, (steps,), in_specs, out_specs, out_shape, name='partial_sums')]
    ppermute x20 -> x22, starting transfers between devices: 32.1 us -> 36.3 us  [from_y(): lax.ppermute(block, 'tensor', [(x * N_Y + (i + o) % N_Y, x * N_Y + i) for...]
    ppermute x3, starting transfers between devices: 3.73 us -> 6.94 us  [from_x(): lax.ppermute(block, 'tensor', [(i, (i + N_Y) % (2 * N_Y)) for i in range(...]
  transfers between devices with their start and end apart: 32 -> 38, of which waited for: 16 -> 17; matrix products, arithmetic and copies ran while one was open for 2% -> 2% of each run, Pallas kernels for 18% -> 19%
where the time goes in v5:
time: 206 us
  waiting for transfers between devices  74.8 us (36%)
  starting transfers between devices  67.7 us (33%)
  Pallas kernels  53.2 us (26%)
  local copies, waits for them, and re-layouts  6.93 us (3%)
  other arithmetic  2.65 us (1%)
    ppermute x22, waiting for transfers between devices, from_y(): lax.ppermute(block, 'tensor', [(x * N_Y + (i + o) % N_Y, x * N_Y + i) for...  45.1 us
    ppermute x22, starting transfers between devices, from_y(): lax.ppermute(block, 'tensor', [(x * N_Y + (i + o) % N_Y, x * N_Y + i) for...  36.3 us
    pallas_call x7, Pallas kernels, partial_sums(): call(kernel, (steps,), in_specs, out_specs, out_shape, name='partial_sums')  28.8 us
    ppermute x12, waiting for transfers between devices, from_z(): return lax.ppermute(block, 'dp', [((i + o) % N_Z, i) for i in range(N_Z)])  26.5 us
    ppermute x12, starting transfers between devices, from_z(): return lax.ppermute(block, 'dp', [((i + o) % N_Z, i) for i in range(N_Z)])  23.2 us
    pallas_call x2, Pallas kernels, weight_terms(): call(kernel, (part // step,), [piece(index) for _, index in flat] + [toke...  17.3 us
    ppermute x3, starting transfers between devices, from_x(): lax.ppermute(block, 'tensor', [(i, (i + N_Y) % (2 * N_Y)) for i in range(...  6.94 us
    pallas_call x1, Pallas kernels, finish(): call(kernel, (rows // step,), [pl.BlockSpec((step, 128), lambda i, at: (i...  4.37 us
  transfers between devices with their start and end apart: 38, of which 17 were waited for; matrix products, arithmetic and copies ran while one was open for 2% of the time, Pallas kernels for 19%

profile of v5, /device:TPU:0, one launch (start us, length us, event | category | flops | bytes accessed | tf_op | source)
XLA Modules:
  0.0 206.1 jit_solution(10779754274234290660)
XLA Ops:
  0.7 2.4 %constant_dynamic-slice_fusion = (bf16[1,4,128,768]{3,2,1,0:T(8,128)(2,1)}, bf16[1,4,128,768]{3,2,1,0:T(8,128)(2,1)S(1)}) fusion(bf16[2,4,128,768]{3,2,1,0:T(8,128)(2,1)} %bitcast.10, s32[]{:T(128)S(6)} %select_n.24, s32[]{:T(128)S(6)} %select_n.23), kind=kLoop, calls=%fused_computation.3 | loop fusion | bytes 3145736 | tf_op jit(solution)/shard_map/dynamic_slice | solution.py:272
  3.0 3.1 %collective-permute-start.16 = (bf16[1,4,128,768]{3,2,1,0:T(8,128)(2,1)}, bf16[1,4,128,768]{3,2,1,0:T(8,128)(2,1)S(1)}, u32[]{:S(2)}, u32[]{:S(2)}) collective-permute-start(bf16[1,4,128,768]{3,2,1,0:T(8,128)(2,1)} %get-tuple-element.168), channel_id=1, source_target_pairs={{0,4},{1,5},{2,6},{3,7},{4,0},{5,1},{6,2},{7,3},{8,12},{9,13},{10,... | collective-permute-start | bytes 2359304 | tf_op jit(solution)/shard_map/ppermute | solution.py:49
  6.1 0.1 pad_add_fusion.at_ref
  6.2 1.6 copy-done
  7.8 2.7 %normalize.1 = (f32[128,128]{1,0:T(8,128)S(1)}, bf16[1,2048,128]{2,1,0:T(8,128)(2,1)S(1)}, bf16[1,2048,128]{2,1,0:T(8,128)(2,1)}, bf16[1,2048,128]{2,1,0:T(8,128)(2,1)S(1)}, bf16[1,2048,128]{2,1,0:T(8,128)(2,1)}) custom-call(s32[2]{0:T(128)S(1)} %pad_add_fusion.at_ref, bf16[128,8192]{1,0:T(8,128)(2,1)S(1)} %bitcast.8, bf16[1,8192]{1,0:T(2,128)(2,1)S(1)} %copy-done.2), custom_call_target="tpu_custom_call" | custom-call | bytes 4194304 | tf_op jit(solution)/shard_map/normalize/pallas_call | solution.py:92
  10.5 0.8 copy-done.3
  11.4 4.0 %collective-permute-start = (bf16[1,2048,128]{2,1,0:T(8,128)(2,1)}, bf16[1,2048,128]{2,1,0:T(8,128)(2,1)S(1)}, u32[]{:S(2)}, u32[]{:S(2)}) collective-permute-start(bf16[1,2048,128]{2,1,0:T(8,128)(2,1)} %get-tuple-element.87), channel_id=1, source_target_pairs={{8,0},{16,8},{24,16},{0,24},{9,1},{17,9},{25,17},{1,25},{10,2},{18... | collective-permute-start | bytes 1572872 | tf_op jit(solution)/shard_map/ppermute | solution.py:37
  15.4 0.0 collective-permute-start.1
  15.4 2.2 %dynamic-slice_bitcast_fusion.refs_6_.refs_8_.refs_12_.refs_14_.refs_4_.refs_2_ = bf16[2048,768]{1,0:T(8,128)(2,1)S(1)} fusion(bf16[1,8192,768]{2,1,0:T(8,128)(2,1)} %param.7, s32[]{:T(128)S(6)} %select_n.21), kind=kLoop, calls=%fused_computation.2 | loop fusion | bytes 6291460 | tf_op jit(solution)/shard_map/dynamic_slice | solution.py:277
  17.5 3.1 %collective-permute-start.3 = (bf16[1,2048,128]{2,1,0:T(8,128)(2,1)S(1)}, bf16[1,2048,128]{2,1,0:T(8,128)(2,1)S(1)}, u32[]{:S(2)}, u32[]{:S(2)}) collective-permute-start(bf16[1,2048,128]{2,1,0:T(8,128)(2,1)S(1)} %get-tuple-element.107.refs_0_), channel_id=1, source_target_pairs={{1,0},{2,1},{3,2},{0,3},{5,4},{6,5},{7,6},{4,7},{9,8},{10,9},{11,1... | collective-permute-start | bytes 1572872 | tf_op jit(solution)/shard_map/ppermute | solution.py:41
  20.6 3.2 %collective-permute-done.16.refs_16_.refs_1_.refs_3_.refs_5_ = bf16[1,4,128,768]{3,2,1,0:T(8,128)(2,1)S(1)} collective-permute-done((bf16[1,4,128,768]{3,2,1,0:T(8,128)(2,1)}, bf16[1,4,128,768]{3,2,1,0:T(8,128)(2,1)S(1)}, u32[]{:S(2)}, u32[]{:S(2)}) %collective-permute-start.16) | collective-permute-done | bytes 786464 | tf_op jit(solution)/shard_map/ppermute | solution.py:49
  23.9 3.2 %collective-permute-start.22 = (bf16[2048,768]{1,0:T(8,128)(2,1)S(1)}, bf16[2048,768]{1,0:T(8,128)(2,1)S(1)}, u32[]{:S(2)}, u32[]{:S(2)}) collective-permute-start(bf16[2048,768]{1,0:T(8,128)(2,1)S(1)} %dynamic-slice_bitcast_fusion.refs_6_.refs_8_.refs_12_.refs_14_.refs_4_.refs_2_), channel_id=1, source_target_pairs={{0,4},{1,5},{2,6},{3,7},{4,0},{5,1},{6,2},{7,3},{8,12},{9,13},{10,... | collective-permute-start | bytes 9437192 | tf_op jit(solution)/shard_map/ppermute | solution.py:49
  27.1 0.0 collective-permute-done.refs_4_
  27.1 2.8 %collective-permute-done.1.refs_12_ = bf16[1,2048,128]{2,1,0:T(8,128)(2,1)S(1)} collective-permute-done((bf16[1,2048,128]{2,1,0:T(8,128)(2,1)}, bf16[1,2048,128]{2,1,0:T(8,128)(2,1)S(1)}, u32[]{:S(2)}, u32[]{:S(2)}) %collective-permute-start.1) | collective-permute-done | bytes 524320 | tf_op jit(solution)/shard_map/ppermute | solution.py:37
  29.9 1.2 collective-permute-start.2
  31.1 0.2 collective-permute-done.3.refs_1_
  31.3 3.7 %collective-permute-start.4 = (bf16[1,2048,128]{2,1,0:T(8,128)(2,1)S(1)}, bf16[1,2048,128]{2,1,0:T(8,128)(2,1)S(1)}, u32[]{:S(2)}, u32[]{:S(2)}) collective-permute-start(bf16[1,2048,128]{2,1,0:T(8,128)(2,1)S(1)} %collective-permute-done.refs_4_), channel_id=1, source_target_pairs={{1,0},{2,1},{3,2},{0,3},{5,4},{6,5},{7,6},{4,7},{9,8},{10,9},{11,1... | collective-permute-start | bytes 1572872 | tf_op jit(solution)/shard_map/ppermute | solution.py:41
  35.0 8.6 %collective-permute-done.2.refs_8_ = bf16[1,2048,128]{2,1,0:T(8,128)(2,1)S(1)} collective-permute-done((bf16[1,2048,128]{2,1,0:T(8,128)(2,1)S(1)}, bf16[1,2048,128]{2,1,0:T(8,128)(2,1)S(1)}, u32[]{:S(2)}, u32[]{:S(2)}) %collective-permute-start.2) | collective-permute-done | bytes 524320 | tf_op jit(solution)/shard_map/ppermute | solution.py:37
  43.6 1.7 collective-permute-start.15
  45.3 0.4 collective-permute-start.19
  45.6 3.0 %collective-permute-start.5 = (bf16[1,2048,128]{2,1,0:T(8,128)(2,1)S(1)}, bf16[1,2048,128]{2,1,0:T(8,128)(2,1)S(1)}, u32[]{:S(2)}, u32[]{:S(2)}) collective-permute-start(bf16[1,2048,128]{2,1,0:T(8,128)(2,1)S(1)} %collective-permute-done.1.refs_12_), channel_id=1, source_target_pairs={{1,0},{2,1},{3,2},{0,3},{5,4},{6,5},{7,6},{4,7},{9,8},{10,9},{11,1... | collective-permute-start | bytes 1572872 | tf_op jit(solution)/shard_map/ppermute | solution.py:41
  48.7 8.5 %collective-permute-done.5.refs_13_ = bf16[1,2048,128]{2,1,0:T(8,128)(2,1)S(1)} collective-permute-done((bf16[1,2048,128]{2,1,0:T(8,128)(2,1)S(1)}, bf16[1,2048,128]{2,1,0:T(8,128)(2,1)S(1)}, u32[]{:S(2)}, u32[]{:S(2)}) %collective-permute-start.5) | collective-permute-done | bytes 524320 | tf_op jit(solution)/shard_map/ppermute | solution.py:41
  57.1 3.6 %collective-permute-done.9.refs_15_ = bf16[1,2048,128]{2,1,0:T(8,128)(2,1)S(1)} collective-permute-done((bf16[1,2048,128]{2,1,0:T(8,128)(2,1)S(1)}, bf16[1,2048,128]{2,1,0:T(8,128)(2,1)S(1)}, u32[]{:S(2)}, u32[]{:S(2)}) %collective-permute-start.9) | collective-permute-done | bytes 524320 | tf_op jit(solution)/shard_map/ppermute | solution.py:41
  60.7 3.2 %collective-permute-start.6 = (bf16[1,2048,128]{2,1,0:T(8,128)(2,1)S(1)}, bf16[1,2048,128]{2,1,0:T(8,128)(2,1)S(1)}, u32[]{:S(2)}, u32[]{:S(2)}) collective-permute-start(bf16[1,2048,128]{2,1,0:T(8,128)(2,1)S(1)} %collective-permute-done.2.refs_8_), channel_id=1, source_target_pairs={{1,0},{2,1},{3,2},{0,3},{5,4},{6,5},{7,6},{4,7},{9,8},{10,9},{11,1... | collective-permute-start | bytes 1572872 | tf_op jit(solution)/shard_map/ppermute | solution.py:41
  64.0 2.9 %collective-permute-start.17 = (bf16[1,4,128,768]{3,2,1,0:T(8,128)(2,1)S(1)}, bf16[1,4,128,768]{3,2,1,0:T(8,128)(2,1)S(1)}, u32[]{:S(2)}, u32[]{:S(2)}) collective-permute-start(bf16[1,4,128,768]{3,2,1,0:T(8,128)(2,1)S(1)} %collective-permute-done.16.refs_16_.refs_1_.refs_3_.refs_5_), channel_id=1, source_target_pairs={{8,0},{16,8},{24,16},{0,24},{9,1},{17,9},{25,17},{1,25},{10,2},{18... | collective-permute-start | bytes 2359304 | tf_op jit(solution)/shard_map/ppermute | solution.py:37
  66.9 6.0 %collective-permute-done.10.refs_11_ = bf16[1,2048,128]{2,1,0:T(8,128)(2,1)S(1)} collective-permute-done((bf16[1,2048,128]{2,1,0:T(8,128)(2,1)S(1)}, bf16[1,2048,128]{2,1,0:T(8,128)(2,1)S(1)}, u32[]{:S(2)}, u32[]{:S(2)}) %collective-permute-start.10) | collective-permute-done | bytes 524320 | tf_op jit(solution)/shard_map/ppermute | solution.py:41
  72.8 3.2 %collective-permute-start.11 = (bf16[1,2048,128]{2,1,0:T(8,128)(2,1)S(1)}, bf16[1,2048,128]{2,1,0:T(8,128)(2,1)S(1)}, u32[]{:S(2)}, u32[]{:S(2)}) collective-permute-start(bf16[1,2048,128]{2,1,0:T(8,128)(2,1)S(1)} %collective-permute-done.3.refs_1_), channel_id=1, source_target_pairs={{1,0},{2,1},{3,2},{0,3},{5,4},{6,5},{7,6},{4,7},{9,8},{10,9},{11,1... | collective-permute-start | bytes 1572872 | tf_op jit(solution)/shard_map/ppermute | solution.py:41
  76.1 4.9 %collective-permute-done.17.refs_17_.refs_3_.refs_9_ = bf16[1,4,128,768]{3,2,1,0:T(8,128)(2,1)S(1)} collective-permute-done((bf16[1,4,128,768]{3,2,1,0:T(8,128)(2,1)S(1)}, bf16[1,4,128,768]{3,2,1,0:T(8,128)(2,1)S(1)}, u32[]{:S(2)}, u32[]{:S(2)}) %collective-permute-start.17) | collective-permute-done | bytes 786464 | tf_op jit(solution)/shard_map/ppermute | solution.py:37
  81.0 3.6 %collective-permute-start.18 = (bf16[1,4,128,768]{3,2,1,0:T(8,128)(2,1)S(1)}, bf16[1,4,128,768]{3,2,1,0:T(8,128)(2,1)S(1)}, u32[]{:S(2)}, u32[]{:S(2)}) collective-permute-start(bf16[1,4,128,768]{3,2,1,0:T(8,128)(2,1)S(1)} %collective-permute-done.15.refs_17_.refs_0_.refs_6_), channel_id=1, source_target_pairs={{8,0},{16,8},{24,16},{0,24},{9,1},{17,9},{25,17},{1,25},{10,2},{18... | collective-permute-start | bytes 2359304 | tf_op jit(solution)/shard_map/ppermute | solution.py:37
  84.6 0.5 collective-permute-done.12.refs_6_
  85.1 3.5 %collective-permute-start.14 = (bf16[1,2048,128]{2,1,0:T(8,128)(2,1)S(1)}, bf16[1,2048,128]{2,1,0:T(8,128)(2,1)S(1)}, u32[]{:S(2)}, u32[]{:S(2)}) collective-permute-start(bf16[1,2048,128]{2,1,0:T(8,128)(2,1)S(1)} %collective-permute-done.5.refs_13_), channel_id=1, source_target_pairs={{1,0},{2,1},{3,2},{0,3},{5,4},{6,5},{7,6},{4,7},{9,8},{10,9},{11,1... | collective-permute-start | bytes 1572872 | tf_op jit(solution)/shard_map/ppermute | solution.py:41
  88.6 6.9 %collective-permute-done.13.refs_10_ = bf16[1,2048,128]{2,1,0:T(8,128)(2,1)S(1)} collective-permute-done((bf16[1,2048,128]{2,1,0:T(8,128)(2,1)S(1)}, bf16[1,2048,128]{2,1,0:T(8,128)(2,1)S(1)}, u32[]{:S(2)}, u32[]{:S(2)}) %collective-permute-start.13) | collective-permute-done | bytes 524320 | tf_op jit(solution)/shard_map/ppermute | solution.py:41
  95.5 0.5 collective-permute-done.18.refs_18_.refs_1_.refs_7_
  96.0 3.4 %collective-permute-done.21.refs_18_.refs_4_.refs_10_ = bf16[1,4,128,768]{3,2,1,0:T(8,128)(2,1)S(1)} collective-permute-done((bf16[1,4,128,768]{3,2,1,0:T(8,128)(2,1)S(1)}, bf16[1,4,128,768]{3,2,1,0:T(8,128)(2,1)S(1)}, u32[]{:S(2)}, u32[]{:S(2)}) %collective-permute-start.21) | collective-permute-done | bytes 786464 | tf_op jit(solution)/shard_map/ppermute | solution.py:37
  99.4 8.7 %weight_terms.3 = bf16[2048,768]{1,0:T(8,128)(2,1)S(1)} custom-call(s32[2]{0:T(128)S(1)} %pad_add_fusion.at_ref, bf16[1,2048,128]{2,1,0:T(8,128)(2,1)S(1)} %get-tuple-element.107.refs_0_, bf16[1,2048,128]{2,1,0:T(8,128)(2,1)S(1)} %collective-permute-done.3.refs_1_, bf16[1,2048,128]{2,1,0:T(8,128)(2,1)S(1)} %collective-permute-done.11.refs_2_, ...), custom_call_target="tpu_custom_call" | custom-call | tf_op jit(solution)/shard_map/weight_terms/pallas_call | solution.py:195
  108.1 0.6 collective-permute-start.23
  108.7 4.0 %partial_sums.7 = (bf16[3,128,1024]{2,1,0:T(8,128)(2,1)S(1)}, bf16[3,128,1024]{2,1,0:T(8,128)(2,1)S(1)}) custom-call(s32[2]{0:T(128)S(1)} %pad_add_fusion.at_ref, bf16[1,4,128,768]{3,2,1,0:T(8,128)(2,1)S(1)} %collective-permute-done.15.refs_17_.refs_0_.refs_6_, bf16[1,4,128,768]{3,2,1,0:T(8,128)(2,1)S(1)} %collective-permute-done.18.refs_18_.refs_1_.refs_7_, ...), custom_call_target="tpu_custom_call" | custom-call | tf_op jit(solution)/shard_map/partial_sums/pallas_call | solution.py:166
  112.6 0.3 collective-permute-start.24
  112.9 3.2 %collective-permute-start.25 = (bf16[3,128,1024]{2,1,0:T(8,128)(2,1)S(1)}, bf16[3,128,1024]{2,1,0:T(8,128)(2,1)S(1)}, u32[]{:S(2)}, u32[]{:S(2)}) collective-permute-start(bf16[3,128,1024]{2,1,0:T(8,128)(2,1)S(1)} %get-tuple-element.139), channel_id=1, source_target_pairs={{1,0},{2,1},{3,2},{0,3},{5,4},{6,5},{7,6},{4,7},{9,8},{10,9},{11,1... | collective-permute-start | bytes 2359304 | tf_op jit(solution)/shard_map/ppermute | solution.py:41
  116.1 4.0 %partial_sums.10 = (bf16[3,128,1024]{2,1,0:T(8,128)(2,1)S(1)}, bf16[3,128,1024]{2,1,0:T(8,128)(2,1)S(1)}) custom-call(s32[2]{0:T(128)S(1)} %pad_add_fusion.at_ref, bf16[1,4,128,768]{3,2,1,0:T(8,128)(2,1)S(1)} %collective-permute-done.15.refs_17_.refs_0_.refs_6_, bf16[1,4,128,768]{3,2,1,0:T(8,128)(2,1)S(1)} %collective-permute-done.18.refs_18_.refs_1_.refs_7_, ...), custom_call_target="tpu_custom_call" | custom-call | tf_op jit(solution)/shard_map/partial_sums/pallas_call | solution.py:166
  120.1 10.1 %collective-permute-done.24.refs_16_ = bf16[3,128,1024]{2,1,0:T(8,128)(2,1)S(1)} collective-permute-done((bf16[3,128,1024]{2,1,0:T(8,128)(2,1)S(1)}, bf16[3,128,1024]{2,1,0:T(8,128)(2,1)S(1)}, u32[]{:S(2)}, u32[]{:S(2)}) %collective-permute-start.24) | collective-permute-done | bytes 786464 | tf_op jit(solution)/shard_map/ppermute | solution.py:41
  130.2 0.4 collective-permute-start.27
  130.6 2.9 %collective-permute-start.29 = (bf16[3,128,1024]{2,1,0:T(8,128)(2,1)S(1)}, bf16[3,128,1024]{2,1,0:T(8,128)(2,1)S(1)}, u32[]{:S(2)}, u32[]{:S(2)}) collective-permute-start(bf16[3,128,1024]{2,1,0:T(8,128)(2,1)S(1)} %get-tuple-element.149), channel_id=1, source_target_pairs={{1,0},{2,1},{3,2},{0,3},{5,4},{6,5},{7,6},{4,7},{9,8},{10,9},{11,1... | collective-permute-start | bytes 2359304 | tf_op jit(solution)/shard_map/ppermute | solution.py:41
  133.5 4.2 %partial_sums.8 = (bf16[3,128,1024]{2,1,0:T(8,128)(2,1)S(1)}, bf16[3,128,1024]{2,1,0:T(8,128)(2,1)S(1)}) custom-call(s32[2]{0:T(128)S(1)} %pad_add_fusion.at_ref, bf16[1,4,128,768]{3,2,1,0:T(8,128)(2,1)S(1)} %collective-permute-done.15.refs_17_.refs_0_.refs_6_, bf16[1,4,128,768]{3,2,1,0:T(8,128)(2,1)S(1)} %collective-permute-done.18.refs_18_.refs_1_.refs_7_, ...), custom_call_target="tpu_custom_call" | custom-call | tf_op jit(solution)/shard_map/partial_sums/pallas_call | solution.py:166
  137.7 1.3 collective-permute-start.26
  139.0 8.7 %collective-permute-done.27.refs_13_ = bf16[3,128,1024]{2,1,0:T(8,128)(2,1)S(1)} collective-permute-done((bf16[3,128,1024]{2,1,0:T(8,128)(2,1)S(1)}, bf16[3,128,1024]{2,1,0:T(8,128)(2,1)S(1)}, u32[]{:S(2)}, u32[]{:S(2)}) %collective-permute-start.27) | collective-permute-done | bytes 786464 | tf_op jit(solution)/shard_map/ppermute | solution.py:41
  147.7 0.6 collective-permute-start.28
  148.3 2.6 %collective-permute-start.30 = (bf16[3,128,1024]{2,1,0:T(8,128)(2,1)S(1)}, bf16[3,128,1024]{2,1,0:T(8,128)(2,1)S(1)}, u32[]{:S(2)}, u32[]{:S(2)}) collective-permute-start(bf16[3,128,1024]{2,1,0:T(8,128)(2,1)S(1)} %get-tuple-element.151), channel_id=1, source_target_pairs={{1,0},{2,1},{3,2},{0,3},{5,4},{6,5},{7,6},{4,7},{9,8},{10,9},{11,1... | collective-permute-start | bytes 2359304 | tf_op jit(solution)/shard_map/ppermute | solution.py:41
  151.0 8.7 %weight_terms.2 = bf16[2048,768]{1,0:T(8,128)(2,1)S(1)} custom-call(s32[2]{0:T(128)S(1)} %pad_add_fusion.at_ref, bf16[1,2048,128]{2,1,0:T(8,128)(2,1)S(1)} %get-tuple-element.107.refs_0_, bf16[1,2048,128]{2,1,0:T(8,128)(2,1)S(1)} %collective-permute-done.3.refs_1_, bf16[1,2048,128]{2,1,0:T(8,128)(2,1)S(1)} %collective-permute-done.11.refs_2_, ...), custom_call_target="tpu_custom_call" | custom-call | tf_op jit(solution)/shard_map/weight_terms/pallas_call | solution.py:195
  159.6 5.2 %partial_sums.9 = (bf16[2,128,1024]{2,1,0:T(8,128)(2,1)S(1)}, bf16[2,128,1024]{2,1,0:T(8,128)(2,1)S(1)}) custom-call(s32[2]{0:T(128)S(1)} %pad_add_fusion.at_ref, bf16[1,4,128,768]{3,2,1,0:T(8,128)(2,1)S(1)} %get-tuple-element.123.refs_16_.refs_0_.refs_2_.refs_4_, bf16[1,4,128,768]{3,2,1,0:T(8,128)(2,1)S(1)} %collective-permute-done.16.refs_16_.refs_1_.refs_3_.refs_5_, ...), custom_call_target="tpu_custom_call" | custom-call | tf_op jit(solution)/shard_map/partial_sums/pallas_call | solution.py:166
  164.9 4.5 %partial_sums.11 = (bf16[2,128,1024]{2,1,0:T(8,128)(2,1)S(1)}, bf16[2,128,1024]{2,1,0:T(8,128)(2,1)S(1)}, bf16[2,128,1024]{2,1,0:T(8,128)(2,1)S(1)}) custom-call(s32[2]{0:T(128)S(1)} %pad_add_fusion.at_ref, bf16[1,4,128,768]{3,2,1,0:T(8,128)(2,1)S(1)} %collective-permute-done.15.refs_17_.refs_0_.refs_6_, ...), custom_call_target="tpu_custom_call" | custom-call | tf_op jit(solution)/shard_map/partial_sums/pallas_call | solution.py:166
  169.4 3.0 %collective-permute-start.32 = (bf16[2,128,1024]{2,1,0:T(8,128)(2,1)S(1)}, bf16[2,128,1024]{2,1,0:T(8,128)(2,1)S(1)}, u32[]{:S(2)}, u32[]{:S(2)}) collective-permute-start(bf16[2,128,1024]{2,1,0:T(8,128)(2,1)S(1)} %get-tuple-element.152), channel_id=1, source_target_pairs={{16,0},{24,8},{0,16},{8,24},{17,1},{25,9},{1,17},{9,25},{18,2},{26... | collective-permute-start | bytes 1572872 | tf_op jit(solution)/shard_map/ppermute | solution.py:37
  172.4 0.4 collective-permute-start.31
  172.8 2.8 %collective-permute-start.35 = (bf16[2,128,1024]{2,1,0:T(8,128)(2,1)S(1)}, bf16[2,128,1024]{2,1,0:T(8,128)(2,1)S(1)}, u32[]{:S(2)}, u32[]{:S(2)}) collective-permute-start(bf16[2,128,1024]{2,1,0:T(8,128)(2,1)S(1)} %get-tuple-element.162), channel_id=1, source_target_pairs={{1,0},{2,1},{3,2},{0,3},{5,4},{6,5},{7,6},{4,7},{9,8},{10,9},{11,1... | collective-permute-start | bytes 1572872 | tf_op jit(solution)/shard_map/ppermute | solution.py:41
  175.6 5.1 %collective-permute-done.32.refs_2_ = bf16[2,128,1024]{2,1,0:T(8,128)(2,1)S(1)} collective-permute-done((bf16[2,128,1024]{2,1,0:T(8,128)(2,1)S(1)}, bf16[2,128,1024]{2,1,0:T(8,128)(2,1)S(1)}, u32[]{:S(2)}, u32[]{:S(2)}) %collective-permute-start.32) | collective-permute-done | bytes 524320 | tf_op jit(solution)/shard_map/ppermute | solution.py:37
  180.7 6.4 %collective-permute-start.33 = (bf16[2,128,1024]{2,1,0:T(8,128)(2,1)S(1)}, bf16[2,128,1024]{2,1,0:T(8,128)(2,1)S(1)}, u32[]{:S(2)}, u32[]{:S(2)}) collective-permute-start(bf16[2,128,1024]{2,1,0:T(8,128)(2,1)S(1)} %get-tuple-element.156), channel_id=1, source_target_pairs={{8,0},{16,8},{24,16},{0,24},{9,1},{17,9},{25,17},{1,25},{10,2},{18... | collective-permute-start | bytes 1572872 | tf_op jit(solution)/shard_map/ppermute | solution.py:37
  187.2 3.4 %partial_sums.12 = (bf16[1,128,1024]{2,1,0:T(8,128)(2,1)S(1)}, bf16[1,128,1024]{2,1,0:T(8,128)(2,1)S(1)}) custom-call(s32[2]{0:T(128)S(1)} %pad_add_fusion.at_ref, bf16[1,4,128,768]{3,2,1,0:T(8,128)(2,1)S(1)} %get-tuple-element.123.refs_16_.refs_0_.refs_2_.refs_4_, bf16[1,4,128,768]{3,2,1,0:T(8,128)(2,1)S(1)} %collective-permute-done.16.refs_16_.refs_1_.refs_3_.refs_5_, ...), custom_call_target="tpu_custom_call" | custom-call | tf_op jit(solution)/shard_map/partial_sums/pallas_call | solution.py:166
  190.6 0.6 collective-permute-start.36
  191.2 2.7 %collective-permute-start.37 = (bf16[1,128,1024]{2,1,0:T(8,128)(2,1)S(1)}, bf16[1,128,1024]{2,1,0:T(8,128)(2,1)S(1)}, u32[]{:S(2)}, u32[]{:S(2)}) collective-permute-start(bf16[1,128,1024]{2,1,0:T(8,128)(2,1)S(1)} %get-tuple-element.167), channel_id=1, source_target_pairs={{1,0},{2,1},{3,2},{0,3},{5,4},{6,5},{7,6},{4,7},{9,8},{10,9},{11,1... | collective-permute-start | bytes 786440 | tf_op jit(solution)/shard_map/ppermute | solution.py:41
  193.9 2.6 %fusion = bf16[1,2048,768]{2,1,0:T(8,128)(2,1)} fusion(bf16[2048,768]{1,0:T(8,128)(2,1)S(1)} %collective-permute-done.23, bf16[2048,768]{1,0:T(8,128)(2,1)S(1)} %weight_terms.2), kind=kLoop, calls=%fused_computation.1 | loop fusion | flops 6291456 | bytes 9437184 | tf_op jit(solution)/shard_map/broadcast_in_dim | solution.py:344
  196.5 1.1 collective-permute-done.34.refs_3_
  197.6 0.7 collective-permute-done.36.refs_8_
  198.2 3.5 %partial_sums.13.refs_0_ = bf16[2,128,1024]{2,1,0:T(8,128)(2,1)S(1)} custom-call(s32[2]{0:T(128)S(1)} %pad_add_fusion.at_ref, bf16[1,4,128,768]{3,2,1,0:T(8,128)(2,1)S(1)} %get-tuple-element.123.refs_16_.refs_0_.refs_2_.refs_4_, bf16[1,4,128,768]{3,2,1,0:T(8,128)(2,1)S(1)} %collective-permute-done.16.refs_16_.refs_1_.refs_3_.refs_5_, ...), custom_call_target="tpu_custom_call" | custom-call | tf_op jit(solution)/shard_map/partial_sums/pallas_call | solution.py:166
  201.7 4.4 %finish.1 = bf16[1,128,8192]{2,1,0:T(8,128)(2,1)} custom-call(s32[2]{0:T(128)S(1)} %pad_add_fusion.at_ref, f32[128,128]{1,0:T(8,128)S(1)} %get-tuple-element.132.r_ref, bf16[1,8192]{1,0:T(2,128)(2,1)S(1)} %copy-done.2, bf16[128,8192]{1,0:T(8,128)(2,1)S(1)} %bitcast.9, bf16[1,128,8192]{2,1,0:T(8,128)(2,1)S(1)} %collective-permute-done.26.u_ref, ...), custom_call_target="tpu_custom_call" | custom-call | tf_op jit(solution)/shard_map/finish/pallas_call | solution.py:236
  (39 shorter events, 0.1 us)
Async XLA Ops:
  0.6 5.6 %copy-start.2 = (bf16[1,8192]{1,0:T(2,128)(2,1)S(1)}, bf16[1,8192]{1,0:T(2,128)(2,1)}, u32[]{:S(2)}) copy-start(bf16[1,8192]{1,0:T(2,128)(2,1)} %g_ref.3) | copy-start | bytes 49156
  3.0 20.9 %collective-permute-start.16 = (bf16[1,4,128,768]{3,2,1,0:T(8,128)(2,1)}, bf16[1,4,128,768]{3,2,1,0:T(8,128)(2,1)S(1)}, u32[]{:S(2)}, u32[]{:S(2)}) collective-permute-start(bf16[1,4,128,768]{3,2,1,0:T(8,128)(2,1)} %get-tuple-element.168), channel_id=1, source_target_pairs={{0,4},{1,5},{2,6},{3,7},{4,0},{5,1},{6,2},{7,3},{8,12},{9,13},{10,... | collective-permute-start | bytes 2359304 | tf_op jit(solution)/shard_map/ppermute | solution.py:49
  6.2 1.6 copy-start
  10.5 0.8 copy-start.3
  11.4 15.8 %collective-permute-start = (bf16[1,2048,128]{2,1,0:T(8,128)(2,1)}, bf16[1,2048,128]{2,1,0:T(8,128)(2,1)S(1)}, u32[]{:S(2)}, u32[]{:S(2)}) collective-permute-start(bf16[1,2048,128]{2,1,0:T(8,128)(2,1)} %get-tuple-element.87), channel_id=1, source_target_pairs={{8,0},{16,8},{24,16},{0,24},{9,1},{17,9},{25,17},{1,25},{10,2},{18... | collective-permute-start | bytes 1572872 | tf_op jit(solution)/shard_map/ppermute | solution.py:37
  15.4 14.5 %collective-permute-start.1 = (bf16[1,2048,128]{2,1,0:T(8,128)(2,1)}, bf16[1,2048,128]{2,1,0:T(8,128)(2,1)S(1)}, u32[]{:S(2)}, u32[]{:S(2)}) collective-permute-start(bf16[1,2048,128]{2,1,0:T(8,128)(2,1)} %get-tuple-element.89), channel_id=1, source_target_pairs={{24,0},{0,8},{8,16},{16,24},{25,1},{1,9},{9,17},{17,25},{26,2},{2,... | collective-permute-start | bytes 1572872 | tf_op jit(solution)/shard_map/ppermute | solution.py:37
  15.4 14.5 %copy-start.4 = (bf16[1,2048,128]{2,1,0:T(8,128)(2,1)S(1)}, bf16[1,2048,128]{2,1,0:T(8,128)(2,1)}, u32[]{:S(2)}) copy-start(bf16[1,2048,128]{2,1,0:T(8,128)(2,1)} %copy-done.3) | copy-start | bytes 1572868
  17.5 13.7 %collective-permute-start.3 = (bf16[1,2048,128]{2,1,0:T(8,128)(2,1)S(1)}, bf16[1,2048,128]{2,1,0:T(8,128)(2,1)S(1)}, u32[]{:S(2)}, u32[]{:S(2)}) collective-permute-start(bf16[1,2048,128]{2,1,0:T(8,128)(2,1)S(1)} %get-tuple-element.107.refs_0_), channel_id=1, source_target_pairs={{1,0},{2,1},{3,2},{0,3},{5,4},{6,5},{7,6},{4,7},{9,8},{10,9},{11,1... | collective-permute-start | bytes 1572872 | tf_op jit(solution)/shard_map/ppermute | solution.py:41
  20.6 14.3 %collective-permute-start.7 = (bf16[1,2048,128]{2,1,0:T(8,128)(2,1)S(1)}, bf16[1,2048,128]{2,1,0:T(8,128)(2,1)S(1)}, u32[]{:S(2)}, u32[]{:S(2)}) collective-permute-start(bf16[1,2048,128]{2,1,0:T(8,128)(2,1)S(1)} %get-tuple-element.107.refs_0_), channel_id=1, source_target_pairs={{3,0},{0,1},{1,2},{2,3},{7,4},{4,5},{5,6},{6,7},{11,8},{8,9},{9,10... | collective-permute-start | bytes 1572872 | tf_op jit(solution)/shard_map/ppermute | solution.py:41
  23.9 75.5 %collective-permute-start.22 = (bf16[2048,768]{1,0:T(8,128)(2,1)S(1)}, bf16[2048,768]{1,0:T(8,128)(2,1)S(1)}, u32[]{:S(2)}, u32[]{:S(2)}) collective-permute-start(bf16[2048,768]{1,0:T(8,128)(2,1)S(1)} %dynamic-slice_bitcast_fusion.refs_6_.refs_8_.refs_12_.refs_14_.refs_4_.refs_2_), channel_id=1, source_target_pairs={{0,4},{1,5},{2,6},{3,7},{4,0},{5,1},{6,2},{7,3},{8,12},{9,13},{10,... | collective-permute-start | bytes 9437192 | tf_op jit(solution)/shard_map/ppermute | solution.py:49
  29.9 13.7 %collective-permute-start.2 = (bf16[1,2048,128]{2,1,0:T(8,128)(2,1)S(1)}, bf16[1,2048,128]{2,1,0:T(8,128)(2,1)S(1)}, u32[]{:S(2)}, u32[]{:S(2)}) collective-permute-start(bf16[1,2048,128]{2,1,0:T(8,128)(2,1)S(1)} %copy-done.4), channel_id=1, source_target_pairs={{16,0},{24,8},{0,16},{8,24},{17,1},{25,9},{1,17},{9,25},{18,2},{26... | collective-permute-start | bytes 1572872 | tf_op jit(solution)/shard_map/ppermute | solution.py:37
  31.3 14.4 %collective-permute-start.4 = (bf16[1,2048,128]{2,1,0:T(8,128)(2,1)S(1)}, bf16[1,2048,128]{2,1,0:T(8,128)(2,1)S(1)}, u32[]{:S(2)}, u32[]{:S(2)}) collective-permute-start(bf16[1,2048,128]{2,1,0:T(8,128)(2,1)S(1)} %collective-permute-done.refs_4_), channel_id=1, source_target_pairs={{1,0},{2,1},{3,2},{0,3},{5,4},{6,5},{7,6},{4,7},{9,8},{10,9},{11,1... | collective-permute-start | bytes 1572872 | tf_op jit(solution)/shard_map/ppermute | solution.py:41
  35.0 13.7 %collective-permute-start.8 = (bf16[1,2048,128]{2,1,0:T(8,128)(2,1)S(1)}, bf16[1,2048,128]{2,1,0:T(8,128)(2,1)S(1)}, u32[]{:S(2)}, u32[]{:S(2)}) collective-permute-start(bf16[1,2048,128]{2,1,0:T(8,128)(2,1)S(1)} %collective-permute-done.refs_4_), channel_id=1, source_target_pairs={{3,0},{0,1},{1,2},{2,3},{7,4},{4,5},{5,6},{6,7},{11,8},{8,9},{9,10... | collective-permute-start | bytes 1572872 | tf_op jit(solution)/shard_map/ppermute | solution.py:41
  43.6 20.4 %collective-permute-start.15 = (bf16[1,4,128,768]{3,2,1,0:T(8,128)(2,1)S(1)}, bf16[1,4,128,768]{3,2,1,0:T(8,128)(2,1)S(1)}, u32[]{:S(2)}, u32[]{:S(2)}) collective-permute-start(bf16[1,4,128,768]{3,2,1,0:T(8,128)(2,1)S(1)} %get-tuple-element.123.refs_16_.refs_0_.refs_2_.refs_4_), channel_id=1, source_target_pairs={{8,0},{16,8},{24,16},{0,24},{9,1},{17,9},{25,17},{1,25},{10,2},{18... | collective-permute-start | bytes 2359304 | tf_op jit(solution)/shard_map/ppermute | solution.py:37
  45.3 21.6 %collective-permute-start.19 = (bf16[1,4,128,768]{3,2,1,0:T(8,128)(2,1)S(1)}, bf16[1,4,128,768]{3,2,1,0:T(8,128)(2,1)S(1)}, u32[]{:S(2)}, u32[]{:S(2)}) collective-permute-start(bf16[1,4,128,768]{3,2,1,0:T(8,128)(2,1)S(1)} %get-tuple-element.123.refs_16_.refs_0_.refs_2_.refs_4_), channel_id=1, source_target_pairs={{24,0},{0,8},{8,16},{16,24},{25,1},{1,9},{9,17},{17,25},{26,2},{2,... | collective-permute-start | bytes 2359304 | tf_op jit(solution)/shard_map/ppermute | solution.py:37
  45.6 11.5 %collective-permute-start.5 = (bf16[1,2048,128]{2,1,0:T(8,128)(2,1)S(1)}, bf16[1,2048,128]{2,1,0:T(8,128)(2,1)S(1)}, u32[]{:S(2)}, u32[]{:S(2)}) collective-permute-start(bf16[1,2048,128]{2,1,0:T(8,128)(2,1)S(1)} %collective-permute-done.1.refs_12_), channel_id=1, source_target_pairs={{1,0},{2,1},{3,2},{0,3},{5,4},{6,5},{7,6},{4,7},{9,8},{10,9},{11,1... | collective-permute-start | bytes 1572872 | tf_op jit(solution)/shard_map/ppermute | solution.py:41
  48.6 12.1 %collective-permute-start.9 = (bf16[1,2048,128]{2,1,0:T(8,128)(2,1)S(1)}, bf16[1,2048,128]{2,1,0:T(8,128)(2,1)S(1)}, u32[]{:S(2)}, u32[]{:S(2)}) collective-permute-start(bf16[1,2048,128]{2,1,0:T(8,128)(2,1)S(1)} %collective-permute-done.1.refs_12_), channel_id=1, source_target_pairs={{3,0},{0,1},{1,2},{2,3},{7,4},{4,5},{5,6},{6,7},{11,8},{8,9},{9,10... | collective-permute-start | bytes 1572872 | tf_op jit(solution)/shard_map/ppermute | solution.py:41
  60.7 12.1 %collective-permute-start.10 = (bf16[1,2048,128]{2,1,0:T(8,128)(2,1)S(1)}, bf16[1,2048,128]{2,1,0:T(8,128)(2,1)S(1)}, u32[]{:S(2)}, u32[]{:S(2)}) collective-permute-start(bf16[1,2048,128]{2,1,0:T(8,128)(2,1)S(1)} %collective-permute-done.2.refs_8_), channel_id=1, source_target_pairs={{3,0},{0,1},{1,2},{2,3},{7,4},{4,5},{5,6},{6,7},{11,8},{8,9},{9,10... | collective-permute-start | bytes 1572872 | tf_op jit(solution)/shard_map/ppermute | solution.py:41
  60.7 12.1 %collective-permute-start.6 = (bf16[1,2048,128]{2,1,0:T(8,128)(2,1)S(1)}, bf16[1,2048,128]{2,1,0:T(8,128)(2,1)S(1)}, u32[]{:S(2)}, u32[]{:S(2)}) collective-permute-start(bf16[1,2048,128]{2,1,0:T(8,128)(2,1)S(1)} %collective-permute-done.2.refs_8_), channel_id=1, source_target_pairs={{1,0},{2,1},{3,2},{0,3},{5,4},{6,5},{7,6},{4,7},{9,8},{10,9},{11,1... | collective-permute-start | bytes 1572872 | tf_op jit(solution)/shard_map/ppermute | solution.py:41
  64.0 17.0 %collective-permute-start.17 = (bf16[1,4,128,768]{3,2,1,0:T(8,128)(2,1)S(1)}, bf16[1,4,128,768]{3,2,1,0:T(8,128)(2,1)S(1)}, u32[]{:S(2)}, u32[]{:S(2)}) collective-permute-start(bf16[1,4,128,768]{3,2,1,0:T(8,128)(2,1)S(1)} %collective-permute-done.16.refs_16_.refs_1_.refs_3_.refs_5_), channel_id=1, source_target_pairs={{8,0},{16,8},{24,16},{0,24},{9,1},{17,9},{25,17},{1,25},{10,2},{18... | collective-permute-start | bytes 2359304 | tf_op jit(solution)/shard_map/ppermute | solution.py:37
  66.9 17.7 %collective-permute-start.20 = (bf16[1,4,128,768]{3,2,1,0:T(8,128)(2,1)S(1)}, bf16[1,4,128,768]{3,2,1,0:T(8,128)(2,1)S(1)}, u32[]{:S(2)}, u32[]{:S(2)}) collective-permute-start(bf16[1,4,128,768]{3,2,1,0:T(8,128)(2,1)S(1)} %collective-permute-done.16.refs_16_.refs_1_.refs_3_.refs_5_), channel_id=1, source_target_pairs={{24,0},{0,8},{8,16},{16,24},{25,1},{1,9},{9,17},{17,25},{26,2},{2,... | collective-permute-start | bytes 2359304 | tf_op jit(solution)/shard_map/ppermute | solution.py:37
  72.8 12.2 %collective-permute-start.12 = (bf16[1,2048,128]{2,1,0:T(8,128)(2,1)S(1)}, bf16[1,2048,128]{2,1,0:T(8,128)(2,1)S(1)}, u32[]{:S(2)}, u32[]{:S(2)}) collective-permute-start(bf16[1,2048,128]{2,1,0:T(8,128)(2,1)S(1)} %collective-permute-done.8.refs_7_), channel_id=1, source_target_pairs={{3,0},{0,1},{1,2},{2,3},{7,4},{4,5},{5,6},{6,7},{11,8},{8,9},{9,10... | collective-permute-start | bytes 1572872 | tf_op jit(solution)/shard_map/ppermute | solution.py:41
  72.8 12.2 %collective-permute-start.11 = (bf16[1,2048,128]{2,1,0:T(8,128)(2,1)S(1)}, bf16[1,2048,128]{2,1,0:T(8,128)(2,1)S(1)}, u32[]{:S(2)}, u32[]{:S(2)}) collective-permute-start(bf16[1,2048,128]{2,1,0:T(8,128)(2,1)S(1)} %collective-permute-done.3.refs_1_), channel_id=1, source_target_pairs={{1,0},{2,1},{3,2},{0,3},{5,4},{6,5},{7,6},{4,7},{9,8},{10,9},{11,1... | collective-permute-start | bytes 1572872 | tf_op jit(solution)/shard_map/ppermute | solution.py:41
  81.0 15.0 %collective-permute-start.18 = (bf16[1,4,128,768]{3,2,1,0:T(8,128)(2,1)S(1)}, bf16[1,4,128,768]{3,2,1,0:T(8,128)(2,1)S(1)}, u32[]{:S(2)}, u32[]{:S(2)}) collective-permute-start(bf16[1,4,128,768]{3,2,1,0:T(8,128)(2,1)S(1)} %collective-permute-done.15.refs_17_.refs_0_.refs_6_), channel_id=1, source_target_pairs={{8,0},{16,8},{24,16},{0,24},{9,1},{17,9},{25,17},{1,25},{10,2},{18... | collective-permute-start | bytes 2359304 | tf_op jit(solution)/shard_map/ppermute | solution.py:37
  84.6 14.8 %collective-permute-start.21 = (bf16[1,4,128,768]{3,2,1,0:T(8,128)(2,1)S(1)}, bf16[1,4,128,768]{3,2,1,0:T(8,128)(2,1)S(1)}, u32[]{:S(2)}, u32[]{:S(2)}) collective-permute-start(bf16[1,4,128,768]{3,2,1,0:T(8,128)(2,1)S(1)} %collective-permute-done.20.refs_19_.refs_5_.refs_11_), channel_id=1, source_target_pairs={{24,0},{0,8},{8,16},{16,24},{25,1},{1,9},{9,17},{17,25},{26,2},{2,... | collective-permute-start | bytes 2359304 | tf_op jit(solution)/shard_map/ppermute | solution.py:37
  85.1 10.4 %collective-permute-start.13 = (bf16[1,2048,128]{2,1,0:T(8,128)(2,1)S(1)}, bf16[1,2048,128]{2,1,0:T(8,128)(2,1)S(1)}, u32[]{:S(2)}, u32[]{:S(2)}) collective-permute-start(bf16[1,2048,128]{2,1,0:T(8,128)(2,1)S(1)} %collective-permute-done.10.refs_11_), channel_id=1, source_target_pairs={{3,0},{0,1},{1,2},{2,3},{7,4},{4,5},{5,6},{6,7},{11,8},{8,9},{9,10... | collective-permute-start | bytes 1572872 | tf_op jit(solution)/shard_map/ppermute | solution.py:41
  85.1 10.4 %collective-permute-start.14 = (bf16[1,2048,128]{2,1,0:T(8,128)(2,1)S(1)}, bf16[1,2048,128]{2,1,0:T(8,128)(2,1)S(1)}, u32[]{:S(2)}, u32[]{:S(2)}) collective-permute-start(bf16[1,2048,128]{2,1,0:T(8,128)(2,1)S(1)} %collective-permute-done.5.refs_13_), channel_id=1, source_target_pairs={{1,0},{2,1},{3,2},{0,3},{5,4},{6,5},{7,6},{4,7},{9,8},{10,9},{11,1... | collective-permute-start | bytes 1572872 | tf_op jit(solution)/shard_map/ppermute | solution.py:41
  108.1 83.2 %collective-permute-start.23 = (bf16[2048,768]{1,0:T(8,128)(2,1)S(1)}, bf16[2048,768]{1,0:T(8,128)(2,1)S(1)}, u32[]{:S(2)}, u32[]{:S(2)}) collective-permute-start(bf16[2048,768]{1,0:T(8,128)(2,1)S(1)} %weight_terms.3), channel_id=1, source_target_pairs={{0,4},{1,5},{2,6},{3,7},{4,0},{5,1},{6,2},{7,3},{8,12},{9,13},{10,... | collective-permute-start | bytes 9437192 | tf_op jit(solution)/shard_map/ppermute | solution.py:49
  112.6 17.6 %collective-permute-start.24 = (bf16[3,128,1024]{2,1,0:T(8,128)(2,1)S(1)}, bf16[3,128,1024]{2,1,0:T(8,128)(2,1)S(1)}, u32[]{:S(2)}, u32[]{:S(2)}) collective-permute-start(bf16[3,128,1024]{2,1,0:T(8,128)(2,1)S(1)} %get-tuple-element.137), channel_id=1, source_target_pairs={{3,0},{0,1},{1,2},{2,3},{7,4},{4,5},{5,6},{6,7},{11,8},{8,9},{9,10... | collective-permute-start | bytes 2359304 | tf_op jit(solution)/shard_map/ppermute | solution.py:41
  112.9 17.7 %collective-permute-start.25 = (bf16[3,128,1024]{2,1,0:T(8,128)(2,1)S(1)}, bf16[3,128,1024]{2,1,0:T(8,128)(2,1)S(1)}, u32[]{:S(2)}, u32[]{:S(2)}) collective-permute-start(bf16[3,128,1024]{2,1,0:T(8,128)(2,1)S(1)} %get-tuple-element.139), channel_id=1, source_target_pairs={{1,0},{2,1},{3,2},{0,3},{5,4},{6,5},{7,6},{4,7},{9,8},{10,9},{11,1... | collective-permute-start | bytes 2359304 | tf_op jit(solution)/shard_map/ppermute | solution.py:41
  130.2 17.5 %collective-permute-start.27 = (bf16[3,128,1024]{2,1,0:T(8,128)(2,1)S(1)}, bf16[3,128,1024]{2,1,0:T(8,128)(2,1)S(1)}, u32[]{:S(2)}, u32[]{:S(2)}) collective-permute-start(bf16[3,128,1024]{2,1,0:T(8,128)(2,1)S(1)} %get-tuple-element.145), channel_id=1, source_target_pairs={{3,0},{0,1},{1,2},{2,3},{7,4},{4,5},{5,6},{6,7},{11,8},{8,9},{9,10... | collective-permute-start | bytes 2359304 | tf_op jit(solution)/shard_map/ppermute | solution.py:41
  130.6 7.1 %copy-start.5 = (bf16[1,128,8192]{2,1,0:T(8,128)(2,1)S(1)}, bf16[1,128,8192]{2,1,0:T(8,128)(2,1)}, u32[]{:S(2)}) copy-start(bf16[1,128,8192]{2,1,0:T(8,128)(2,1)} %param.9) | copy-start | bytes 6291460
  130.6 17.7 %collective-permute-start.29 = (bf16[3,128,1024]{2,1,0:T(8,128)(2,1)S(1)}, bf16[3,128,1024]{2,1,0:T(8,128)(2,1)S(1)}, u32[]{:S(2)}, u32[]{:S(2)}) collective-permute-start(bf16[3,128,1024]{2,1,0:T(8,128)(2,1)S(1)} %get-tuple-element.149), channel_id=1, source_target_pairs={{1,0},{2,1},{3,2},{0,3},{5,4},{6,5},{7,6},{4,7},{9,8},{10,9},{11,1... | collective-permute-start | bytes 2359304 | tf_op jit(solution)/shard_map/ppermute | solution.py:41
  137.7 64.0 %collective-permute-start.26 = (bf16[1,128,8192]{2,1,0:T(8,128)(2,1)S(1)}, bf16[1,128,8192]{2,1,0:T(8,128)(2,1)S(1)}, u32[]{:S(2)}, u32[]{:S(2)}) collective-permute-start(bf16[1,128,8192]{2,1,0:T(8,128)(2,1)S(1)} %copy-done.5), channel_id=1, source_target_pairs={{32,0},{64,32},{96,64},{33,1},{65,33},{97,65},{34,2},{66,34},{98,6... | collective-permute-start | bytes 6291464 | tf_op jit(solution)/shard_map/ppermute | solution.py:328
  147.7 17.1 %collective-permute-start.28 = (bf16[3,128,1024]{2,1,0:T(8,128)(2,1)S(1)}, bf16[3,128,1024]{2,1,0:T(8,128)(2,1)S(1)}, u32[]{:S(2)}, u32[]{:S(2)}) collective-permute-start(bf16[3,128,1024]{2,1,0:T(8,128)(2,1)S(1)} %get-tuple-element.146), channel_id=1, source_target_pairs={{3,0},{0,1},{1,2},{2,3},{7,4},{4,5},{5,6},{6,7},{11,8},{8,9},{9,10... | collective-permute-start | bytes 2359304 | tf_op jit(solution)/shard_map/ppermute | solution.py:41
  148.3 16.5 %collective-permute-start.30 = (bf16[3,128,1024]{2,1,0:T(8,128)(2,1)S(1)}, bf16[3,128,1024]{2,1,0:T(8,128)(2,1)S(1)}, u32[]{:S(2)}, u32[]{:S(2)}) collective-permute-start(bf16[3,128,1024]{2,1,0:T(8,128)(2,1)S(1)} %get-tuple-element.151), channel_id=1, source_target_pairs={{1,0},{2,1},{3,2},{0,3},{5,4},{6,5},{7,6},{4,7},{9,8},{10,9},{11,1... | collective-permute-start | bytes 2359304 | tf_op jit(solution)/shard_map/ppermute | solution.py:41
  169.4 11.3 %collective-permute-start.32 = (bf16[2,128,1024]{2,1,0:T(8,128)(2,1)S(1)}, bf16[2,128,1024]{2,1,0:T(8,128)(2,1)S(1)}, u32[]{:S(2)}, u32[]{:S(2)}) collective-permute-start(bf16[2,128,1024]{2,1,0:T(8,128)(2,1)S(1)} %get-tuple-element.152), channel_id=1, source_target_pairs={{16,0},{24,8},{0,16},{8,24},{17,1},{25,9},{1,17},{9,25},{18,2},{26... | collective-permute-start | bytes 1572872 | tf_op jit(solution)/shard_map/ppermute | solution.py:37
  172.4 14.8 %collective-permute-start.31 = (bf16[2,128,1024]{2,1,0:T(8,128)(2,1)S(1)}, bf16[2,128,1024]{2,1,0:T(8,128)(2,1)S(1)}, u32[]{:S(2)}, u32[]{:S(2)}) collective-permute-start(bf16[2,128,1024]{2,1,0:T(8,128)(2,1)S(1)} %get-tuple-element.154), channel_id=1, source_target_pairs={{3,0},{0,1},{1,2},{2,3},{7,4},{4,5},{5,6},{6,7},{11,8},{8,9},{9,10... | collective-permute-start | bytes 1572872 | tf_op jit(solution)/shard_map/ppermute | solution.py:41
  172.8 14.4 %collective-permute-start.35 = (bf16[2,128,1024]{2,1,0:T(8,128)(2,1)S(1)}, bf16[2,128,1024]{2,1,0:T(8,128)(2,1)S(1)}, u32[]{:S(2)}, u32[]{:S(2)}) collective-permute-start(bf16[2,128,1024]{2,1,0:T(8,128)(2,1)S(1)} %get-tuple-element.162), channel_id=1, source_target_pairs={{1,0},{2,1},{3,2},{0,3},{5,4},{6,5},{7,6},{4,7},{9,8},{10,9},{11,1... | collective-permute-start | bytes 1572872 | tf_op jit(solution)/shard_map/ppermute | solution.py:41
  180.7 15.8 %collective-permute-start.33 = (bf16[2,128,1024]{2,1,0:T(8,128)(2,1)S(1)}, bf16[2,128,1024]{2,1,0:T(8,128)(2,1)S(1)}, u32[]{:S(2)}, u32[]{:S(2)}) collective-permute-start(bf16[2,128,1024]{2,1,0:T(8,128)(2,1)S(1)} %get-tuple-element.156), channel_id=1, source_target_pairs={{8,0},{16,8},{24,16},{0,24},{9,1},{17,9},{25,17},{1,25},{10,2},{18... | collective-permute-start | bytes 1572872 | tf_op jit(solution)/shard_map/ppermute | solution.py:37
  187.2 10.4 %collective-permute-start.34 = (bf16[2,128,1024]{2,1,0:T(8,128)(2,1)S(1)}, bf16[2,128,1024]{2,1,0:T(8,128)(2,1)S(1)}, u32[]{:S(2)}, u32[]{:S(2)}) collective-permute-start(bf16[2,128,1024]{2,1,0:T(8,128)(2,1)S(1)} %get-tuple-element.158), channel_id=1, source_target_pairs={{24,0},{0,8},{8,16},{16,24},{25,1},{1,9},{9,17},{17,25},{26,2},{2,... | collective-permute-start | bytes 1572872 | tf_op jit(solution)/shard_map/ppermute | solution.py:37
  190.6 7.7 %collective-permute-start.36 = (bf16[1,128,1024]{2,1,0:T(8,128)(2,1)S(1)}, bf16[1,128,1024]{2,1,0:T(8,128)(2,1)S(1)}, u32[]{:S(2)}, u32[]{:S(2)}) collective-permute-start(bf16[1,128,1024]{2,1,0:T(8,128)(2,1)S(1)} %get-tuple-element.165), channel_id=1, source_target_pairs={{3,0},{0,1},{1,2},{2,3},{7,4},{4,5},{5,6},{6,7},{11,8},{8,9},{9,10... | collective-permute-start | bytes 786440 | tf_op jit(solution)/shard_map/ppermute | solution.py:41
  191.2 7.0 %collective-permute-start.37 = (bf16[1,128,1024]{2,1,0:T(8,128)(2,1)S(1)}, bf16[1,128,1024]{2,1,0:T(8,128)(2,1)S(1)}, u32[]{:S(2)}, u32[]{:S(2)}) collective-permute-start(bf16[1,128,1024]{2,1,0:T(8,128)(2,1)S(1)} %get-tuple-element.167), channel_id=1, source_target_pairs={{1,0},{2,1},{3,2},{0,3},{5,4},{6,5},{7,6},{4,7},{9,8},{10,9},{11,1... | collective-permute-start | bytes 786440 | tf_op jit(solution)/shard_map/ppermute | solution.py:41
  196.5 5.3 %copy-start.1 = (bf16[1,128,8192]{2,1,0:T(8,128)(2,1)S(1)}, bf16[1,128,8192]{2,1,0:T(8,128)(2,1)}, u32[]{:S(2)}) copy-start(bf16[1,128,8192]{2,1,0:T(8,128)(2,1)} %param.5) | copy-start | bytes 6291460
